TPU v7x, 512 devices: a whole 4x8x8 slice. The times are simulated.
512 devices in a mesh: op: 128 (over y, z, core), blk: 4 (over x).
Axes of the slice: x: 4, y: 8, z: 8, core: 2. Of those that a mesh axis runs over, the one named last changes fastest.
Arguments:
- wavefunction: bfloat16 [2, 8, 384, 384], P(None, 'blk'), may hold values from -160 to 160
- left_ops: bfloat16 [512, 8, 384, 384], P('op', 'blk'), may hold values from -1.25 to 1.25
- right_ops: bfloat16 [512, 8, 384, 384], P('op', 'blk'), may hold values from -0.013671875 to 0.013671875
- shifts: int32 [512], P('op'), may hold values from -1 to 1
- sector_sizes: int32 [8], replicated, may hold values from 1 to 384, 2688 in all
- site_coef: float32 [128, 512], P('op'), may hold values from 0.25 to 4
- site_energy: float32 [128], P('op'), may hold values from -3 to -1
- site_owner: int32 [1], replicated, may hold values from 0 to 127
Outputs:
- residual: float32 [384, 2, 8, 384], P('op', None, 'blk')
- rayleigh: float32 [2], replicated
Inputs may be any that keep to these rules, and one draw needn't show every extreme that they name: Left and right blocks of pair k map sector b - shifts[k] to sector b. `sector_sizes`: the sizes sum to 2688; the largest equals 384.
All inputs are finite; a program needn't handle non-finite values.
Results may differ from a plain program's by a relative error of at most 0.00055.
The roundings to bfloat16 on the way count: a program that leaves them out, or rounds other values in their place, can miss the bound.
Values may be sent and summed in bfloat16 or wider, within the bound.
No kernel may reach another device: no remote copies, remote signals or barrier semaphores. Data moves between devices by JAX's collectives and lax.ppermute only.
A program may use at most 64 MiB of HBM per device.

v0:
```python
import jax
import jax.numpy as jnp
from jax import lax
from jax.sharding import PartitionSpec as P


def padded_2(cells, sides, width):
    for axis, dim in sides:
        count = lax.axis_size(axis)
        ends = count - 1
        head = lax.slice_in_dim(cells, 0, width, axis=dim)
        tail = lax.slice_in_dim(cells, cells.shape[dim] - width, cells.shape[dim], axis=dim)
        cells = jnp.concatenate(
            [
                lax.ppermute(tail, axis, [(i, (i + 1) % count) for i in range(ends)]),
                cells,
                lax.ppermute(head, axis, [((i + 1) % count, i) for i in range(ends)]),
            ],
            axis=dim,
        )
    return cells


def spread(value, axis, source):
    kept = jnp.where(lax.axis_index(axis) == source, value, 0).astype(value.dtype)
    return lax.psum(kept, axis)


def on_device(
    wavefunction, left_ops, right_ops, shifts, sector_sizes, site_coef, site_energy, site_owner
):
    vectors, local_count, sect_size, _ = wavefunction.shape
    pair_count = left_ops.shape[0]
    row_share = sect_size // lax.axis_size("op")
    my_index = lax.axis_index("op")
    first_sector = lax.axis_index("blk") * local_count
    row_ids = jnp.arange(sect_size, dtype=jnp.int32)
    local_sizes = lax.dynamic_slice_in_dim(sector_sizes, first_sector, local_count, 0)
    live_rows = row_ids[None, :] < local_sizes[:, None]
    live_mask = live_rows[:, :, None] & live_rows[:, None, :]
    psi_live = jnp.where(live_mask[None], wavefunction, jnp.zeros((), wavefunction.dtype))
    padded = padded_2(psi_live, (("blk", 1),), 1)
    coef_rows, energies = (
        spread(site_coef, "op", site_owner[0]),
        spread(site_energy, "op", site_owner[0]),
    )
    weights = lax.dynamic_slice_in_dim(coef_rows[0], my_index * pair_count, pair_count, 0)
    energy = energies[0]
    sources = [
        lax.dynamic_slice_in_dim(padded, 1 - shifts[slot], local_count, 1)
        for slot in range(pair_count)
    ]
    live_float = jnp.transpose(live_mask, (1, 0, 2)).astype(jnp.float32)
    psi_rows = jnp.transpose(
        lax.dynamic_slice_in_dim(psi_live, my_index * row_share, row_share, 2), (2, 0, 1, 3)
    ).astype(jnp.float32)
    running = jnp.zeros((sect_size, vectors, local_count, sect_size), jnp.float32)
    for slot in range(pair_count):
        left_part = jnp.einsum(
            "bis,vbsc->ivbc", left_ops[slot], sources[slot], preferred_element_type=jnp.float32
        ).astype(jnp.bfloat16)
        full_term = jnp.einsum(
            "ivbc,bdc->ivbd", left_part, right_ops[slot], preferred_element_type=jnp.float32
        )
        running = running + weights[slot] * full_term
    summed = lax.psum(running * live_float[:, None], "op")
    psi_float = jnp.transpose(psi_live, (2, 0, 1, 3)).astype(jnp.float32)
    norm_part = jnp.sum(psi_float * psi_float, axis=(0, 2, 3))
    cross_part = jnp.sum(psi_float * summed, axis=(0, 2, 3))
    norm_sum, cross_sum = lax.psum((norm_part, cross_part), "blk")
    own_rows = lax.dynamic_slice_in_dim(summed, my_index * row_share, row_share, 0)
    rayleigh = (cross_sum + energy * norm_sum) / (norm_sum + 1e-06)
    residual = own_rows + (energy - rayleigh)[None, :, None, None] * psi_rows
    return (residual, rayleigh)


def solution(mesh):
    return jax.shard_map(
        on_device,
        mesh=mesh,
        in_specs=(
            P(None, "blk", None, None),
            P("op", "blk", None, None),
            P("op", "blk", None, None),
            P("op"),
            P(),
            P("op", None),
            P("op"),
            P(),
        ),
        out_specs=(P("op", None, "blk", None), P()),
        check_vma=False,
    )
```

profile of v0, /device:TPU:1, one launch (start us, length us, event | category | flops | bytes accessed | tf_op | source)
XLA Modules:
  0.0 522.0 jit_solution(491935301173895240)
XLA Ops:
  7.2 0.0 all-reduce.4.cloned.1.call-start
  7.2 0.7 dynamic_slice.25
  7.9 0.1 iota_compare_fusion.1
  8.0 0.2 broadcast_and_fusion
  8.2 0.0 copy-start.1
  8.2 0.0 copy-start.4
  8.3 0.0 copy-start.5
  8.3 1.6 copy_select_fusion
  9.9 0.1 fusion.49
  10.0 0.0 copy-done.1
  10.0 4.0 collective-permute-start
  14.0 1.3 collective-permute-start.1
  15.3 0.0 copy-done.4
  15.3 0.6 fusion.51
  22.4 0.0 copy-done.5
  22.4 255.1 %all-reduce = (f32[1,512]{1,0:T(1,128)S(1)}, f32[]{:T(128)}) all-reduce(f32[1,512]{1,0:T(1,128)S(1)} %broadcast_select_fusion, f32[]{:T(128)} %bitcast.43), channel_id=1, replica_groups=mesh['op'=128,'blk'=4] {'op'}, use_global_device_ids=true, to_apply=%region_0.1 | all-reduce | flops 513 | bytes 4104 | tf_op jit(solution)/shard_map/psum | solution.py:26
  277.5 0.1 constant_dynamic-slice_fusion
  277.6 0.6 fusion.50
  278.2 0.1 iota_compare_fusion
  278.3 1.2 and_convert_fusion
  279.5 0.0 collective-permute-done
  279.5 0.0 copy-start.3
  279.5 0.8 copy-done.3
  280.3 0.0 collective-permute-done.1
  280.3 1.6 pad_maximum_fusion
  281.9 4.2 fusion.6
  286.1 4.2 fusion.7
  290.2 4.1 fusion.8
  294.3 9.2 %bitcast_multiply_fusion.2 = f32[384,2,2,384]{3,0,1,2:T(8,128)} fusion(f32[2,384,2,384]{3,1,2,0:T(8,128)} %fusion.6, f32[2,384,2,384]{3,1,2,0:T(8,128)} %fusion.7, f32[2,384,2,384]{3,1,2,0:T(8,128)} %fusion.8, f32[384,2,384]{2,0,1:T(8,128)} %and_convert_fusion, bf16[2,4,384,384]{3,2,0,1:T(8,128)(2,1)S(1)} %pad_maximum_fusion, s32[]{:T(128)S(6)} %select_n.50, ...), kind=kOutput, calls=%fused_computation.5 | convolution fusion | flops 911278080 | bytes 12978180 | tf_op jit(solution)/shard_map/ivbc,bdc->ivbd/dot_general | solution.py:62
  303.6 0.0 copy-start
  303.6 0.0 copy-start.2
  303.6 0.0 all-reduce.4.cloned.1.call-update
  303.6 197.9 %all-reduce.4.cloned.1.call-done = f32[384,2,2,384]{3,0,1,2:T(8,128)} async-done(((f32[384,2,2,384]{3,0,1,2:T(8,128)}), f32[384,2,2,384]{3,0,1,2:T(8,128)}) %all-reduce.4.cloned.1.call-update) | async-done | bytes 2359312 | tf_op jit(solution)/shard_map/psum | solution.py:66
  501.5 0.0 copy-done
  501.5 0.0 copy-done.2
  501.5 2.5 fusion
  504.0 8.4 %all-reduce.1 = (f32[2]{0:T(128)S(1)}, f32[2]{0:T(128)S(1)}) all-reduce(f32[2]{0:T(128)S(1)} %get-tuple-element.5, f32[2]{0:T(128)S(1)} %get-tuple-element.4), channel_id=1, replica_groups=mesh['op'=128,'blk'=4] {'blk'}, use_global_device_ids=true, to_apply=%region_6.7 | all-reduce | flops 4 | bytes 32 | tf_op jit(solution)/shard_map/psum | solution.py:70
  512.4 1.1 broadcast_subtract_fusion
  513.5 1.0 bitcast_add_fusion
  514.5 0.6 copy.11
  (1 shorter events, 0.0 us)
Async XLA Ops:
  7.2 494.3 %all-reduce.4.cloned.1.call-start = ((), (), s32[]{:S(2)}) async-start(), calls=%async_computation | async-start | bytes 4718592 | tf_op jit(solution)/shard_map/psum | solution.py:66
  8.2 1.8 copy-start.1
  8.2 7.0 %copy-start.4 = (s32[4]{0:T(128)S(1)}, s32[4]{0:T(128)}, u32[]{:S(2)}) copy-start(s32[4]{0:T(128)} %param.11) | copy-start | bytes 52
  8.3 14.1 %copy-start.5 = (f32[1,512]{1,0:T(1,128)S(1)}, f32[1,512]{1,0:T(1,128)}, u32[]{:S(2)}) copy-start(f32[1,512]{1,0:T(1,128)} %param.13) | copy-start | bytes 6148
  10.0 269.5 %collective-permute-start = (bf16[2,1,384,384]{3,2,0,1:T(8,128)(2,1)S(1)}, bf16[2,1,384,384]{3,2,0,1:T(8,128)(2,1)S(1)}, u32[]{:S(2)}, u32[]{:S(2)}) collective-permute-start(bf16[2,1,384,384]{3,2,0,1:T(8,128)(2,1)S(1)} %get-tuple-element.12), channel_id=1, source_target_pairs={{0,1},{1,2},{2,3},{4,5},{5,6},{6,7},{8,9},{9,10},{10,11},{12,13},{... | collective-permute-start | bytes 1769480 | tf_op jit(solution)/shard_map/ppermute | solution.py:15
  14.0 266.3 %collective-permute-start.1 = (bf16[2,1,384,384]{3,2,0,1:T(8,128)(2,1)S(1)}, bf16[2,1,384,384]{3,2,0,1:T(8,128)(2,1)}, u32[]{:S(2)}, u32[]{:S(2)}) collective-permute-start(bf16[2,1,384,384]{3,2,0,1:T(8,128)(2,1)S(1)} %get-tuple-element.13), channel_id=1, source_target_pairs={{1,0},{2,1},{3,2},{5,4},{6,5},{7,6},{9,8},{10,9},{11,10},{13,12},{... | collective-permute-start | bytes 1769480 | tf_op jit(solution)/shard_map/ppermute | solution.py:17
  279.5 0.8 copy-start.3
  303.6 197.9 %copy-start = (bf16[2,2,384,384]{3,2,1,0:T(8,128)(2,1)S(1)}, bf16[2,2,384,384]{3,2,1,0:T(8,128)(2,1)}, u32[]{:S(2)}) copy-start(bf16[2,2,384,384]{3,2,1,0:T(8,128)(2,1)} %param.8) | copy-start | bytes 3538948
  303.6 197.9 %copy-start.2 = (pred[2,384,384]{2,1,0:T(8,128)(4,1)S(1)}, pred[2,384,384]{2,1,0:T(8,128)(4,1)}, u32[]{:S(2)}) copy-start(pred[2,384,384]{2,1,0:T(8,128)(4,1)} %copy-done.1) | copy-start | bytes 884740
Sparse Core Ops, SparseCore 0:
  303.7 197.7 all-reduce.3
where the time goes:
time: 525 us; the launch traced here: 522 us
  blocking collectives  264 us (50%)
  waiting for transfers between devices  198 us (38%)
  matrix products  21.7 us (4%)
  between operations  20.6 us (4%)
  other arithmetic  9.36 us (2%)
  starting transfers between devices  5.31 us (1%)
    psum x1, blocking collectives, spread(): return lax.psum(kept, axis)  255 us
    psum x1, waiting for transfers between devices, on_device(): summed = lax.psum(running * live_float[:, None], 'op')  198 us
    dot_general x4, matrix products, on_device(): jnp.einsum('ivbc,bdc->ivbd', left_part, right_ops[slot], preferred_elemen...  21.7 us
  transfers between devices with their start and end apart: 3, of which 1 were waited for; matrix products, arithmetic and copies ran while one was open for 0% of the time, Pallas kernels for 0%

commit v1 on v0

v1 whole, which is shorter than its diff:
```python
import functools

import jax
import jax.numpy as jnp
from jax import lax
from jax.experimental import pallas as pl
from jax.experimental.pallas import tpu as pltpu
from jax.sharding import Mesh, PartitionSpec as P

F32, F16, BF16 = jnp.float32, jnp.float16, jnp.bfloat16
OP = ("chip", "core")
SPLIT = 2048.0


def sigma_kernel(
    pairs, meta, weight, psi, halo, left_own, left_got, right_own, right_got, acc, stats, src
):
    step = pl.program_id(0)
    size = acc.shape[1]
    core = meta[2 * pairs + 3]

    @pl.when(step == 0)
    def _():
        row = lax.broadcasted_iota(jnp.int32, (size, size), 0)
        col = lax.broadcasted_iota(jnp.int32, (size, size), 1)
        for slot in range(3):
            live = jnp.maximum(row, col) < meta[2 * pairs + slot]
            for v in range(2):
                block = psi[v, slot] if slot < 2 else halo[v]
                src[slot, :, v * size : (v + 1) * size] = jnp.where(
                    live, block.astype(F32), 0.0
                ).astype(BF16)

    def add_pair(left, right):
        part = jnp.dot(left[...], src[meta[step]], preferred_element_type=F32).astype(BF16)
        for v in range(2):
            term = weight[step] * lax.dot_general(
                part[:, v * size : (v + 1) * size],
                right[...],
                (((1,), (1,)), ((), ())),
                preferred_element_type=F32,
            )

            @pl.when(step == 0)
            def _():
                acc[v] = term

            @pl.when(step > 0)
            def _():
                acc[v] += term

    @pl.when(step < pairs)
    def _():
        add_pair(left_own.at[0, 0], right_own.at[0, 0])

    @pl.when(step >= pairs)
    def _():
        add_pair(left_got.at[0], right_got.at[0])

    @pl.when(step == 2 * pairs - 1)
    def _():
        top = 0.0
        for v in range(2):
            own = src[core, :, v * size : (v + 1) * size].astype(F32)
            total = acc[v]
            stats[v] = jnp.sum(own * total)
            stats[2 + v] = jnp.sum(own * own)
            top = jnp.maximum(top, jnp.max(jnp.abs(total)))
        stats[4] = top


def sigma_partial(meta, weight, psi, halo, left, left_got, right, right_got):
    pairs, _, size, _ = left.shape
    own = pl.BlockSpec(
        (1, 1, size, size), lambda i, m, w: (jnp.minimum(i, pairs - 1), m[2 * pairs + 3], 0, 0)
    )
    got = pl.BlockSpec((1, size, size), lambda i, m, w: (jnp.maximum(i - pairs, 0), 0, 0))
    whole = lambda shape: pl.BlockSpec(shape, lambda i, m, w: (0,) * len(shape))
    return pl.pallas_call(
        functools.partial(sigma_kernel, pairs),
        grid_spec=pltpu.PrefetchScalarGridSpec(
            num_scalar_prefetch=2,
            grid=(2 * pairs,),
            in_specs=[whole(psi.shape), whole(halo.shape), own, got, own, got],
            out_specs=[whole((2, size, size)), pl.BlockSpec(memory_space=pltpu.SMEM)],
            scratch_shapes=[pltpu.VMEM((3, size, 2 * size), BF16)],
        ),
        out_shape=[
            jax.ShapeDtypeStruct((2, size, size), F32),
            jax.ShapeDtypeStruct((8,), F32),
        ],
        compiler_params=pltpu.CompilerParams(
            dimension_semantics=("arbitrary",), vmem_limit_bytes=40 * 1024 * 1024
        ),
        cost_estimate=pl.CostEstimate(
            flops=2 * pairs * 8 * size**3,
            bytes_accessed=2 * (4 * pairs + 6) * size * size + 8 * size * size,
            transcendentals=0,
        ),
        name="sigma_partial",
    )(meta, weight, psi, halo, left, left_got, right, right_got)


def power_above(value, head):
    return jnp.maximum(jnp.ceil(jnp.log2(jnp.maximum(value, 1e-30))), -90.0) - head


def on_device(
    wavefunction, left_ops, right_ops, shifts, sector_sizes, site_coef, site_energy, site_owner
):
    vectors, _, size, _ = wavefunction.shape
    pairs = left_ops.shape[0]
    sectors = sector_sizes.shape[0]
    chips, blks = lax.axis_size("chip"), lax.axis_size("blk")
    chip, core, blk = lax.axis_index("chip"), lax.axis_index("core"), lax.axis_index("blk")
    other = 1 - core
    op = chip * 2 + core
    chip_rows = size // chips
    rows = chip_rows // 2

    swap = [(0, 1), (1, 0)]
    take = lambda array, index: lax.dynamic_index_in_dim(array, index, 1, keepdims=False)
    halo_path = [(x, x + 1) for x in range(blks - 1)] + [
        (blks + x + 1, blks + x) for x in range(blks - 1)
    ]
    halo = lax.ppermute(take(wavefunction, other), ("core", "blk"), halo_path)
    left_got = lax.ppermute(take(left_ops, other), "core", swap)
    right_got = lax.ppermute(take(right_ops, other), "core", swap)

    words = jnp.concatenate(
        [
            jnp.repeat(site_coef.reshape(chips, 2 * pairs), 2, axis=0),
            jnp.broadcast_to(
                jnp.concatenate([site_energy, shifts.astype(F32)])[None], (2 * chips, 1 + pairs)
            ),
        ],
        axis=1,
    )
    words = lax.all_to_all(words, OP, 0, 0, tiled=True)
    owned = lax.dynamic_index_in_dim(words, site_owner[0], 0, keepdims=False)
    energy = owned[2 * pairs]
    shifts_got = lax.dynamic_slice(words, (chip * 2 + other, 2 * pairs + 1), (1, pairs))[0]
    chip_weights = owned[: 2 * pairs].reshape(2, pairs)
    weights = jnp.where(core == 0, chip_weights, chip_weights[::-1]).reshape(-1)
    place = core - jnp.concatenate([shifts, jnp.round(shifts_got).astype(jnp.int32)])
    slots = jnp.where((place == 0) | (place == 1), place, 2)
    far = 2 * blk - 1 + 3 * core
    ids = jnp.stack([2 * blk, 2 * blk + 1, far])
    sizes = jnp.where(
        (ids >= 0) & (ids < sectors), sector_sizes[jnp.clip(ids, 0, sectors - 1)], 0
    )
    meta = jnp.concatenate([slots, sizes, core[None]]).astype(jnp.int32)
    partial, stats = sigma_partial(
        meta, weights, wavefunction, halo, left_ops, left_got, right_ops, right_got
    )

    level = power_above(stats[4], 14.0)
    cross = stats[:2]
    cross_level = power_above(jnp.max(jnp.abs(cross)), 0.0)
    value = cross * jnp.exp2(-cross_level)
    pieces = []
    for _ in range(3):
        piece = value.astype(F16)
        pieces.append(piece)
        value = (value - piece.astype(F32)) * SPLIT
    tags = jnp.concatenate([jnp.stack([level, cross_level]).astype(F16)] + pieces)
    blocks = (partial * jnp.exp2(-level)).astype(F16)
    blocks = blocks.reshape(vectors, chips, chip_rows, size).transpose(1, 0, 2, 3)
    lines = vectors * chip_rows * size // 128
    blocks = jnp.concatenate(
        [
            blocks.reshape(chips, lines, 128),
            jnp.broadcast_to(jnp.pad(tags, (0, 120))[None, None], (chips, 1, 128)),
            jnp.zeros((chips, -(lines + 1) % 8, 128), F16),
        ],
        axis=1,
    )
    blocks = lax.all_to_all(blocks, "chip", 0, 0, tiled=True)
    tags = blocks[:, lines, :8].astype(F32)
    cross = jnp.sum(
        (tags[:, 2:4] + (tags[:, 4:6] + tags[:, 6:8] / SPLIT) / SPLIT) * jnp.exp2(tags[:, 1:2]),
        axis=0,
    )
    summed = jnp.sum(
        blocks[:, :lines].astype(F32) * jnp.exp2(tags[:, 0])[:, None, None], axis=0
    ).reshape(vectors, 2, rows, size)

    got = lax.ppermute(take(summed, other), "core", swap)
    kept = take(summed, core)
    ours = jnp.where(core == 0, jnp.stack([kept, got], 2), jnp.stack([got, kept], 2))
    sums = jnp.broadcast_to(jnp.concatenate([cross, stats[2:4]])[None], (2 * blks, 4))
    sums = jnp.sum(lax.all_to_all(sums, ("core", "blk"), 0, 0, tiled=True), axis=0)
    cross_sum, norm_sum = sums[:2], sums[2:]
    rayleigh = (cross_sum + energy * norm_sum) / (norm_sum + 1e-06)

    first = op * rows
    own_sizes = lax.dynamic_slice_in_dim(sector_sizes, 2 * blk, 2, 0)[:, None, None]
    row_ids = first + jnp.arange(rows, dtype=jnp.int32)[None, :, None]
    col_ids = jnp.arange(size, dtype=jnp.int32)[None, None, :]
    live = ((row_ids < own_sizes) & (col_ids < own_sizes)).transpose(1, 0, 2)[:, None]
    psi_rows = lax.dynamic_slice_in_dim(wavefunction, first, rows, 2)
    psi_rows = psi_rows.transpose(2, 0, 1, 3).astype(F32)
    value = ours.transpose(1, 0, 2, 3) + (energy - rayleigh)[None, :, None, None] * psi_rows
    return jnp.where(live, value, 0.0), rayleigh


def solution(mesh):
    ops, blks = mesh.devices.shape
    split = Mesh(mesh.devices.reshape(ops // 2, 2, blks), OP + ("blk",))
    return jax.shard_map(
        on_device,
        mesh=split,
        in_specs=(
            P(None, "blk", None, None),
            P(OP, "blk", None, None),
            P(OP, "blk", None, None),
            P(OP),
            P(),
            P(OP, None),
            P(OP),
            P(),
        ),
        out_specs=(P(OP, None, "blk", None), P()),
        check_vma=False,
    )
```

time: 525 us -> 116 us (0.22)
  blocking collectives: 264 us -> 0 us
  waiting for transfers between devices: 198 us -> 22.6 us
  starting transfers between devices: 5.31 us -> 47.9 us
  matrix products: 21.7 us -> 0 us
  between operations: 20.6 us -> 3.73 us
  local copies, waits for them, and re-layouts: 3.61 us -> 18.7 us
  Pallas kernels: 0 us -> 13 us
    psum x2 -> x0, blocking collectives: 264 us -> none  [the longest x1 255 us: spread(): return lax.psum(kept, axis)]
    psum x1 -> x0, waiting for transfers between devices: 198 us -> none  [on_device(): summed = lax.psum(running * live_float[:, None], 'op')]
    all_to_all x0 -> x3, starting transfers between devices: none -> 39.6 us  [the longest x1 18.9 us: on_device(): words = lax.all_to_all(words, OP, 0, 0, tiled=True)]
    dot_general x4 -> x0, matrix products: 21.7 us -> none  [on_device(): jnp.einsum('ivbc,bdc->ivbd', left_part, right_ops[slot], preferred_elemen...]
    all_to_all x0 -> x3, waiting for transfers between devices: none -> 19.2 us  [the longest x1 16.9 us: on_device(): blocks = lax.all_to_all(blocks, 'chip', 0, 0, tiled=True)]
    pallas_call x0 -> x1, Pallas kernels: none -> 13 us  [sigma_partial(): pl.pallas_call(functools.partial(sigma_kernel, pairs), grid_spec=pltpu.Pr...]
    unnamed x13 -> x24, local copies, waits for them, and re-layouts: 1.46 us -> 6.96 us
  transfers between devices with their start and end apart: 3 -> 7, of which waited for: 1 -> 3; matrix products, arithmetic and copies ran while one was open for 0% -> 11% of each run, Pallas kernels for 0% -> 0%
where the time goes in v1:
time: 116 us; the launch traced here: 115 us
  starting transfers between devices  47.9 us (41%)
  waiting for transfers between devices  22.6 us (19%)
  local copies, waits for them, and re-layouts  18.7 us (16%)
  Pallas kernels  13 us (11%)
  other arithmetic  9.04 us (8%)
  between operations  3.73 us (3%)
    all_to_all x1, starting transfers between devices, on_device(): words = lax.all_to_all(words, OP, 0, 0, tiled=True)  18.9 us
    all_to_all x1, waiting for transfers between devices, on_device(): blocks = lax.all_to_all(blocks, 'chip', 0, 0, tiled=True)  16.9 us
    pallas_call x1, Pallas kernels, sigma_partial(): pl.pallas_call(functools.partial(sigma_kernel, pairs), grid_spec=pltpu.Pr...  13 us
    all_to_all x1, starting transfers between devices, on_device(): blocks = lax.all_to_all(blocks, 'chip', 0, 0, tiled=True)  12.3 us
    all_to_all x1, starting transfers between devices, on_device(): lax.all_to_all(sums, ('core', 'blk'), 0, 0, tiled=True)  8.44 us
    unnamed x24, local copies, waits for them, and re-layouts  6.96 us
    squeeze x3, local copies, waits for them, and re-layouts, on_device(): lax.dynamic_index_in_dim(array, index, 1, keepdims=False)  4.63 us
    ppermute x1, waiting for transfers between devices, on_device(): halo = lax.ppermute(take(wavefunction, other), ('core', 'blk'), halo_path)  3.41 us
  transfers between devices with their start and end apart: 7, of which 3 were waited for; matrix products, arithmetic and copies ran while one was open for 11% of the time, Pallas kernels for 0%

profile of v1, /device:TPU:1, one launch (start us, length us, event | category | flops | bytes accessed | tf_op | source)
XLA Modules:
  0.0 115.0 jit_solution(9538532637802426072)
XLA Ops:
  0.6 0.5 broadcast.159
  1.1 1.3 %reduce.12 = f32[512]{0:T(512)S(1)} reduce(f32[1,512]{1,0:T(1,128)} %param.13, f32[]{:T(128)} %broadcast.159), dimensions={0}, to_apply=%param.13.reduce_sub_computation.3 | reduce | bytes 4100 | tf_op args[5]
  2.5 0.1 reshape.180
  2.6 0.7 convert_element_type.43
  3.9 0.1 pad_maximum_fusion.1
  4.0 0.6 pad_maximum_fusion
  4.6 18.9 %all-to-all-start = ((f32[128,1,13]{2,1,0:T(1,128)}), f32[128,1,13]{2,1,0:T(1,128)}, u32[]{:S(2)}, u32[]{:S(2)}) async-start(f32[128,1,13]{2,1,0:T(1,128)} %bitcast.2), calls=%async_computation | async-start | bytes 131072 | tf_op jit(solution)/shard_map/all_to_all | solution.py:139
  23.5 0.0 copy-start.1
  23.5 2.6 %dynamic-slice_bitcast_fusion.1 = bf16[4,384,384]{2,1,0:T(8,128)(2,1)} fusion(bf16[4,2,384,384]{3,2,1,0:T(8,128)(2,1)} %left_own.1, s32[]{:T(128)S(6)} %select_n.72), kind=kLoop, calls=%fused_computation.4 | loop fusion | bytes 2359300 | tf_op jit(solution)/shard_map/jit(dynamic_index_in_dim)/squeeze | solution.py:122
  26.1 3.0 %collective-permute-start.1 = (bf16[4,384,384]{2,1,0:T(8,128)(2,1)}, bf16[4,384,384]{2,1,0:T(8,128)(2,1)S(1)}, u32[]{:S(2)}, u32[]{:S(2)}) collective-permute-start(bf16[4,384,384]{2,1,0:T(8,128)(2,1)} %dynamic-slice_bitcast_fusion.1), channel_id=1, source_target_pairs={{0,4},{4,0},{1,5},{5,1},{2,6},{6,2},{3,7},{7,3},{8,12},{12,8},{9,1... | collective-permute-start | bytes 3538952 | tf_op jit(solution)/shard_map/ppermute | solution.py:127
  29.1 0.0 copy-start
  29.1 1.2 %dynamic-slice_bitcast_fusion = bf16[4,384,384]{2,1,0:T(8,128)(2,1)} fusion(bf16[4,2,384,384]{3,2,1,0:T(8,128)(2,1)S(1)} %copy-done.1, s32[]{:T(128)S(6)} %select_n.72), kind=kLoop, calls=%fused_computation.3 | loop fusion | bytes 2359300 | tf_op jit(solution)/shard_map/jit(dynamic_index_in_dim)/squeeze | solution.py:122
  30.3 2.0 %collective-permute-start.2 = (bf16[4,384,384]{2,1,0:T(8,128)(2,1)}, bf16[4,384,384]{2,1,0:T(8,128)(2,1)}, u32[]{:S(2)}, u32[]{:S(2)}) collective-permute-start(bf16[4,384,384]{2,1,0:T(8,128)(2,1)} %dynamic-slice_bitcast_fusion), channel_id=1, source_target_pairs={{0,4},{4,0},{1,5},{5,1},{2,6},{6,2},{3,7},{7,3},{8,12},{12,8},{9,1... | collective-permute-start | bytes 3538952 | tf_op jit(solution)/shard_map/ppermute | solution.py:128
  32.4 0.9 dynamic-slice_bitcast_fusion.2
  33.3 1.3 %collective-permute-start = (bf16[2,384,384]{2,1,0:T(8,128)(2,1)}, bf16[2,384,384]{2,1,0:T(8,128)(2,1)}, u32[]{:S(2)}, u32[]{:S(2)}) collective-permute-start(bf16[2,384,384]{2,1,0:T(8,128)(2,1)} %dynamic-slice_bitcast_fusion.2), channel_id=1, source_target_pairs={{0,1},{1,2},{2,3},{5,4},{6,5},{7,6},{8,9},{9,10},{10,11},{13,12},{... | collective-permute-start | bytes 1769480 | tf_op jit(solution)/shard_map/ppermute | solution.py:126
  34.6 0.1 fusion.16
  34.7 0.6 gather_fusion
  35.3 0.1 and_select_fusion
  36.0 0.6 pad.13.clone
  36.6 0.0 all-to-all-done
  36.6 0.7 fusion.15
  37.3 0.6 copy-done.9
  37.9 0.1 reshape.182
  38.0 0.6 broadcast_select_fusion
  38.5 0.8 reshape.183.weight
  39.3 0.7 fusion.14
  40.0 0.7 or_select_fusion
  40.7 0.1 pad_add_fusion.meta
  40.8 3.4 %collective-permute-done.halo = bf16[2,384,384]{2,1,0:T(8,128)(2,1)} collective-permute-done((bf16[2,384,384]{2,1,0:T(8,128)(2,1)}, bf16[2,384,384]{2,1,0:T(8,128)(2,1)}, u32[]{:S(2)}, u32[]{:S(2)}) %collective-permute-start) | collective-permute-done | bytes 589856 | tf_op jit(solution)/shard_map/ppermute | solution.py:126
  44.2 0.0 collective-permute-done.1.left_got
  44.2 1.0 copy-done.5
  45.2 0.0 collective-permute-done.2.right_got
  45.2 1.7 %copy-done.2 = bf16[4,2,384,384]{3,2,1,0:T(8,128)(2,1)S(1)} copy-done((bf16[4,2,384,384]{3,2,1,0:T(8,128)(2,1)S(1)}, bf16[4,2,384,384]{3,2,1,0:T(8,128)(2,1)}, u32[]{:S(2)}) %copy-start.2) | copy-done | bytes 2359320
  46.9 1.3 %copy-done.4 = bf16[2,2,384,384]{3,2,1,0:T(8,128)(2,1)S(1)} copy-done((bf16[2,2,384,384]{3,2,1,0:T(8,128)(2,1)S(1)}, bf16[2,2,384,384]{3,2,1,0:T(8,128)(2,1)}, u32[]{:S(2)}) %copy-start.4) | copy-done | bytes 1179672
  48.2 1.3 %copy-done.6 = bf16[4,384,384]{2,1,0:T(8,128)(2,1)S(1)} copy-done((bf16[4,384,384]{2,1,0:T(8,128)(2,1)S(1)}, bf16[4,384,384]{2,1,0:T(8,128)(2,1)}, u32[]{:S(2)}) %copy-start.6) | copy-done | bytes 1179672
  49.4 13.0 %sigma_partial.1 = (f32[2,384,384]{2,1,0:T(8,128)S(1)}, f32[8]{0:T(128)S(1)}) custom-call(s32[12]{0:T(128)S(1)} %pad_add_fusion.meta, f32[8]{0:T(128)S(1)} %reshape.183.weight, bf16[2,2,384,384]{3,2,1,0:T(8,128)(2,1)S(1)} %copy-done.4, bf16[2,384,384]{2,1,0:T(8,128)(2,1)} %collective-permute-done.halo, bf16[4,2,384,384]{3,2,1,0:T(8,128)(2,1)S(1)} %copy-done, ...), custom_call_target="tpu_custom_call" | custom-call | flops 3623878656 | bytes 7667712 | tf_op jit(solution)/shard_map/sigma_partial/pallas_call | solution.py:79
  62.5 0.6 slice.45
  63.0 0.7 abs_reduce_fusion
  65.2 0.1 multiply_convert_fusion
  65.3 0.8 copy.56
  66.1 0.2 copy.57
  66.3 0.4 reshape.185
  66.8 0.1 fusion.17
  66.9 0.1 concatenate.33
  67.0 1.1 maximum_maximum_fusion
  68.2 12.3 %all-to-all-start.1 = ((f16[64,40,128]{2,1,0:T(8,128)(2,1)}), f16[64,40,128]{2,1,0:T(8,128)(2,1)S(1)}, u32[]{:S(2)}, u32[]{:S(2)}) async-start(f16[64,40,128]{2,1,0:T(8,128)(2,1)} %maximum_maximum_fusion), calls=%async_computation.1 | async-start | bytes 1310720 | tf_op jit(solution)/shard_map/all_to_all | solution.py:178
  80.5 0.1 dynamic_slice.33
  80.6 0.8 constant_dynamic-slice_fusion
  81.4 0.1 broadcast_compare_fusion
  81.4 0.1 iota_compare_fusion
  81.5 0.1 broadcast_and_fusion
  81.6 0.6 slice.50
  82.2 16.9 %all-to-all-done.1 = f16[64,40,128]{2,1,0:T(8,128)(2,1)S(1)} async-done(((f16[64,40,128]{2,1,0:T(8,128)(2,1)}), f16[64,40,128]{2,1,0:T(8,128)(2,1)S(1)}, u32[]{:S(2)}, u32[]{:S(2)}) %all-to-all-start.1) | async-done | bytes 655392 | tf_op jit(solution)/shard_map/all_to_all | solution.py:178
  99.2 0.2 fusion.1
  99.3 0.1 fusion.6
  99.5 0.1 pad_maximum_fusion.2
  99.6 0.6 broadcast_in_dim.59
  100.2 8.4 %all-to-all-start.2 = ((f32[8,1,4]{2,1,0:T(1,128)}), f32[8,1,4]{2,1,0:T(1,128)S(1)}, u32[]{:S(2)}, u32[]{:S(2)}) async-start(f32[8,1,4]{2,1,0:T(1,128)} %broadcast_in_dim.59), calls=%async_computation.2 | async-start | bytes 8192 | tf_op jit(solution)/shard_map/all_to_all | solution.py:192
  108.6 0.2 multiply_reduce_fusion
  108.9 1.9 %collective-permute-start.3 = (f32[2,3,384]{2,0,1:T(2,128)S(1)}, f32[2,3,384]{2,0,1:T(2,128)S(1)}, u32[]{:S(2)}, u32[]{:S(2)}) collective-permute-start(f32[2,3,384]{2,0,1:T(2,128)S(1)} %bitcast.55), channel_id=1, source_target_pairs={{0,4},{4,0},{1,5},{5,1},{2,6},{6,2},{3,7},{7,3},{8,12},{12,8},{9,1... | collective-permute-start | bytes 27656 | tf_op jit(solution)/shard_map/ppermute | solution.py:188
  110.8 2.3 %all-to-all-done.2 = f32[8,1,4]{2,1,0:T(1,128)S(1)} async-done(((f32[8,1,4]{2,1,0:T(1,128)}), f32[8,1,4]{2,1,0:T(1,128)S(1)}, u32[]{:S(2)}, u32[]{:S(2)}) %all-to-all-start.2) | async-done | bytes 160 | tf_op jit(solution)/shard_map/all_to_all | solution.py:192
  113.1 1.2 %broadcast_subtract_fusion = (f32[2]{0:T(128)S(1)}, f32[2]{0:T(128)}) fusion(f32[]{:T(128)} %bitcast.26, f32[4]{0:T(128)S(1)} %reduce_sum.29), kind=kLoop, calls=%fused_computation.57 | loop fusion | flops 10 | bytes 36 | tf_op jit(solution)/shard_map/sub | solution.py:203
  114.3 0.1 fusion.11
  114.4 0.6 copy.62
  (31 shorter events, 0.3 us)
Async XLA Ops:
  4.6 32.0 %all-to-all-start = ((f32[128,1,13]{2,1,0:T(1,128)}), f32[128,1,13]{2,1,0:T(1,128)}, u32[]{:S(2)}, u32[]{:S(2)}) async-start(f32[128,1,13]{2,1,0:T(1,128)} %bitcast.2), calls=%async_computation | async-start | bytes 131072 | tf_op jit(solution)/shard_map/all_to_all | solution.py:139
  23.5 5.6 %copy-start.1 = (bf16[4,2,384,384]{3,2,1,0:T(8,128)(2,1)S(1)}, bf16[4,2,384,384]{3,2,1,0:T(8,128)(2,1)}, u32[]{:S(2)}) copy-start(bf16[4,2,384,384]{3,2,1,0:T(8,128)(2,1)} %right_own.1) | copy-start | bytes 7077892
  26.1 6.3 %copy-start.3 = (bf16[2,2,384,384]{3,2,1,0:T(8,128)(2,1)S(1)}, bf16[2,2,384,384]{3,2,1,0:T(8,128)(2,1)}, u32[]{:S(2)}) copy-start(bf16[2,2,384,384]{3,2,1,0:T(8,128)(2,1)} %psi.1) | copy-start | bytes 3538948
  26.1 18.1 %collective-permute-start.1 = (bf16[4,384,384]{2,1,0:T(8,128)(2,1)}, bf16[4,384,384]{2,1,0:T(8,128)(2,1)S(1)}, u32[]{:S(2)}, u32[]{:S(2)}) collective-permute-start(bf16[4,384,384]{2,1,0:T(8,128)(2,1)} %dynamic-slice_bitcast_fusion.1), channel_id=1, source_target_pairs={{0,4},{4,0},{1,5},{5,1},{2,6},{6,2},{3,7},{7,3},{8,12},{12,8},{9,1... | collective-permute-start | bytes 3538952 | tf_op jit(solution)/shard_map/ppermute | solution.py:127
  29.1 16.1 %copy-start = (bf16[4,2,384,384]{3,2,1,0:T(8,128)(2,1)S(1)}, bf16[4,2,384,384]{3,2,1,0:T(8,128)(2,1)}, u32[]{:S(2)}) copy-start(bf16[4,2,384,384]{3,2,1,0:T(8,128)(2,1)} %left_own.1) | copy-start | bytes 7077892
  30.3 4.3 %copy-start.7 = (s32[8]{0:T(128)S(1)}, s32[8]{0:T(128)}, u32[]{:S(2)}) copy-start(s32[8]{0:T(128)} %param.12) | copy-start | bytes 100
  30.3 14.9 %collective-permute-start.2 = (bf16[4,384,384]{2,1,0:T(8,128)(2,1)}, bf16[4,384,384]{2,1,0:T(8,128)(2,1)}, u32[]{:S(2)}, u32[]{:S(2)}) collective-permute-start(bf16[4,384,384]{2,1,0:T(8,128)(2,1)} %dynamic-slice_bitcast_fusion), channel_id=1, source_target_pairs={{0,4},{4,0},{1,5},{5,1},{2,6},{6,2},{3,7},{7,3},{8,12},{12,8},{9,1... | collective-permute-start | bytes 3538952 | tf_op jit(solution)/shard_map/ppermute | solution.py:128
  33.3 10.9 %collective-permute-start = (bf16[2,384,384]{2,1,0:T(8,128)(2,1)}, bf16[2,384,384]{2,1,0:T(8,128)(2,1)}, u32[]{:S(2)}, u32[]{:S(2)}) collective-permute-start(bf16[2,384,384]{2,1,0:T(8,128)(2,1)} %dynamic-slice_bitcast_fusion.2), channel_id=1, source_target_pairs={{0,1},{1,2},{2,3},{5,4},{6,5},{7,6},{8,9},{9,10},{10,11},{13,12},{... | collective-permute-start | bytes 1769480 | tf_op jit(solution)/shard_map/ppermute | solution.py:126
  37.3 0.6 copy-start.9
  44.2 1.0 copy-start.5
  45.2 1.7 %copy-start.2 = (bf16[4,2,384,384]{3,2,1,0:T(8,128)(2,1)S(1)}, bf16[4,2,384,384]{3,2,1,0:T(8,128)(2,1)}, u32[]{:S(2)}) copy-start(bf16[4,2,384,384]{3,2,1,0:T(8,128)(2,1)} %right_own.1) | copy-start | bytes 7077892
  46.9 1.3 %copy-start.4 = (bf16[2,2,384,384]{3,2,1,0:T(8,128)(2,1)S(1)}, bf16[2,2,384,384]{3,2,1,0:T(8,128)(2,1)}, u32[]{:S(2)}) copy-start(bf16[2,2,384,384]{3,2,1,0:T(8,128)(2,1)} %psi.1) | copy-start | bytes 3538948
  48.2 1.3 %copy-start.6 = (bf16[4,384,384]{2,1,0:T(8,128)(2,1)S(1)}, bf16[4,384,384]{2,1,0:T(8,128)(2,1)}, u32[]{:S(2)}) copy-start(bf16[4,384,384]{2,1,0:T(8,128)(2,1)} %copy-done.5) | copy-start | bytes 3538948
  66.1 0.9 copy-start.8
  67.0 14.6 %copy-start.10 = (f32[1,13]{1,0:T(1,128)S(1)}, f32[1,13]{1,0:T(1,128)}, u32[]{:S(2)}) copy-start(f32[1,13]{1,0:T(1,128)} %copy-done.9) | copy-start | bytes 160
  68.2 31.0 %all-to-all-start.1 = ((f16[64,40,128]{2,1,0:T(8,128)(2,1)}), f16[64,40,128]{2,1,0:T(8,128)(2,1)S(1)}, u32[]{:S(2)}, u32[]{:S(2)}) async-start(f16[64,40,128]{2,1,0:T(8,128)(2,1)} %maximum_maximum_fusion), calls=%async_computation.1 | async-start | bytes 1310720 | tf_op jit(solution)/shard_map/all_to_all | solution.py:178
  100.2 12.9 %all-to-all-start.2 = ((f32[8,1,4]{2,1,0:T(1,128)}), f32[8,1,4]{2,1,0:T(1,128)S(1)}, u32[]{:S(2)}, u32[]{:S(2)}) async-start(f32[8,1,4]{2,1,0:T(1,128)} %broadcast_in_dim.59), calls=%async_computation.2 | async-start | bytes 8192 | tf_op jit(solution)/shard_map/all_to_all | solution.py:192
  108.9 5.4 %collective-permute-start.3 = (f32[2,3,384]{2,0,1:T(2,128)S(1)}, f32[2,3,384]{2,0,1:T(2,128)S(1)}, u32[]{:S(2)}, u32[]{:S(2)}) collective-permute-start(f32[2,3,384]{2,0,1:T(2,128)S(1)} %bitcast.55), channel_id=1, source_target_pairs={{0,4},{4,0},{1,5},{5,1},{2,6},{6,2},{3,7},{7,3},{8,12},{12,8},{9,1... | collective-permute-start | bytes 27656 | tf_op jit(solution)/shard_map/ppermute | solution.py:188

commit v2 on v0

v2 whole, which is shorter than its diff:
```python
import functools

import jax
import jax.numpy as jnp
from jax import lax
from jax.experimental import pallas as pl
from jax.experimental.pallas import tpu as pltpu
from jax.sharding import Mesh, PartitionSpec as P

F32, F16, BF16 = jnp.float32, jnp.float16, jnp.bfloat16
OP = ("chip", "core")
HEAD, PIECE = 1024.0, 2048.0
TILES = 4
LANES = 128
SMEM = pl.BlockSpec(memory_space=pltpu.SMEM)
VMEM = pl.BlockSpec(memory_space=pltpu.VMEM)
ANY = pl.BlockSpec(memory_space=pl.ANY)


def products(core, shifts, src, left, right, terms, lefts, rights, sems):
    pairs, size = lefts.shape[0], lefts.shape[1]
    for k in range(pairs):
        pltpu.make_async_copy(left.at[k, core], lefts.at[k], sems.at[0, k]).wait()
        slot = core - shifts[k]
        slot = jnp.where((slot == 0) | (slot == 1), slot, 2)
        part = jnp.dot(lefts[k], src[slot], preferred_element_type=F32).astype(BF16)
        pltpu.make_async_copy(right.at[k, core], rights.at[k], sems.at[1, k]).wait()
        for v in range(2):
            terms[k, v] = lax.dot_general(
                part[:, v * size : (v + 1) * size],
                rights[k],
                (((1,), (1,)), ((), ())),
                preferred_element_type=F32,
            )


def start_loads(core, left, right, lefts, rights, sems):
    for k in range(lefts.shape[0]):
        pltpu.make_async_copy(left.at[k, core], lefts.at[k], sems.at[0, k]).start()
        pltpu.make_async_copy(right.at[k, core], rights.at[k], sems.at[1, k]).start()


def own_kernel(
    place, shifts, sizes, psi, halo, left, right, terms, src, psis, halos, lefts, rights, sems, more
):
    core, blk = place[0], place[1]
    psi_copy = pltpu.make_async_copy(psi, psis, more.at[0])
    halo_copy = pltpu.make_async_copy(halo, halos, more.at[1])
    psi_copy.start()
    halo_copy.start()
    start_loads(core, left, right, lefts, rights, sems)
    size = psis.shape[2]
    row = lax.broadcasted_iota(jnp.int32, (size, size), 0)
    col = lax.broadcasted_iota(jnp.int32, (size, size), 1)
    reach = jnp.maximum(row, col)
    far = 2 * blk - 1 + 3 * core
    inside = (far >= 0) & (far < sizes.shape[0])
    far_size = jnp.where(inside, sizes[jnp.clip(far, 0, sizes.shape[0] - 1)], 0)
    for slot, live_size in enumerate((sizes[2 * blk], sizes[2 * blk + 1], far_size)):
        if slot == 0:
            psi_copy.wait()
        if slot == 2:
            halo_copy.wait()
        live = jnp.where(reach < live_size, 1.0, 0.0).astype(BF16)
        for v in range(2):
            block = psis[v, slot] if slot < 2 else halos[v]
            src[slot, :, v * size : (v + 1) * size] = block * live
    products(core, shifts, src, left, right, terms, lefts, rights, sems)


def got_kernel(place, shifts, src, left, right, terms, lefts, rights, sems):
    core = place[0]
    start_loads(core, left, right, lefts, rights, sems)
    products(core, shifts, src, left, right, terms, lefts, rights, sems)


def estimate(pairs, size):
    return pl.CostEstimate(
        flops=8 * pairs * size**3, bytes_accessed=20 * pairs * size * size, transcendentals=0
    )


def load_scratch(pairs, size):
    return [
        pltpu.VMEM((pairs, size, size), BF16),
        pltpu.VMEM((pairs, size, size), BF16),
        pltpu.SemaphoreType.DMA((2, pairs)),
    ]


def own_terms(place, shifts, sizes, psi, halo, left, right):
    pairs, _, size, _ = left.shape
    return pl.pallas_call(
        own_kernel,
        in_specs=[SMEM] * 3 + [ANY] * 4,
        out_specs=[VMEM, VMEM],
        out_shape=[
            jax.ShapeDtypeStruct((pairs, 2, size, size), F32),
            jax.ShapeDtypeStruct((3, size, 2 * size), BF16),
        ],
        scratch_shapes=[pltpu.VMEM(psi.shape, BF16), pltpu.VMEM(halo.shape, BF16)]
        + load_scratch(pairs, size)
        + [pltpu.SemaphoreType.DMA((2,))],
        compiler_params=pltpu.CompilerParams(vmem_limit_bytes=32 * 1024 * 1024),
        cost_estimate=estimate(pairs, size),
        name="own_terms",
    )(place, shifts, sizes, psi, halo, left, right)


def got_terms(place, shifts, src, left, right):
    pairs, _, size, _ = left.shape
    return pl.pallas_call(
        got_kernel,
        in_specs=[SMEM] * 2 + [VMEM] + [ANY] * 2,
        out_specs=VMEM,
        out_shape=jax.ShapeDtypeStruct((pairs, 2, size, size), F32),
        scratch_shapes=load_scratch(pairs, size),
        compiler_params=pltpu.CompilerParams(vmem_limit_bytes=32 * 1024 * 1024),
        cost_estimate=estimate(pairs, size),
        name="got_terms",
    )(place, shifts, src, left, right)


def level_of(top, head):
    return jnp.maximum(jnp.ceil(jnp.log2(jnp.maximum(top, 1e-30))), -90.0) - head


def folded(values):
    rows, columns = values.shape
    total = None
    for r in range(0, rows, 8):
        for c in range(0, columns, LANES):
            part = values[r : r + 8, c : c + LANES]
            total = part if total is None else total + part
    return total


def combine_kernel(chip_rows, place, owner, words, own, got, src, packed, norm, sums):
    step = pl.program_id(0)
    pairs, _, rows, size = own.shape
    core, chip = place[0], place[2]
    here = rows // chip_rows
    parts = size // LANES
    tag = 2 * parts * chip_rows
    tagged = packed.shape[1] - tag
    line = jnp.broadcast_to(words[owner[0], 0:1, :], (8, LANES))
    first = lax.rem(chip * 2 * pairs, LANES)
    own_weight = pltpu.roll(line, LANES - first - core * pairs, 1)
    got_weight = pltpu.roll(line, LANES - first - (1 - core) * pairs, 1)

    @pl.when(step == 0)
    def _():
        sums[...] = jnp.zeros_like(sums)

    totals = []
    for v in range(2):
        total = own_weight[0:1, 0:1] * own[0, v]
        for k in range(1, pairs):
            total += own_weight[0:1, k : k + 1] * own[k, v]
        for k in range(pairs):
            total += got_weight[0:1, k : k + 1] * got[k, v]
        psi = src[0, :, v * size : (v + 1) * size].astype(F32)
        sums[v] += folded(psi * total)
        sums[2 + v] += folded(psi * psi)
        totals.append(total)
    top = jnp.max(jnp.maximum(jnp.abs(totals[0]), jnp.abs(totals[1])), keepdims=True)
    level = level_of(top, 14.0)
    scale = jnp.exp2(-level)
    row = lax.broadcasted_iota(jnp.int32, (tagged, LANES), 0)
    lane = lax.broadcasted_iota(jnp.int32, (tagged, LANES), 1)
    mark = jnp.where(row == 0, level, 0.0)
    for v in range(2):
        scaled = totals[v] * scale
        for j in range(here):
            for t in range(parts):
                at = (v * parts + t) * chip_rows
                packed[step * here + j, at : at + chip_rows, :] = scaled[
                    j * chip_rows : (j + 1) * chip_rows, t * LANES : (t + 1) * LANES
                ]
    for j in range(here):
        packed[step * here + j, tag:, :] = mark

    @pl.when(step == pl.num_programs(0) - 1)
    def _():
        cross = [jnp.sum(sums[v], keepdims=True) for v in range(2)]
        level = level_of(jnp.maximum(jnp.abs(cross[0]), jnp.abs(cross[1])), 0.0)
        values = [level]
        rest = [value * jnp.exp2(-level) * HEAD for value in cross]
        for _ in range(3):
            heads = [jnp.round(value) for value in rest]
            values += heads
            rest = [(value - head) * PIECE for value, head in zip(rest, heads)]
        tags = jnp.zeros((tagged, LANES), F32)
        for i, value in enumerate(values):
            tags = jnp.where((row == 0) & (lane == i + 1), value, tags)
        for j in range(packed.shape[0]):
            packed[j, tag:, :] = jnp.where(lane == 0, packed[j, tag:, :], tags)
        for v in range(2):
            norm[v : v + 1, :] = jnp.broadcast_to(jnp.sum(sums[2 + v], keepdims=True), (1, LANES))


def combined(chips, place, owner, words, own, got, src):
    pairs, _, size, _ = own.shape
    chip_rows = size // chips
    tile = size // TILES
    lines = -(-(2 * chip_rows * size // LANES + 1) // 8) * 8
    whole = lambda shape: pl.BlockSpec(shape, lambda i, p, o: (0,) * len(shape))
    terms = pl.BlockSpec((pairs, 2, tile, size), lambda i, p, o: (0, 0, i, 0))
    return pl.pallas_call(
        functools.partial(combine_kernel, chip_rows),
        grid_spec=pltpu.PrefetchScalarGridSpec(
            num_scalar_prefetch=2,
            grid=(TILES,),
            in_specs=[
                whole(words.shape),
                terms,
                terms,
                pl.BlockSpec((1, tile, 2 * size), lambda i, p, o: (p[0], i, 0)),
            ],
            out_specs=[whole((chips, lines, LANES)), whole((2, LANES))],
            scratch_shapes=[pltpu.VMEM((4, 8, LANES), F32)],
        ),
        out_shape=[
            jax.ShapeDtypeStruct((chips, lines, LANES), F32),
            jax.ShapeDtypeStruct((2, LANES), F32),
        ],
        compiler_params=pltpu.CompilerParams(vmem_limit_bytes=32 * 1024 * 1024),
        name="combined",
    )(place, owner, words, own, got, src)


def on_device(
    wavefunction, left_ops, right_ops, shifts, sector_sizes, site_coef, site_energy, site_owner
):
    size = wavefunction.shape[2]
    pairs = left_ops.shape[0]
    chips, blks = lax.axis_size("chip"), lax.axis_size("blk")
    chip, core, blk = lax.axis_index("chip"), lax.axis_index("core"), lax.axis_index("blk")
    chip_rows = size // chips
    rows = chip_rows // 2
    parts = size // LANES
    place = jnp.stack([core, blk, chip]).astype(jnp.int32)

    swap = [(0, 1), (1, 0)]
    halo_path = [(x, x + 1) for x in range(blks - 1)] + [
        (blks + x + 1, blks + x) for x in range(blks - 1)
    ]
    edge = lax.dynamic_index_in_dim(wavefunction, 1 - core, 1, keepdims=False)
    halo = lax.ppermute(edge, ("core", "blk"), halo_path)
    lines = site_coef.reshape(-1, 1, LANES)
    lines = jnp.broadcast_to(lines, (lines.shape[0], 2 * chips // lines.shape[0], LANES))
    words = jnp.stack(
        [lines.reshape(2 * chips, LANES), jnp.broadcast_to(site_energy[:, None], (2 * chips, LANES))],
        axis=1,
    )
    words = lax.all_to_all(words, OP, 0, 0, tiled=True)
    left_got = lax.ppermute(left_ops, "core", swap)
    right_got = lax.ppermute(right_ops, "core", swap)
    shifts_got = lax.ppermute(shifts, "core", swap)

    own, src = own_terms(place, shifts, sector_sizes, wavefunction, halo, left_ops, right_ops)
    got = got_terms(place, shifts_got, src, left_got, right_got)
    packed, norm = combined(chips, place, site_owner, words, own, got, src)

    blocks = lax.all_to_all(packed.astype(F16), "chip", 0, 0, tiled=True)
    tag = 2 * parts * chip_rows
    tags = blocks[:, tag, :8].astype(F32)
    cross = jnp.sum(
        (tags[:, 2:4] + (tags[:, 4:6] + tags[:, 6:8] / PIECE) / PIECE)
        / HEAD
        * jnp.exp2(tags[:, 1:2]),
        axis=0,
    )
    summed = jnp.sum(blocks[:, :tag].astype(F32) * jnp.exp2(tags[:, 0])[:, None, None], axis=0)

    halves = summed.reshape(2 * parts, 2, rows, LANES).transpose(1, 0, 2, 3)
    halves = halves.reshape(2, 1, 2 * parts * rows, LANES)
    halves = jnp.broadcast_to(halves, (2, blks) + halves.shape[2:])
    sums = jnp.pad(jnp.concatenate([cross, norm[:, 0]]), (0, LANES - 4))
    sums = jnp.broadcast_to(sums[None, None, None], (2, blks, 1, LANES))
    sent = jnp.concatenate([halves, sums], axis=2).reshape(2 * blks, -1, LANES)
    came = lax.all_to_all(sent, ("core", "blk"), 0, 0, tiled=True)
    sums = jnp.sum(came[:, -1, :4], axis=0)
    energy = lax.dynamic_index_in_dim(words[:, 1, 0], site_owner[0], 0, keepdims=False)
    cross_sum, norm_sum = sums[:2], sums[2:]
    rayleigh = (cross_sum + energy * norm_sum) / (norm_sum + 1e-06)
    ours = lax.dynamic_index_in_dim(came.reshape(2, blks, -1, LANES), blk, 1, keepdims=False)
    ours = ours[:, :-1].reshape(2, 2, parts, rows, LANES).transpose(3, 1, 0, 2, 4)
    ours = ours.reshape(rows, 2, 2, size)

    first = (chip * 2 + core) * rows
    own_sizes = lax.dynamic_slice_in_dim(sector_sizes, 2 * blk, 2, 0)[:, None]
    row_ids = (first + jnp.arange(rows, dtype=jnp.int32))[:, None, None, None]
    col_ids = jnp.arange(size, dtype=jnp.int32)
    live = (row_ids < own_sizes) & (col_ids < own_sizes)
    psi_rows = lax.dynamic_slice_in_dim(wavefunction, first, rows, 2)
    psi_rows = psi_rows.transpose(2, 0, 1, 3).astype(F32)
    value = ours + (energy - rayleigh)[None, :, None, None] * psi_rows
    return jnp.where(live, value, 0.0), rayleigh


def solution(mesh):
    ops, blks = mesh.devices.shape
    split = Mesh(mesh.devices.reshape(ops // 2, 2, blks), OP + ("blk",))
    return jax.shard_map(
        on_device,
        mesh=split,
        in_specs=(
            P(None, "blk", None, None),
            P(OP, "blk", None, None),
            P(OP, "blk", None, None),
            P(OP),
            P(),
            P(OP, None),
            P(OP),
            P(),
        ),
        out_specs=(P(OP, None, "blk", None), P()),
        check_vma=False,
    )
```

time: 525 us -> 113 us (0.22)
  blocking collectives: 264 us -> 0 us
  waiting for transfers between devices: 198 us -> 22 us
  starting transfers between devices: 5.31 us -> 48.1 us
  matrix products: 21.7 us -> 0 us
  between operations: 20.6 us -> 2.16 us
  Pallas kernels: 0 us -> 16.5 us
  local copies, waits for them, and re-layouts: 3.61 us -> 19.1 us
    psum x2 -> x0, blocking collectives: 264 us -> none  [the longest x1 255 us: spread(): return lax.psum(kept, axis)]
    psum x1 -> x0, waiting for transfers between devices: 198 us -> none  [on_device(): summed = lax.psum(running * live_float[:, None], 'op')]
    all_to_all x0 -> x3, starting transfers between devices: none -> 33.7 us  [the longest x1 13.8 us: on_device(): words = lax.all_to_all(words, OP, 0, 0, tiled=True)]
    all_to_all x0 -> x3, waiting for transfers between devices: none -> 22 us  [the longest x1 18.4 us: on_device(): blocks = lax.all_to_all(packed.astype(F16), 'chip', 0, 0, tiled=True)]
    dot_general x4 -> x0, matrix products: 21.7 us -> none  [on_device(): jnp.einsum('ivbc,bdc->ivbd', left_part, right_ops[slot], preferred_elemen...]
    pallas_call x0 -> x3, Pallas kernels: none -> 16.5 us  [the longest x1 6.58 us: own_terms(): pl.pallas_call(own_kernel, in_specs=[SMEM] * 3 + [ANY] * 4, out_specs=[VM...]
    unnamed x13 -> x20, local copies, waits for them, and re-layouts: 1.46 us -> 14.9 us
    ppermute x2 -> x4, starting transfers between devices: 5.27 us -> 14.4 us  [the longest x1 8.79 us: on_device(): left_got = lax.ppermute(left_ops, 'core', swap)]
  transfers between devices with their start and end apart: 3 -> 7, of which waited for: 1 -> 2; matrix products, arithmetic and copies ran while one was open for 0% -> 4% of each run, Pallas kernels for 0% -> 12%
where the time goes in v2:
time: 113 us; the launch traced here: 112 us
  starting transfers between devices  48.1 us (43%)
  waiting for transfers between devices  22 us (19%)
  local copies, waits for them, and re-layouts  19.1 us (17%)
  Pallas kernels  16.5 us (15%)
  other arithmetic  4.45 us (4%)
  between operations  2.16 us (2%)
    all_to_all x1, waiting for transfers between devices, on_device(): blocks = lax.all_to_all(packed.astype(F16), 'chip', 0, 0, tiled=True)  18.4 us
    unnamed x20, local copies, waits for them, and re-layouts  14.9 us
    all_to_all x1, starting transfers between devices, on_device(): words = lax.all_to_all(words, OP, 0, 0, tiled=True)  13.8 us
    all_to_all x1, starting transfers between devices, on_device(): blocks = lax.all_to_all(packed.astype(F16), 'chip', 0, 0, tiled=True)  12.8 us
    ppermute x1, starting transfers between devices, on_device(): left_got = lax.ppermute(left_ops, 'core', swap)  8.79 us
    all_to_all x1, starting transfers between devices, on_device(): came = lax.all_to_all(sent, ('core', 'blk'), 0, 0, tiled=True)  7.17 us
    pallas_call x1, Pallas kernels, own_terms(): pl.pallas_call(own_kernel, in_specs=[SMEM] * 3 + [ANY] * 4, out_specs=[VM...  6.58 us
    pallas_call x1, Pallas kernels, got_terms(): pl.pallas_call(got_kernel, in_specs=[SMEM] * 2 + [VMEM] + [ANY] * 2, out_...  6.41 us
  transfers between devices with their start and end apart: 7, of which 2 were waited for; matrix products, arithmetic and copies ran while one was open for 4% of the time, Pallas kernels for 12%

profile of v2, /device:TPU:1, one launch (start us, length us, event | category | flops | bytes accessed | tf_op | source)
XLA Modules:
  0.0 112.3 jit_solution(10704750582400999399)
XLA Ops:
  0.6 8.8 %collective-permute-start.2 = (bf16[4,2,384,384]{3,2,1,0:T(8,128)(2,1)}, bf16[4,2,384,384]{3,2,1,0:T(8,128)(2,1)}, u32[]{:S(2)}, u32[]{:S(2)}) collective-permute-start(bf16[4,2,384,384]{3,2,1,0:T(8,128)(2,1)} %left.1), channel_id=1, source_target_pairs={{0,4},{4,0},{1,5},{5,1},{2,6},{6,2},{3,7},{7,3},{8,12},{12,8},{9,1... | collective-permute-start | bytes 7077896 | tf_op jit(solution)/shard_map/ppermute | solution.py:257
  9.4 1.9 %collective-permute-start.3 = (bf16[4,2,384,384]{3,2,1,0:T(8,128)(2,1)}, bf16[4,2,384,384]{3,2,1,0:T(8,128)(2,1)}, u32[]{:S(2)}, u32[]{:S(2)}) collective-permute-start(bf16[4,2,384,384]{3,2,1,0:T(8,128)(2,1)} %right.1), channel_id=1, source_target_pairs={{0,4},{4,0},{1,5},{5,1},{2,6},{6,2},{3,7},{7,3},{8,12},{12,8},{9,1... | collective-permute-start | bytes 7077896 | tf_op jit(solution)/shard_map/ppermute | solution.py:258
  11.4 1.1 %dynamic-slice_bitcast_fusion = bf16[2,384,384]{2,1,0:T(8,128)(2,1)S(1)} fusion(bf16[2,2,384,384]{3,2,1,0:T(8,128)(2,1)} %psi.1, s32[]{:T(128)S(6)} %select_n.23), kind=kLoop, calls=%fused_computation.1 | loop fusion | bytes 1179652 | tf_op jit(solution)/shard_map/jit(dynamic_index_in_dim)/squeeze | solution.py:248
  12.5 1.3 %collective-permute-start = (bf16[2,384,384]{2,1,0:T(8,128)(2,1)S(1)}, bf16[2,384,384]{2,1,0:T(8,128)(2,1)S(1)}, u32[]{:S(2)}, u32[]{:S(2)}) collective-permute-start(bf16[2,384,384]{2,1,0:T(8,128)(2,1)S(1)} %dynamic-slice_bitcast_fusion), channel_id=1, source_target_pairs={{0,1},{1,2},{2,3},{5,4},{6,5},{7,6},{8,9},{9,10},{10,11},{13,12},{... | collective-permute-start | bytes 1769480 | tf_op jit(solution)/shard_map/ppermute | solution.py:249
  13.8 2.4 %collective-permute-start.1 = (s32[4]{0:T(128)}, s32[4]{0:T(128)S(1)}, u32[]{:S(2)}, u32[]{:S(2)}) collective-permute-start(s32[4]{0:T(128)} %shifts.1), channel_id=1, source_target_pairs={{0,4},{4,0},{1,5},{5,1},{2,6},{6,2},{3,7},{7,3},{8,12},{12,8},{9,1... | collective-permute-start | bytes 56 | tf_op jit(solution)/shard_map/ppermute | solution.py:259
  16.9 0.7 broadcast_in_dim.20
  17.6 0.7 stack.19
  18.3 13.8 %all-to-all-start = ((f32[128,2,128]{2,1,0:T(2,128)}), f32[128,2,128]{2,1,0:T(2,128)S(1)}, u32[]{:S(2)}, u32[]{:S(2)}) async-start(f32[128,2,128]{2,1,0:T(2,128)} %stack.19), calls=%async_computation | async-start | bytes 262144 | tf_op jit(solution)/shard_map/all_to_all | solution.py:256
  32.7 0.1 pad_add_fusion.place
  32.8 0.0 collective-permute-done.halo
  32.8 0.0 copy-start.4
  32.8 1.3 %copy-done.4 = bf16[2,2,384,384]{3,2,1,0:T(8,128)(2,1)S(1)} copy-done((bf16[2,2,384,384]{3,2,1,0:T(8,128)(2,1)S(1)}, bf16[2,2,384,384]{3,2,1,0:T(8,128)(2,1)}, u32[]{:S(2)}) %copy-start.4) | copy-done | bytes 1179672
  34.1 0.0 copy-start.5
  34.1 1.7 %copy-done.5 = bf16[4,2,384,384]{3,2,1,0:T(8,128)(2,1)S(1)} copy-done((bf16[4,2,384,384]{3,2,1,0:T(8,128)(2,1)S(1)}, bf16[4,2,384,384]{3,2,1,0:T(8,128)(2,1)}, u32[]{:S(2)}) %copy-start.5) | copy-done | bytes 2359320
  35.7 0.0 copy-start.6
  35.7 1.7 %copy-done.6 = bf16[4,2,384,384]{3,2,1,0:T(8,128)(2,1)S(1)} copy-done((bf16[4,2,384,384]{3,2,1,0:T(8,128)(2,1)S(1)}, bf16[4,2,384,384]{3,2,1,0:T(8,128)(2,1)}, u32[]{:S(2)}) %copy-start.6) | copy-done | bytes 2359320
  37.4 0.0 copy-start.7
  37.4 0.7 copy-done.7
  38.1 0.0 copy-start.8
  38.1 0.7 copy-done.8
  38.7 6.6 %own_terms.1 = (f32[4,2,384,384]{3,2,1,0:T(8,128)S(1)}, bf16[3,384,768]{2,1,0:T(8,128)(2,1)S(1)}) custom-call(s32[3]{0:T(128)S(1)} %pad_add_fusion.place, s32[4]{0:T(128)S(1)} %copy-done.7, s32[8]{0:T(128)S(1)} %copy-done.8, bf16[2,2,384,384]{3,2,1,0:T(8,128)(2,1)S(1)} %copy-done.4, bf16[2,384,384]{2,1,0:T(8,128)(2,1)S(1)} %collective-permute-done.halo, ...), custom_call_target="tpu_custom_call" | custom-call | flops 1811939328 | bytes 11796480 | tf_op jit(solution)/shard_map/own_terms/pallas_call | solution.py:93
  45.3 0.0 copy-start.2
  45.3 2.1 %copy-done.2 = f32[4,2,384,384]{3,2,1,0:T(8,128)} copy-done((f32[4,2,384,384]{3,2,1,0:T(8,128)}, f32[4,2,384,384]{3,2,1,0:T(8,128)S(1)}, u32[]{:S(2)}) %copy-start.2) | copy-done | bytes 4718616
  47.4 0.0 collective-permute-done.1.shifts
  47.4 0.0 collective-permute-done.2.left
  47.4 0.0 collective-permute-done.3.right
  47.4 6.4 %got_terms.1.got = f32[4,2,384,384]{3,2,1,0:T(8,128)S(1)} custom-call(s32[3]{0:T(128)S(1)} %pad_add_fusion.place, s32[4]{0:T(128)S(1)} %collective-permute-done.1.shifts, bf16[3,384,768]{2,1,0:T(8,128)(2,1)S(1)} %get-tuple-element.7.src, bf16[4,2,384,384]{3,2,1,0:T(8,128)(2,1)} %collective-permute-done.2.left, ...), custom_call_target="tpu_custom_call" | custom-call | flops 1811939328 | bytes 11796480 | tf_op jit(solution)/shard_map/got_terms/pallas_call | solution.py:112
  53.9 0.0 copy-start
  53.9 2.2 %copy-done = f32[4,2,384,384]{3,2,1,0:T(8,128)} copy-done((f32[4,2,384,384]{3,2,1,0:T(8,128)}, f32[4,2,384,384]{3,2,1,0:T(8,128)S(1)}, u32[]{:S(2)}) %copy-start) | copy-done | bytes 4718616
  56.0 0.0 all-to-all-done.words
  56.0 0.0 copy-start.1
  56.0 2.3 %copy-done.1 = f32[4,2,384,384]{3,2,1,0:T(8,128)S(1)} copy-done((f32[4,2,384,384]{3,2,1,0:T(8,128)S(1)}, f32[4,2,384,384]{3,2,1,0:T(8,128)}, u32[]{:S(2)}) %copy-start.1) | copy-done | bytes 4718616
  58.4 0.0 copy-start.3
  58.4 2.3 %copy-done.3 = f32[4,2,384,384]{3,2,1,0:T(8,128)S(1)} copy-done((f32[4,2,384,384]{3,2,1,0:T(8,128)S(1)}, f32[4,2,384,384]{3,2,1,0:T(8,128)}, u32[]{:S(2)}) %copy-start.3) | copy-done | bytes 4718616
  60.7 3.5 %combined.1 = (f32[64,40,128]{2,1,0:T(8,128)S(1)}, f32[2,128]{1,0:T(2,128)S(1)}) custom-call(s32[3]{0:T(128)S(1)} %pad_add_fusion.place, s32[1]{0:T(128)} %copy.26.owner, f32[128,2,128]{2,1,0:T(2,128)S(1)} %all-to-all-done.words, f32[4,2,384,384]{3,2,1,0:T(8,128)S(1)} %copy-done.3, f32[4,2,384,384]{3,2,1,0:T(8,128)S(1)} %copy-done.1, ...), custom_call_target="tpu_custom_call" | custom-call | tf_op jit(solution)/shard_map/combined/pallas_call | solution.py:209
  64.2 0.0 copy-start.9
  64.2 0.9 convert_element_type.18
  65.1 12.8 %all-to-all-start.1 = ((f16[64,40,128]{2,1,0:T(8,128)(2,1)}), f16[64,40,128]{2,1,0:T(8,128)(2,1)S(1)}, u32[]{:S(2)}, u32[]{:S(2)}) async-start(f16[64,40,128]{2,1,0:T(8,128)(2,1)} %convert_element_type.18), calls=%async_computation.1 | async-start | bytes 1310720 | tf_op jit(solution)/shard_map/all_to_all | solution.py:265
  77.9 0.0 copy-done.9
  77.9 0.1 dynamic_slice.18
  78.0 0.1 broadcast_compare_fusion
  78.1 0.1 iota_compare_fusion
  78.1 0.1 broadcast_and_fusion
  78.2 0.1 slice_reduce_fusion.1
  78.3 18.4 %all-to-all-done.1 = f16[64,40,128]{2,1,0:T(8,128)(2,1)S(1)} async-done(((f16[64,40,128]{2,1,0:T(8,128)(2,1)}), f16[64,40,128]{2,1,0:T(8,128)(2,1)S(1)}, u32[]{:S(2)}, u32[]{:S(2)}) %all-to-all-start.1) | async-done | bytes 655392 | tf_op jit(solution)/shard_map/all_to_all | solution.py:265
  96.8 0.2 fusion.9
  97.0 0.2 multiply_reduce_fusion
  97.2 0.1 fusion.7
  97.3 0.1 fusion.11
  97.5 0.7 pad_maximum_fusion
  98.1 7.2 %all-to-all-start.2 = ((f32[8,19,128]{2,1,0:T(8,128)}), f32[8,19,128]{2,1,0:T(8,128)S(1)}, u32[]{:S(2)}, u32[]{:S(2)}) async-start(f32[8,19,128]{2,1,0:T(8,128)} %bitcast.10), calls=%async_computation.2 | async-start | bytes 196608 | tf_op jit(solution)/shard_map/all_to_all | solution.py:282
  105.3 0.8 constant_dynamic-slice_fusion
  106.1 0.1 slice.60
  106.2 0.5 constant_dynamic-slice_fusion.1
  106.7 3.6 %all-to-all-done.2 = f32[8,19,128]{2,1,0:T(8,128)S(1)} async-done(((f32[8,19,128]{2,1,0:T(8,128)}), f32[8,19,128]{2,1,0:T(8,128)S(1)}, u32[]{:S(2)}, u32[]{:S(2)}) %all-to-all-start.2) | async-done | bytes 77856 | tf_op jit(solution)/shard_map/all_to_all | solution.py:282
  110.4 1.2 %broadcast_subtract_fusion = (f32[2]{0:T(128)S(1)}, f32[2]{0:T(128)}) fusion(f32[]{:T(128)} %bitcast.16, f32[4]{0:T(128)S(1)} %slice_reduce_fusion), kind=kLoop, calls=%fused_computation.33 | loop fusion | flops 10 | bytes 36 | tf_op jit(solution)/shard_map/sub | solution.py:298
  111.7 0.7 fusion.10
  (13 shorter events, 0.2 us)
Async XLA Ops:
  0.6 46.8 %collective-permute-start.2 = (bf16[4,2,384,384]{3,2,1,0:T(8,128)(2,1)}, bf16[4,2,384,384]{3,2,1,0:T(8,128)(2,1)}, u32[]{:S(2)}, u32[]{:S(2)}) collective-permute-start(bf16[4,2,384,384]{3,2,1,0:T(8,128)(2,1)} %left.1), channel_id=1, source_target_pairs={{0,4},{4,0},{1,5},{5,1},{2,6},{6,2},{3,7},{7,3},{8,12},{12,8},{9,1... | collective-permute-start | bytes 7077896 | tf_op jit(solution)/shard_map/ppermute | solution.py:257
  9.4 38.0 %collective-permute-start.3 = (bf16[4,2,384,384]{3,2,1,0:T(8,128)(2,1)}, bf16[4,2,384,384]{3,2,1,0:T(8,128)(2,1)}, u32[]{:S(2)}, u32[]{:S(2)}) collective-permute-start(bf16[4,2,384,384]{3,2,1,0:T(8,128)(2,1)} %right.1), channel_id=1, source_target_pairs={{0,4},{4,0},{1,5},{5,1},{2,6},{6,2},{3,7},{7,3},{8,12},{12,8},{9,1... | collective-permute-start | bytes 7077896 | tf_op jit(solution)/shard_map/ppermute | solution.py:258
  12.5 20.3 %collective-permute-start = (bf16[2,384,384]{2,1,0:T(8,128)(2,1)S(1)}, bf16[2,384,384]{2,1,0:T(8,128)(2,1)S(1)}, u32[]{:S(2)}, u32[]{:S(2)}) collective-permute-start(bf16[2,384,384]{2,1,0:T(8,128)(2,1)S(1)} %dynamic-slice_bitcast_fusion), channel_id=1, source_target_pairs={{0,1},{1,2},{2,3},{5,4},{6,5},{7,6},{8,9},{9,10},{10,11},{13,12},{... | collective-permute-start | bytes 1769480 | tf_op jit(solution)/shard_map/ppermute | solution.py:249
  13.8 33.6 %collective-permute-start.1 = (s32[4]{0:T(128)}, s32[4]{0:T(128)S(1)}, u32[]{:S(2)}, u32[]{:S(2)}) collective-permute-start(s32[4]{0:T(128)} %shifts.1), channel_id=1, source_target_pairs={{0,4},{4,0},{1,5},{5,1},{2,6},{6,2},{3,7},{7,3},{8,12},{12,8},{9,1... | collective-permute-start | bytes 56 | tf_op jit(solution)/shard_map/ppermute | solution.py:259
  18.3 37.7 %all-to-all-start = ((f32[128,2,128]{2,1,0:T(2,128)}), f32[128,2,128]{2,1,0:T(2,128)S(1)}, u32[]{:S(2)}, u32[]{:S(2)}) async-start(f32[128,2,128]{2,1,0:T(2,128)} %stack.19), calls=%async_computation | async-start | bytes 262144 | tf_op jit(solution)/shard_map/all_to_all | solution.py:256
  32.8 1.3 %copy-start.4 = (bf16[2,2,384,384]{3,2,1,0:T(8,128)(2,1)S(1)}, bf16[2,2,384,384]{3,2,1,0:T(8,128)(2,1)}, u32[]{:S(2)}) copy-start(bf16[2,2,384,384]{3,2,1,0:T(8,128)(2,1)} %psi.1) | copy-start | bytes 3538948
  34.1 1.7 %copy-start.5 = (bf16[4,2,384,384]{3,2,1,0:T(8,128)(2,1)S(1)}, bf16[4,2,384,384]{3,2,1,0:T(8,128)(2,1)}, u32[]{:S(2)}) copy-start(bf16[4,2,384,384]{3,2,1,0:T(8,128)(2,1)} %left.1) | copy-start | bytes 7077892
  35.7 1.7 %copy-start.6 = (bf16[4,2,384,384]{3,2,1,0:T(8,128)(2,1)S(1)}, bf16[4,2,384,384]{3,2,1,0:T(8,128)(2,1)}, u32[]{:S(2)}) copy-start(bf16[4,2,384,384]{3,2,1,0:T(8,128)(2,1)} %right.1) | copy-start | bytes 7077892
  37.4 0.7 copy-start.7
  38.1 0.7 copy-start.8
  45.3 2.1 %copy-start.2 = (f32[4,2,384,384]{3,2,1,0:T(8,128)}, f32[4,2,384,384]{3,2,1,0:T(8,128)S(1)}, u32[]{:S(2)}) copy-start(f32[4,2,384,384]{3,2,1,0:T(8,128)S(1)} %get-tuple-element.6.own) | copy-start | bytes 14155780
  53.9 2.2 %copy-start = (f32[4,2,384,384]{3,2,1,0:T(8,128)}, f32[4,2,384,384]{3,2,1,0:T(8,128)S(1)}, u32[]{:S(2)}) copy-start(f32[4,2,384,384]{3,2,1,0:T(8,128)S(1)} %got_terms.1.got) | copy-start | bytes 14155780
  56.0 2.3 %copy-start.1 = (f32[4,2,384,384]{3,2,1,0:T(8,128)S(1)}, f32[4,2,384,384]{3,2,1,0:T(8,128)}, u32[]{:S(2)}) copy-start(f32[4,2,384,384]{3,2,1,0:T(8,128)} %copy-done) | copy-start | bytes 14155780
  58.4 2.3 %copy-start.3 = (f32[4,2,384,384]{3,2,1,0:T(8,128)S(1)}, f32[4,2,384,384]{3,2,1,0:T(8,128)}, u32[]{:S(2)}) copy-start(f32[4,2,384,384]{3,2,1,0:T(8,128)} %copy-done.2) | copy-start | bytes 14155780
  64.2 13.7 %copy-start.9 = (s32[8]{0:T(128)S(1)}, s32[8]{0:T(128)}, u32[]{:S(2)}) copy-start(s32[8]{0:T(128)} %sizes.1) | copy-start | bytes 100
  65.1 31.6 %all-to-all-start.1 = ((f16[64,40,128]{2,1,0:T(8,128)(2,1)}), f16[64,40,128]{2,1,0:T(8,128)(2,1)S(1)}, u32[]{:S(2)}, u32[]{:S(2)}) async-start(f16[64,40,128]{2,1,0:T(8,128)(2,1)} %convert_element_type.18), calls=%async_computation.1 | async-start | bytes 1310720 | tf_op jit(solution)/shard_map/all_to_all | solution.py:265
  98.1 12.2 %all-to-all-start.2 = ((f32[8,19,128]{2,1,0:T(8,128)}), f32[8,19,128]{2,1,0:T(8,128)S(1)}, u32[]{:S(2)}, u32[]{:S(2)}) async-start(f32[8,19,128]{2,1,0:T(8,128)} %bitcast.10), calls=%async_computation.2 | async-start | bytes 196608 | tf_op jit(solution)/shard_map/all_to_all | solution.py:282

commit v3 on v2

v3 whole, which is shorter than its diff:
```python
import functools

import jax
import jax.numpy as jnp
from jax import lax
from jax.experimental import pallas as pl
from jax.experimental.pallas import tpu as pltpu
from jax.sharding import Mesh, PartitionSpec as P

F32, F16, BF16 = jnp.float32, jnp.float16, jnp.bfloat16
OP = ("chip", "core")
HEAD, PIECE = 1024.0, 2048.0
TILES = 4
LANES = 128
SMEM = pl.BlockSpec(memory_space=pltpu.SMEM)
VMEM = pl.BlockSpec(memory_space=pltpu.VMEM)
HBM = pl.BlockSpec(memory_space=pltpu.HBM)
CORE, BLK, CHIP, SHIFTS = 0, 1, 2, 3


def loads(core, left, right, lefts, rights, sems):
    return [
        (
            pltpu.make_async_copy(left.at[k, core], lefts.at[k], sems.at[0, k]),
            pltpu.make_async_copy(right.at[k, core], rights.at[k], sems.at[1, k]),
        )
        for k in range(lefts.shape[0])
    ]


def product(core, shift, src, left, right, copies):
    size = left.shape[0]
    copies[0].wait()
    slot = core - shift
    slot = jnp.where((slot == 0) | (slot == 1), slot, 2)
    part = jnp.dot(left[...], src[slot], preferred_element_type=F32).astype(BF16)
    copies[1].wait()
    return [
        lax.dot_general(
            part[:, v * size : (v + 1) * size],
            right[...],
            (((1,), (1,)), ((), ())),
            preferred_element_type=F32,
        )
        for v in range(2)
    ]


def own_kernel(
    sectors, table, psi, halo, left, right, left_got, right_got, terms, sources,
    psis, halos, lefts, rights, made, src, sems, out_sems, more,
):
    core, blk = table[CORE], table[BLK]
    pairs, size = lefts.shape[0], lefts.shape[1]
    psi_copy = pltpu.make_async_copy(psi, psis, more.at[0])
    halo_copy = pltpu.make_async_copy(halo, halos, more.at[1])
    psi_copy.start()
    halo_copy.start()
    copies = loads(core, left, right, lefts, rights, sems)
    for pair in copies:
        for copy in pair:
            copy.start()
    row = lax.broadcasted_iota(jnp.int32, (size, size), 0)
    col = lax.broadcasted_iota(jnp.int32, (size, size), 1)
    reach = jnp.maximum(row, col)
    sizes = SHIFTS + pairs
    far = 2 * blk - 1 + 3 * core
    inside = (far >= 0) & (far < sectors)
    far_size = jnp.where(inside, table[sizes + jnp.clip(far, 0, sectors - 1)], 0)
    live_sizes = (table[sizes + 2 * blk], table[sizes + 2 * blk + 1], far_size)
    psi_copy.wait()
    halo_copy.wait()
    for slot, live_size in enumerate(live_sizes):
        live = jnp.where(reach < live_size, 1.0, 0.0).astype(BF16)
        for v in range(2):
            block = psis[v, slot] if slot < 2 else halos[v]
            src[slot, :, v * size : (v + 1) * size] = block * live
    source_copy = pltpu.make_async_copy(src, sources, more.at[2])
    source_copy.start()
    outs = []
    for k in range(pairs):
        terms_k = product(core, table[SHIFTS + k], src, lefts.at[k], rights.at[k], copies[k])
        for v in range(2):
            made[k, v] = terms_k[v]
        outs.append(pltpu.make_async_copy(made.at[k], terms.at[k], out_sems.at[k]))
        outs[k].start()
    source_copy.wait()
    for out in outs:
        out.wait()


def estimate(pairs, size):
    return pl.CostEstimate(
        flops=8 * pairs * size**3, bytes_accessed=20 * pairs * size * size, transcendentals=0
    )


def own_terms(sectors, table, psi, halo, left, right, left_got, right_got):
    pairs, _, size, _ = left.shape
    return pl.pallas_call(
        functools.partial(own_kernel, sectors),
        in_specs=[SMEM] + [HBM] * 6,
        out_specs=[HBM, HBM],
        out_shape=[
            jax.ShapeDtypeStruct((pairs, 2, size, size), F32),
            jax.ShapeDtypeStruct((3, size, 2 * size), BF16),
        ],
        scratch_shapes=[
            pltpu.VMEM(psi.shape, BF16),
            pltpu.VMEM(halo.shape, BF16),
            pltpu.VMEM((pairs, size, size), BF16),
            pltpu.VMEM((pairs, size, size), BF16),
            pltpu.VMEM((pairs, 2, size, size), F32),
            pltpu.VMEM((3, size, 2 * size), BF16),
            pltpu.SemaphoreType.DMA((2, pairs)),
            pltpu.SemaphoreType.DMA((pairs,)),
            pltpu.SemaphoreType.DMA((3,)),
        ],
        compiler_params=pltpu.CompilerParams(vmem_limit_bytes=62_850_000),
        cost_estimate=estimate(pairs, size),
        name="own_terms",
    )(table, psi, halo, left, right, left_got, right_got)


def level_of(top, head):
    return jnp.maximum(jnp.ceil(jnp.log2(jnp.maximum(top, 1e-30))), -90.0) - head


def folded(values):
    rows, columns = values.shape
    total = None
    for r in range(0, rows, 8):
        for c in range(0, columns, LANES):
            part = values[r : r + 8, c : c + LANES]
            total = part if total is None else total + part
    return total


def sigma_kernel(
    table, owner, words, own, sources, left, right, packed, norm,
    lefts, rights, owns, src, acc, sems, own_sems, more,
):
    core, chip = table[CORE], table[CHIP]
    pairs, size = lefts.shape[0], lefts.shape[1]
    source_copy = pltpu.make_async_copy(sources, src, more.at[0])
    source_copy.start()
    copies = loads(core, left, right, lefts, rights, sems)
    own_copies = [
        pltpu.make_async_copy(own.at[k], owns.at[k], own_sems.at[k]) for k in range(pairs)
    ]
    for k in range(pairs):
        copies[k][0].start()
        copies[k][1].start()
        own_copies[k].start()

    chips = packed.shape[0]
    chip_rows = size // chips
    parts = size // LANES
    tag = 2 * parts * chip_rows
    tagged = packed.shape[1] - tag
    line = jnp.broadcast_to(words[owner[0], 0:1, :], (8, LANES))
    first = lax.rem(chip * 2 * pairs, LANES)
    own_weight = pltpu.roll(line, LANES - first - core * pairs, 1)
    got_weight = pltpu.roll(line, LANES - first - (1 - core) * pairs, 1)
    facts = words[2 * chip + 1 - core, 1:2, :]
    spot = lax.broadcasted_iota(jnp.int32, (1, LANES), 1)
    shifts = [
        jnp.sum(jnp.where(spot == 1 + k, facts, 0.0)).astype(jnp.int32) for k in range(pairs)
    ]

    source_copy.wait()
    for k in range(pairs):
        terms = product(core, shifts[k], src, lefts.at[k], rights.at[k], copies[k])
        own_copies[k].wait()
        for v in range(2):
            total = got_weight[0:1, k : k + 1] * terms[v] + own_weight[0:1, k : k + 1] * owns[k, v]
            acc[v] = total if k == 0 else acc[v] + total

    tile = size // TILES
    here = chips // TILES
    row = lax.broadcasted_iota(jnp.int32, (tagged, LANES), 0)
    lane = lax.broadcasted_iota(jnp.int32, (tagged, LANES), 1)
    sums = [None] * 4
    for step in range(TILES):
        rows = slice(step * tile, (step + 1) * tile)
        top = None
        for v in range(2):
            total = acc[v, rows, :]
            psi = src[core, rows, v * size : (v + 1) * size].astype(F32)
            for i, part in ((v, folded(psi * total)), (2 + v, folded(psi * psi))):
                sums[i] = part if sums[i] is None else sums[i] + part
            high = jnp.max(jnp.abs(total), keepdims=True)
            top = high if top is None else jnp.maximum(top, high)
        level = level_of(top, 14.0)
        scale = jnp.exp2(-level)
        mark = jnp.where(row == 0, level, 0.0)
        for v in range(2):
            for j in range(here):
                chip_at = step * here + j
                for t in range(parts):
                    at = (v * parts + t) * chip_rows
                    packed[chip_at, at : at + chip_rows, :] = scale * acc[
                        v, chip_at * chip_rows : (chip_at + 1) * chip_rows, t * LANES : (t + 1) * LANES
                    ]
        for j in range(here):
            packed[step * here + j, tag:, :] = mark

    cross = [jnp.sum(sums[v], keepdims=True) for v in range(2)]
    level = level_of(jnp.maximum(jnp.abs(cross[0]), jnp.abs(cross[1])), 0.0)
    values = [level]
    rest = [value * jnp.exp2(-level) * HEAD for value in cross]
    for _ in range(3):
        heads = [jnp.round(value) for value in rest]
        values += heads
        rest = [(value - head) * PIECE for value, head in zip(rest, heads)]
    tags = jnp.zeros((tagged, LANES), F32)
    for i, value in enumerate(values):
        tags = jnp.where((row == 0) & (lane == i + 1), value, tags)
    for j in range(chips):
        packed[j, tag:, :] = jnp.where(lane == 0, packed[j, tag:, :], tags)
    for v in range(2):
        norm[v : v + 1, :] = jnp.broadcast_to(jnp.sum(sums[2 + v], keepdims=True), (1, LANES))


def sigma_blocks(chips, table, owner, words, own, sources, left, right):
    pairs, _, size, _ = left.shape
    lines = -(-(2 * size * size // chips // LANES + 1) // 8) * 8
    return pl.pallas_call(
        sigma_kernel,
        in_specs=[SMEM] * 2 + [VMEM] + [HBM] * 4,
        out_specs=[VMEM, VMEM],
        out_shape=[
            jax.ShapeDtypeStruct((chips, lines, LANES), F32),
            jax.ShapeDtypeStruct((2, LANES), F32),
        ],
        scratch_shapes=[
            pltpu.VMEM((pairs, size, size), BF16),
            pltpu.VMEM((pairs, size, size), BF16),
            pltpu.VMEM((pairs, 2, size, size), F32),
            pltpu.VMEM((3, size, 2 * size), BF16),
            pltpu.VMEM((2, size, size), F32),
            pltpu.SemaphoreType.DMA((2, pairs)),
            pltpu.SemaphoreType.DMA((pairs,)),
            pltpu.SemaphoreType.DMA((1,)),
        ],
        compiler_params=pltpu.CompilerParams(vmem_limit_bytes=61_880_000),
        cost_estimate=estimate(pairs, size),
        name="sigma_blocks",
    )(table, owner, words, own, sources, left, right)


def on_device(
    wavefunction, left_ops, right_ops, shifts, sector_sizes, site_coef, site_energy, site_owner
):
    size = wavefunction.shape[2]
    pairs = left_ops.shape[0]
    chips, blks = lax.axis_size("chip"), lax.axis_size("blk")
    chip, core, blk = lax.axis_index("chip"), lax.axis_index("core"), lax.axis_index("blk")
    chip_rows = size // chips
    rows = chip_rows // 2
    parts = size // LANES
    table = jnp.concatenate(
        [jnp.stack([core, blk, chip]).astype(jnp.int32), shifts, sector_sizes]
    )

    swap = [(0, 1), (1, 0)]
    halo_path = [(x, x + 1) for x in range(blks - 1)] + [
        (blks + x + 1, blks + x) for x in range(blks - 1)
    ]
    edge = lax.dynamic_index_in_dim(wavefunction, 1 - core, 1, keepdims=False)
    halo = lax.ppermute(edge, ("core", "blk"), halo_path)
    lines = site_coef.reshape(-1, 1, LANES)
    lines = jnp.broadcast_to(lines, (lines.shape[0], 2 * chips // lines.shape[0], LANES))
    facts = jnp.concatenate([site_energy, shifts.astype(F32)])
    facts = jnp.pad(facts, (0, LANES - 1 - pairs))
    words = jnp.stack(
        [lines.reshape(2 * chips, LANES), jnp.broadcast_to(facts, (2 * chips, LANES))], axis=1
    )
    words = lax.all_to_all(words, OP, 0, 0, tiled=True)
    left_got = lax.ppermute(left_ops, "core", swap)
    right_got = lax.ppermute(right_ops, "core", swap)
    own, sources = own_terms(
        sector_sizes.shape[0],
        table,
        wavefunction,
        halo,
        left_ops,
        right_ops,
        left_got,
        right_got,
    )
    packed, norm = sigma_blocks(
        chips, table, site_owner, words, own, sources, left_got, right_got
    )

    blocks = lax.all_to_all(packed.astype(F16), "chip", 0, 0, tiled=True)
    tag = 2 * parts * chip_rows
    tags = blocks[:, tag, :8].astype(F32)
    cross = jnp.sum(
        (tags[:, 2:4] + (tags[:, 4:6] + tags[:, 6:8] / PIECE) / PIECE)
        / HEAD
        * jnp.exp2(tags[:, 1:2]),
        axis=0,
    )
    summed = jnp.sum(blocks[:, :tag].astype(F32) * jnp.exp2(tags[:, 0])[:, None, None], axis=0)

    halves = summed.reshape(2 * parts, 2, rows, LANES).transpose(1, 0, 2, 3)
    halves = halves.reshape(2, 1, 2 * parts * rows, LANES)
    halves = jnp.broadcast_to(halves, (2, blks) + halves.shape[2:])
    sums = jnp.pad(jnp.concatenate([cross, norm[:, 0]]), (0, LANES - 4))
    sums = jnp.broadcast_to(sums[None, None, None], (2, blks, 1, LANES))
    sent = jnp.concatenate([halves, sums], axis=2).reshape(2 * blks, -1, LANES)
    came = lax.all_to_all(sent, ("core", "blk"), 0, 0, tiled=True)
    sums = jnp.sum(came[:, -1, :4], axis=0)
    energy = lax.dynamic_index_in_dim(words[:, 1, 0], site_owner[0], 0, keepdims=False)
    cross_sum, norm_sum = sums[:2], sums[2:]
    rayleigh = (cross_sum + energy * norm_sum) / (norm_sum + 1e-06)
    ours = lax.dynamic_index_in_dim(came.reshape(2, blks, -1, LANES), blk, 1, keepdims=False)
    ours = ours[:, :-1].reshape(2, 2, parts, rows, LANES).transpose(3, 1, 0, 2, 4)
    ours = ours.reshape(rows, 2, 2, size)

    first = (chip * 2 + core) * rows
    own_sizes = lax.dynamic_slice_in_dim(sector_sizes, 2 * blk, 2, 0)[:, None]
    row_ids = (first + jnp.arange(rows, dtype=jnp.int32))[:, None, None, None]
    col_ids = jnp.arange(size, dtype=jnp.int32)
    live = (row_ids < own_sizes) & (col_ids < own_sizes)
    psi_rows = lax.dynamic_slice_in_dim(wavefunction, first, rows, 2)
    psi_rows = psi_rows.transpose(2, 0, 1, 3).astype(F32)
    value = ours + (energy - rayleigh)[None, :, None, None] * psi_rows
    return jnp.where(live, value, 0.0), rayleigh


def solution(mesh):
    ops, blks = mesh.devices.shape
    split = Mesh(mesh.devices.reshape(ops // 2, 2, blks), OP + ("blk",))
    return jax.shard_map(
        on_device,
        mesh=split,
        in_specs=(
            P(None, "blk", None, None),
            P(OP, "blk", None, None),
            P(OP, "blk", None, None),
            P(OP),
            P(),
            P(OP, None),
            P(OP),
            P(),
        ),
        out_specs=(P(OP, None, "blk", None), P()),
        check_vma=False,
    )
```

time: 113 us -> 107 us (0.947)
  local copies, waits for them, and re-layouts: 19.1 us -> 7.29 us
  Pallas kernels: 16.5 us -> 20.7 us
  other arithmetic: 4.45 us -> 7.2 us
  starting transfers between devices: 48.1 us -> 46 us
    unnamed x20 -> x14, local copies, waits for them, and re-layouts: 14.9 us -> 2.29 us
    pallas_call x3 -> x2, Pallas kernels: 16.5 us -> 20.7 us  [the longest x1 11.8 us: sigma_blocks(): pl.pallas_call(sigma_kernel, in_specs=[SMEM] * 2 + [VMEM] + [HBM] * 4, ou...]
    ppermute x1 -> x0, starting transfers between devices: 2.44 us -> none  [on_device(): shifts_got = lax.ppermute(shifts, 'core', swap)]
    convert_element_type x1, other arithmetic: 0.93 us -> 2.25 us  [on_device(): blocks = lax.all_to_all(packed.astype(F16), 'chip', 0, 0, tiled=True)]
  transfers between devices with their start and end apart: 7 -> 6, of which waited for: 2 -> 3; matrix products, arithmetic and copies ran while one was open for 4% -> 6% of each run, Pallas kernels for 12% -> 8%
where the time goes in v3:
time: 107 us; the launch traced here: 106 us
  starting transfers between devices  46 us (43%)
  waiting for transfers between devices  22.4 us (21%)
  Pallas kernels  20.7 us (19%)
  local copies, waits for them, and re-layouts  7.29 us (7%)
  other arithmetic  7.2 us (7%)
  between operations  2.18 us (2%)
    all_to_all x1, waiting for transfers between devices, on_device(): blocks = lax.all_to_all(packed.astype(F16), 'chip', 0, 0, tiled=True)  18.4 us
    all_to_all x1, starting transfers between devices, on_device(): words = lax.all_to_all(words, OP, 0, 0, tiled=True)  14.2 us
    all_to_all x1, starting transfers between devices, on_device(): blocks = lax.all_to_all(packed.astype(F16), 'chip', 0, 0, tiled=True)  12.5 us
    pallas_call x1, Pallas kernels, sigma_blocks(): pl.pallas_call(sigma_kernel, in_specs=[SMEM] * 2 + [VMEM] + [HBM] * 4, ou...  11.8 us
    pallas_call x1, Pallas kernels, own_terms(): pl.pallas_call(functools.partial(own_kernel, sectors), in_specs=[SMEM] +...  8.92 us
    ppermute x1, starting transfers between devices, on_device(): left_got = lax.ppermute(left_ops, 'core', swap)  8.92 us
    all_to_all x1, starting transfers between devices, on_device(): came = lax.all_to_all(sent, ('core', 'blk'), 0, 0, tiled=True)  7.18 us
    all_to_all x1, waiting for transfers between devices, on_device(): came = lax.all_to_all(sent, ('core', 'blk'), 0, 0, tiled=True)  3.59 us
  transfers between devices with their start and end apart: 6, of which 3 were waited for; matrix products, arithmetic and copies ran while one was open for 6% of the time, Pallas kernels for 8%

profile of v3, /device:TPU:1, one launch (start us, length us, event | category | flops | bytes accessed | tf_op | source)
XLA Modules:
  0.0 105.7 jit_solution(8803268213357135317)
XLA Ops:
  0.6 0.0 copy-start.4
  0.6 0.0 copy-start.5
  0.7 8.9 %collective-permute-start.1 = (bf16[4,2,384,384]{3,2,1,0:T(8,128)(2,1)}, bf16[4,2,384,384]{3,2,1,0:T(8,128)(2,1)S(1)}, u32[]{:S(2)}, u32[]{:S(2)}) collective-permute-start(bf16[4,2,384,384]{3,2,1,0:T(8,128)(2,1)} %left.1), channel_id=1, source_target_pairs={{0,4},{4,0},{1,5},{5,1},{2,6},{6,2},{3,7},{7,3},{8,12},{12,8},{9,1... | collective-permute-start | bytes 7077896 | tf_op jit(solution)/shard_map/ppermute | solution.py:280
  9.6 1.9 %collective-permute-start.2 = (bf16[4,2,384,384]{3,2,1,0:T(8,128)(2,1)}, bf16[4,2,384,384]{3,2,1,0:T(8,128)(2,1)}, u32[]{:S(2)}, u32[]{:S(2)}) collective-permute-start(bf16[4,2,384,384]{3,2,1,0:T(8,128)(2,1)} %right.1), channel_id=1, source_target_pairs={{0,4},{4,0},{1,5},{5,1},{2,6},{6,2},{3,7},{7,3},{8,12},{12,8},{9,1... | collective-permute-start | bytes 7077896 | tf_op jit(solution)/shard_map/ppermute | solution.py:281
  11.5 1.9 %dynamic-slice_bitcast_fusion = bf16[2,384,384]{2,1,0:T(8,128)(2,1)} fusion(bf16[2,2,384,384]{3,2,1,0:T(8,128)(2,1)} %psi.1, s32[]{:T(128)S(6)} %select_n.23), kind=kLoop, calls=%fused_computation.1 | loop fusion | bytes 1179652 | tf_op jit(solution)/shard_map/jit(dynamic_index_in_dim)/squeeze | solution.py:270
  13.5 1.3 %collective-permute-start = (bf16[2,384,384]{2,1,0:T(8,128)(2,1)}, bf16[2,384,384]{2,1,0:T(8,128)(2,1)S(1)}, u32[]{:S(2)}, u32[]{:S(2)}) collective-permute-start(bf16[2,384,384]{2,1,0:T(8,128)(2,1)} %dynamic-slice_bitcast_fusion), channel_id=1, source_target_pairs={{0,1},{1,2},{2,3},{5,4},{6,5},{7,6},{8,9},{9,10},{10,11},{13,12},{... | collective-permute-start | bytes 1769480 | tf_op jit(solution)/shard_map/ppermute | solution.py:271
  14.7 0.7 convert_element_type.23
  16.1 0.1 fusion.11
  16.2 0.7 broadcast_in_dim.40
  16.9 0.8 pad_maximum_fusion
  17.6 14.2 %all-to-all-start = ((f32[128,2,128]{2,1,0:T(2,128)}), f32[128,2,128]{2,1,0:T(2,128)S(1)}, u32[]{:S(2)}, u32[]{:S(2)}) async-start(f32[128,2,128]{2,1,0:T(2,128)} %pad_maximum_fusion), calls=%async_computation | async-start | bytes 262144 | tf_op jit(solution)/shard_map/all_to_all | solution.py:279
  32.5 0.0 copy-done.4
  32.5 0.0 copy-done.5
  32.5 0.6 concatenate.12.table
  33.1 0.0 collective-permute-done.halo
  33.1 0.0 copy-start.3
  33.1 0.0 collective-permute-done.1.left_got.left
  33.1 0.0 copy-start
  33.2 0.0 collective-permute-done.2.right_got.right
  33.2 0.8 copy-done.3
  34.0 0.8 copy-done
  34.8 8.9 %own_terms.1 = (f32[4,2,384,384]{3,2,1,0:T(8,128)}, bf16[3,384,768]{2,1,0:T(8,128)(2,1)}) custom-call(s32[15]{0:T(128)} %concatenate.12.table, bf16[2,2,384,384]{3,2,1,0:T(8,128)(2,1)} %psi.1, bf16[2,384,384]{2,1,0:T(8,128)(2,1)} %copy-done.3, bf16[4,2,384,384]{3,2,1,0:T(8,128)(2,1)} %left.1, bf16[4,2,384,384]{3,2,1,0:T(8,128)(2,1)} %right.1, ...), custom_call_target="tpu_custom_call" | custom-call | flops 1811939328 | bytes 11796480 | tf_op jit(solution)/shard_map/own_terms/pallas_call | solution.py:100
  43.7 0.4 all-to-all-done.words
  44.1 0.0 copy-start.1
  44.1 0.7 copy-done.1
  44.8 11.8 %sigma_blocks.1 = (f32[64,40,128]{2,1,0:T(8,128)}, f32[2,128]{1,0:T(2,128)}) custom-call(s32[15]{0:T(128)} %concatenate.12.table, s32[1]{0:T(128)} %copy.26.owner, f32[128,2,128]{2,1,0:T(2,128)} %copy-done.1, f32[4,2,384,384]{3,2,1,0:T(8,128)} %get-tuple-element.6.own, bf16[3,384,768]{2,1,0:T(8,128)(2,1)} %get-tuple-element.7.sources, ...), custom_call_target="tpu_custom_call" | custom-call | flops 1811939328 | bytes 11796480 | tf_op jit(solution)/shard_map/sigma_blocks/pallas_call | solution.py:228
  56.5 0.0 copy-start.6
  56.5 2.2 %convert_element_type.24 = f16[64,40,128]{2,1,0:T(8,128)(2,1)} convert(f32[64,40,128]{2,1,0:T(8,128)} %get-tuple-element.8) | non-fusion elementwise | flops 327680 | bytes 1966080 | tf_op jit(solution)/shard_map/convert_element_type | solution.py:296
  58.8 0.0 copy-start.2
  58.8 12.5 %all-to-all-start.1 = ((f16[64,40,128]{2,1,0:T(8,128)(2,1)}), f16[64,40,128]{2,1,0:T(8,128)(2,1)S(1)}, u32[]{:S(2)}, u32[]{:S(2)}) async-start(f16[64,40,128]{2,1,0:T(8,128)(2,1)} %convert_element_type.24), calls=%async_computation.1 | async-start | bytes 1310720 | tf_op jit(solution)/shard_map/all_to_all | solution.py:296
  71.3 0.1 dynamic_slice.18
  71.4 0.1 broadcast_compare_fusion
  71.5 0.1 iota_compare_fusion
  71.5 0.1 broadcast_and_fusion
  71.6 0.0 copy-done.6
  71.6 0.1 slice_reduce_fusion.1
  71.7 18.4 %all-to-all-done.1 = f16[64,40,128]{2,1,0:T(8,128)(2,1)S(1)} async-done(((f16[64,40,128]{2,1,0:T(8,128)(2,1)}), f16[64,40,128]{2,1,0:T(8,128)(2,1)S(1)}, u32[]{:S(2)}, u32[]{:S(2)}) %all-to-all-start.1) | async-done | bytes 655392 | tf_op jit(solution)/shard_map/all_to_all | solution.py:296
  90.2 0.2 fusion.9
  90.4 0.2 multiply_reduce_fusion
  90.6 0.1 fusion.7
  90.8 0.1 fusion.12
  90.9 0.6 pad_maximum_fusion.1
  91.5 7.2 %all-to-all-start.2 = ((f32[8,19,128]{2,1,0:T(8,128)}), f32[8,19,128]{2,1,0:T(8,128)S(1)}, u32[]{:S(2)}, u32[]{:S(2)}) async-start(f32[8,19,128]{2,1,0:T(8,128)} %bitcast.9), calls=%async_computation.2 | async-start | bytes 196608 | tf_op jit(solution)/shard_map/all_to_all | solution.py:313
  98.7 0.8 constant_dynamic-slice_fusion
  99.5 0.0 copy-done.2
  99.5 0.1 slice.60
  99.6 0.5 constant_dynamic-slice_fusion.1
  100.1 3.6 %all-to-all-done.2 = f32[8,19,128]{2,1,0:T(8,128)S(1)} async-done(((f32[8,19,128]{2,1,0:T(8,128)}), f32[8,19,128]{2,1,0:T(8,128)S(1)}, u32[]{:S(2)}, u32[]{:S(2)}) %all-to-all-start.2) | async-done | bytes 77856 | tf_op jit(solution)/shard_map/all_to_all | solution.py:313
  103.8 1.2 %broadcast_subtract_fusion = (f32[2]{0:T(128)S(1)}, f32[2]{0:T(128)}) fusion(f32[]{:T(128)} %bitcast.15, f32[4]{0:T(128)S(1)} %slice_reduce_fusion), kind=kLoop, calls=%fused_computation.36 | loop fusion | flops 10 | bytes 36 | tf_op jit(solution)/shard_map/sub | solution.py:329
  105.1 0.7 fusion.10
  (14 shorter events, 0.2 us)
Async XLA Ops:
  0.6 31.9 %copy-start.4 = (s32[4]{0:T(128)S(1)}, s32[4]{0:T(128)}, u32[]{:S(2)}) copy-start(s32[4]{0:T(128)} %param.11) | copy-start | bytes 52
  0.6 31.9 %copy-start.5 = (s32[8]{0:T(128)S(1)}, s32[8]{0:T(128)}, u32[]{:S(2)}) copy-start(s32[8]{0:T(128)} %param.12) | copy-start | bytes 100
  0.7 32.5 %collective-permute-start.1 = (bf16[4,2,384,384]{3,2,1,0:T(8,128)(2,1)}, bf16[4,2,384,384]{3,2,1,0:T(8,128)(2,1)S(1)}, u32[]{:S(2)}, u32[]{:S(2)}) collective-permute-start(bf16[4,2,384,384]{3,2,1,0:T(8,128)(2,1)} %left.1), channel_id=1, source_target_pairs={{0,4},{4,0},{1,5},{5,1},{2,6},{6,2},{3,7},{7,3},{8,12},{12,8},{9,1... | collective-permute-start | bytes 7077896 | tf_op jit(solution)/shard_map/ppermute | solution.py:280
  9.6 23.6 %collective-permute-start.2 = (bf16[4,2,384,384]{3,2,1,0:T(8,128)(2,1)}, bf16[4,2,384,384]{3,2,1,0:T(8,128)(2,1)}, u32[]{:S(2)}, u32[]{:S(2)}) collective-permute-start(bf16[4,2,384,384]{3,2,1,0:T(8,128)(2,1)} %right.1), channel_id=1, source_target_pairs={{0,4},{4,0},{1,5},{5,1},{2,6},{6,2},{3,7},{7,3},{8,12},{12,8},{9,1... | collective-permute-start | bytes 7077896 | tf_op jit(solution)/shard_map/ppermute | solution.py:281
  13.5 19.7 %collective-permute-start = (bf16[2,384,384]{2,1,0:T(8,128)(2,1)}, bf16[2,384,384]{2,1,0:T(8,128)(2,1)S(1)}, u32[]{:S(2)}, u32[]{:S(2)}) collective-permute-start(bf16[2,384,384]{2,1,0:T(8,128)(2,1)} %dynamic-slice_bitcast_fusion), channel_id=1, source_target_pairs={{0,1},{1,2},{2,3},{5,4},{6,5},{7,6},{8,9},{9,10},{10,11},{13,12},{... | collective-permute-start | bytes 1769480 | tf_op jit(solution)/shard_map/ppermute | solution.py:271
  17.6 26.5 %all-to-all-start = ((f32[128,2,128]{2,1,0:T(2,128)}), f32[128,2,128]{2,1,0:T(2,128)S(1)}, u32[]{:S(2)}, u32[]{:S(2)}) async-start(f32[128,2,128]{2,1,0:T(2,128)} %pad_maximum_fusion), calls=%async_computation | async-start | bytes 262144 | tf_op jit(solution)/shard_map/all_to_all | solution.py:279
  33.1 0.8 copy-start.3
  33.1 1.6 %copy-start = (bf16[4,2,384,384]{3,2,1,0:T(8,128)(2,1)}, bf16[4,2,384,384]{3,2,1,0:T(8,128)(2,1)S(1)}, u32[]{:S(2)}) copy-start(bf16[4,2,384,384]{3,2,1,0:T(8,128)(2,1)S(1)} %collective-permute-done.1.left_got.left) | copy-start | bytes 7077892
  44.1 0.7 copy-start.1
  56.5 15.1 %copy-start.6 = (f32[2,128]{1,0:T(2,128)S(1)}, f32[2,128]{1,0:T(2,128)}, u32[]{:S(2)}) copy-start(f32[2,128]{1,0:T(2,128)} %get-tuple-element.9) | copy-start | bytes 3076
  58.8 40.7 %copy-start.2 = (f32[128,2,128]{2,1,0:T(2,128)S(1)}, f32[128,2,128]{2,1,0:T(2,128)}, u32[]{:S(2)}) copy-start(f32[128,2,128]{2,1,0:T(2,128)} %copy-done.1) | copy-start | bytes 393220
  58.8 31.4 %all-to-all-start.1 = ((f16[64,40,128]{2,1,0:T(8,128)(2,1)}), f16[64,40,128]{2,1,0:T(8,128)(2,1)S(1)}, u32[]{:S(2)}, u32[]{:S(2)}) async-start(f16[64,40,128]{2,1,0:T(8,128)(2,1)} %convert_element_type.24), calls=%async_computation.1 | async-start | bytes 1310720 | tf_op jit(solution)/shard_map/all_to_all | solution.py:296
  91.5 12.2 %all-to-all-start.2 = ((f32[8,19,128]{2,1,0:T(8,128)}), f32[8,19,128]{2,1,0:T(8,128)S(1)}, u32[]{:S(2)}, u32[]{:S(2)}) async-start(f32[8,19,128]{2,1,0:T(8,128)} %bitcast.9), calls=%async_computation.2 | async-start | bytes 196608 | tf_op jit(solution)/shard_map/all_to_all | solution.py:313

commit v4 on v3

--- a/solution.py
+++ b/solution.py
@@ -16,6 +16,53 @@
 VMEM = pl.BlockSpec(memory_space=pltpu.VMEM)
 HBM = pl.BlockSpec(memory_space=pltpu.HBM)
 CORE, BLK, CHIP, SHIFTS = 0, 1, 2, 3
+
+
+def prep_kernel(coef, energy, shifts, sizes, psi, words, edge, table, sems):
+    core = lax.axis_index("core")
+    copies = [
+        pltpu.make_async_copy(psi.at[v, 1 - core], edge.at[v], sems.at[v]) for v in range(2)
+    ]
+    for copy in copies:
+        copy.start()
+    table[CORE] = core
+    table[BLK] = lax.axis_index("blk")
+    table[CHIP] = lax.axis_index("chip")
+    pairs, sectors = shifts.shape[0], sizes.shape[0]
+    for k in range(pairs):
+        table[SHIFTS + k] = shifts[k]
+    for b in range(sectors):
+        table[SHIFTS + pairs + b] = sizes[b]
+    spot = lax.broadcasted_iota(jnp.int32, (2, LANES), 1)
+    row = lax.broadcasted_iota(jnp.int32, (2, LANES), 0)
+    facts = jnp.where(spot == 0, energy[0], 0.0)
+    for k in range(pairs):
+        facts = jnp.where(spot == 1 + k, shifts[k].astype(F32), facts)
+    lines = coef.shape[1] // LANES
+    each = words.shape[0] // lines
+    for i in range(lines):
+        line = jnp.broadcast_to(coef[0:1, i * LANES : (i + 1) * LANES], (2, LANES))
+        block = jnp.where(row == 0, line, facts)
+        words[i * each : (i + 1) * each] = jnp.broadcast_to(block[None], (each, 2, LANES))
+    for copy in copies:
+        copy.wait()
+
+
+def prepared(ops, coef, energy, shifts, sizes, psi):
+    size = psi.shape[2]
+    return pl.pallas_call(
+        prep_kernel,
+        in_specs=[VMEM] + [SMEM] * 3 + [HBM],
+        out_specs=[VMEM, HBM, SMEM],
+        out_shape=[
+            jax.ShapeDtypeStruct((ops, 2, LANES), F32),
+            jax.ShapeDtypeStruct((2, size, size), BF16),
+            jax.ShapeDtypeStruct((SHIFTS + shifts.shape[0] + sizes.shape[0],), jnp.int32),
+        ],
+        scratch_shapes=[pltpu.SemaphoreType.DMA((2,))],
+        compiler_params=pltpu.CompilerParams(vmem_limit_bytes=60_000_000),
+        name="prepared",
+    )(coef, energy, shifts, sizes, psi)
 
 
 def loads(core, left, right, lefts, rights, sems):
@@ -151,6 +198,7 @@
     for k in range(pairs):
         copies[k][0].start()
         copies[k][1].start()
+    for k in range(pairs):
         own_copies[k].start()
 
     chips = packed.shape[0]
@@ -171,10 +219,11 @@
     source_copy.wait()
     for k in range(pairs):
         terms = product(core, shifts[k], src, lefts.at[k], rights.at[k], copies[k])
+        for v in range(2):
+            total = got_weight[0:1, k : k + 1] * terms[v]
+            acc[v] = total if k == 0 else acc[v] + total
+    for k in range(pairs):
         own_copies[k].wait()
-        for v in range(2):
-            total = got_weight[0:1, k : k + 1] * terms[v] + own_weight[0:1, k : k + 1] * owns[k, v]
-            acc[v] = total if k == 0 else acc[v] + total
 
     tile = size // TILES
     here = chips // TILES
@@ -186,6 +235,9 @@
         top = None
         for v in range(2):
             total = acc[v, rows, :]
+            for k in range(pairs):
+                total += own_weight[0:1, k : k + 1] * owns[k, v, rows, :]
+            acc[v, rows, :] = total
             psi = src[core, rows, v * size : (v + 1) * size].astype(F32)
             for i, part in ((v, folded(psi * total)), (2 + v, folded(psi * psi))):
                 sums[i] = part if sums[i] is None else sums[i] + part
@@ -243,7 +295,7 @@
             pltpu.SemaphoreType.DMA((pairs,)),
             pltpu.SemaphoreType.DMA((1,)),
         ],
-        compiler_params=pltpu.CompilerParams(vmem_limit_bytes=61_880_000),
+        compiler_params=pltpu.CompilerParams(vmem_limit_bytes=55_000_000),
         cost_estimate=estimate(pairs, size),
         name="sigma_blocks",
     )(table, owner, words, own, sources, left, right)
@@ -259,23 +311,15 @@
     chip_rows = size // chips
     rows = chip_rows // 2
     parts = size // LANES
-    table = jnp.concatenate(
-        [jnp.stack([core, blk, chip]).astype(jnp.int32), shifts, sector_sizes]
+    words, edge, table = prepared(
+        2 * chips, site_coef, site_energy, shifts, sector_sizes, wavefunction
     )
 
     swap = [(0, 1), (1, 0)]
     halo_path = [(x, x + 1) for x in range(blks - 1)] + [
         (blks + x + 1, blks + x) for x in range(blks - 1)
     ]
-    edge = lax.dynamic_index_in_dim(wavefunction, 1 - core, 1, keepdims=False)
     halo = lax.ppermute(edge, ("core", "blk"), halo_path)
-    lines = site_coef.reshape(-1, 1, LANES)
-    lines = jnp.broadcast_to(lines, (lines.shape[0], 2 * chips // lines.shape[0], LANES))
-    facts = jnp.concatenate([site_energy, shifts.astype(F32)])
-    facts = jnp.pad(facts, (0, LANES - 1 - pairs))
-    words = jnp.stack(
-        [lines.reshape(2 * chips, LANES), jnp.broadcast_to(facts, (2 * chips, LANES))], axis=1
-    )
     words = lax.all_to_all(words, OP, 0, 0, tiled=True)
     left_got = lax.ppermute(left_ops, "core", swap)
     right_got = lax.ppermute(right_ops, "core", swap)

time: 107 us -> 118 us (1.10)
  Pallas kernels: 20.7 us -> 39.1 us
  local copies, waits for them, and re-layouts: 7.29 us -> 3.32 us
  other arithmetic: 7.2 us -> 4.38 us
    pallas_call x0 -> x1, Pallas kernels: none -> 20.5 us  [prepared(): pl.pallas_call(prep_kernel, in_specs=[VMEM] + [SMEM] * 3 + [HBM], out_spe...]
    pallas_call x1, Pallas kernels: 11.8 us -> 9.62 us  [sigma_blocks(): pl.pallas_call(sigma_kernel, in_specs=[SMEM] * 2 + [VMEM] + [HBM] * 4, ou...]
    squeeze x1 -> x0, local copies, waits for them, and re-layouts: 1.94 us -> none  [on_device(): edge = lax.dynamic_index_in_dim(wavefunction, 1 - core, 1, keepdims=False)]
    convert_element_type x1, other arithmetic: 2.25 us -> 0.94 us  [on_device(): blocks = lax.all_to_all(packed.astype(F16), 'chip', 0, 0, tiled=True)]
  transfers between devices with their start and end apart: 6 -> 6, of which waited for: 3 -> 3; matrix products, arithmetic and copies ran while one was open for 6% -> 2% of each run, Pallas kernels for 8% -> 25%
where the time goes in v4:
time: 118 us; the launch traced here: 117 us
  starting transfers between devices  45.4 us (38%)
  Pallas kernels  39.1 us (33%)
  waiting for transfers between devices  22.7 us (19%)
  other arithmetic  4.38 us (4%)
  local copies, waits for them, and re-layouts  3.32 us (3%)
  between operations  2.14 us (2%)
    pallas_call x1, Pallas kernels, prepared(): pl.pallas_call(prep_kernel, in_specs=[VMEM] + [SMEM] * 3 + [HBM], out_spe...  20.5 us
    all_to_all x1, waiting for transfers between devices, on_device(): blocks = lax.all_to_all(packed.astype(F16), 'chip', 0, 0, tiled=True)  18.4 us
    all_to_all x1, starting transfers between devices, on_device(): words = lax.all_to_all(words, OP, 0, 0, tiled=True)  14.2 us
    all_to_all x1, starting transfers between devices, on_device(): blocks = lax.all_to_all(packed.astype(F16), 'chip', 0, 0, tiled=True)  12.1 us
    pallas_call x1, Pallas kernels, sigma_blocks(): pl.pallas_call(sigma_kernel, in_specs=[SMEM] * 2 + [VMEM] + [HBM] * 4, ou...  9.62 us
    pallas_call x1, Pallas kernels, own_terms(): pl.pallas_call(functools.partial(own_kernel, sectors), in_specs=[SMEM] +...  9.06 us
    ppermute x1, starting transfers between devices, on_device(): left_got = lax.ppermute(left_ops, 'core', swap)  8.79 us
    all_to_all x1, starting transfers between devices, on_device(): came = lax.all_to_all(sent, ('core', 'blk'), 0, 0, tiled=True)  7.18 us
  transfers between devices with their start and end apart: 6, of which 3 were waited for; matrix products, arithmetic and copies ran while one was open for 2% of the time, Pallas kernels for 25%

profile of v4, /device:TPU:1, one launch (start us, length us, event | category | flops | bytes accessed | tf_op | source)
XLA Modules:
  0.0 117.1 jit_solution(7906168449909468630)
XLA Ops:
  0.6 8.8 %collective-permute-start.1 = (bf16[4,2,384,384]{3,2,1,0:T(8,128)(2,1)}, bf16[4,2,384,384]{3,2,1,0:T(8,128)(2,1)S(1)}, u32[]{:S(2)}, u32[]{:S(2)}) collective-permute-start(bf16[4,2,384,384]{3,2,1,0:T(8,128)(2,1)} %left.1), channel_id=1, source_target_pairs={{0,4},{4,0},{1,5},{5,1},{2,6},{6,2},{3,7},{7,3},{8,12},{12,8},{9,1... | collective-permute-start | bytes 7077896 | tf_op jit(solution)/shard_map/ppermute | solution.py:324
  9.4 1.9 %collective-permute-start.2 = (bf16[4,2,384,384]{3,2,1,0:T(8,128)(2,1)}, bf16[4,2,384,384]{3,2,1,0:T(8,128)(2,1)}, u32[]{:S(2)}, u32[]{:S(2)}) collective-permute-start(bf16[4,2,384,384]{3,2,1,0:T(8,128)(2,1)} %right.1), channel_id=1, source_target_pairs={{0,4},{4,0},{1,5},{5,1},{2,6},{6,2},{3,7},{7,3},{8,12},{12,8},{9,1... | collective-permute-start | bytes 7077896 | tf_op jit(solution)/shard_map/ppermute | solution.py:325
  12.0 20.5 %prepared.1 = (f32[128,2,128]{2,1,0:T(2,128)}, bf16[2,384,384]{2,1,0:T(8,128)(2,1)}, s32[15]{0:T(128)}) custom-call(f32[1,512]{1,0:T(1,128)} %coef.1, f32[1]{0:T(128)S(6)} %copy.25.energy, s32[4]{0:T(128)} %shifts.1, s32[8]{0:T(128)} %sizes.1, bf16[2,2,384,384]{3,2,1,0:T(8,128)(2,1)} %psi.3), custom_call_target="tpu_custom_call" | custom-call | tf_op jit(solution)/shard_map/prepared/pallas_call | solution.py:53
  32.5 1.3 %collective-permute-start = (bf16[2,384,384]{2,1,0:T(8,128)(2,1)}, bf16[2,384,384]{2,1,0:T(8,128)(2,1)S(1)}, u32[]{:S(2)}, u32[]{:S(2)}) collective-permute-start(bf16[2,384,384]{2,1,0:T(8,128)(2,1)} %get-tuple-element.11), channel_id=1, source_target_pairs={{0,1},{1,2},{2,3},{5,4},{6,5},{7,6},{8,9},{9,10},{10,11},{13,12},{... | collective-permute-start | bytes 1769480 | tf_op jit(solution)/shard_map/ppermute | solution.py:322
  33.8 14.2 %all-to-all-start = ((f32[128,2,128]{2,1,0:T(2,128)}), f32[128,2,128]{2,1,0:T(2,128)S(1)}, u32[]{:S(2)}, u32[]{:S(2)}) async-start(f32[128,2,128]{2,1,0:T(2,128)} %get-tuple-element.10), calls=%async_computation | async-start | bytes 262144 | tf_op jit(solution)/shard_map/all_to_all | solution.py:323
  48.6 0.0 collective-permute-done.halo
  48.6 0.0 copy-start.2
  48.6 0.0 collective-permute-done.1.left_got.left
  48.7 0.0 copy-start.1
  48.7 0.0 collective-permute-done.2.right_got.right
  48.7 0.8 copy-done.2
  49.4 0.8 copy-done.1
  50.3 0.0 copy-start
  50.3 9.1 %own_terms.1 = (f32[4,2,384,384]{3,2,1,0:T(8,128)}, bf16[3,384,768]{2,1,0:T(8,128)(2,1)}) custom-call(s32[15]{0:T(128)} %get-tuple-element.9.table, bf16[2,2,384,384]{3,2,1,0:T(8,128)(2,1)} %psi.3, bf16[2,384,384]{2,1,0:T(8,128)(2,1)} %copy-done.2, bf16[4,2,384,384]{3,2,1,0:T(8,128)(2,1)} %left.1, bf16[4,2,384,384]{3,2,1,0:T(8,128)(2,1)} %right.1, ...), custom_call_target="tpu_custom_call" | custom-call | flops 1811939328 | bytes 11796480 | tf_op jit(solution)/shard_map/own_terms/pallas_call | solution.py:147
  59.3 0.7 all-to-all-done.words
  60.0 0.0 copy-done
  60.0 9.6 %sigma_blocks.1 = (f32[64,40,128]{2,1,0:T(8,128)S(1)}, f32[2,128]{1,0:T(2,128)S(1)}) custom-call(s32[15]{0:T(128)S(1)} %copy-done, s32[1]{0:T(128)} %copy.26.owner, f32[128,2,128]{2,1,0:T(2,128)S(1)} %all-to-all-done.words, f32[4,2,384,384]{3,2,1,0:T(8,128)} %get-tuple-element.12.own, bf16[3,384,768]{2,1,0:T(8,128)(2,1)} %get-tuple-element.13.sources, ...), custom_call_target="tpu_custom_call" | custom-call | flops 1811939328 | bytes 11796480 | tf_op jit(solution)/shard_map/sigma_blocks/pallas_call | solution.py:280
  69.7 0.0 copy-start.3
  69.7 0.9 convert_element_type.18
  70.6 12.1 %all-to-all-start.1 = ((f16[64,40,128]{2,1,0:T(8,128)(2,1)}), f16[64,40,128]{2,1,0:T(8,128)(2,1)S(1)}, u32[]{:S(2)}, u32[]{:S(2)}) async-start(f16[64,40,128]{2,1,0:T(8,128)(2,1)} %convert_element_type.18), calls=%async_computation.1 | async-start | bytes 1310720 | tf_op jit(solution)/shard_map/all_to_all | solution.py:340
  82.7 0.0 copy-done.3
  82.7 0.1 dynamic_slice.14
  82.8 0.1 broadcast_compare_fusion
  82.9 0.1 iota_compare_fusion
  82.9 0.1 broadcast_and_fusion
  83.0 0.1 slice_reduce_fusion.1
  83.1 18.4 %all-to-all-done.1 = f16[64,40,128]{2,1,0:T(8,128)(2,1)S(1)} async-done(((f16[64,40,128]{2,1,0:T(8,128)(2,1)}), f16[64,40,128]{2,1,0:T(8,128)(2,1)S(1)}, u32[]{:S(2)}, u32[]{:S(2)}) %all-to-all-start.1) | async-done | bytes 655392 | tf_op jit(solution)/shard_map/all_to_all | solution.py:340
  101.6 0.2 fusion.9
  101.8 0.1 fusion.7
  101.9 0.2 multiply_reduce_fusion
  102.2 0.1 fusion.11
  102.2 0.7 pad_maximum_fusion
  102.9 7.2 %all-to-all-start.2 = ((f32[8,19,128]{2,1,0:T(8,128)}), f32[8,19,128]{2,1,0:T(8,128)S(1)}, u32[]{:S(2)}, u32[]{:S(2)}) async-start(f32[8,19,128]{2,1,0:T(8,128)} %bitcast.3), calls=%async_computation.2 | async-start | bytes 196608 | tf_op jit(solution)/shard_map/all_to_all | solution.py:357
  110.1 0.8 constant_dynamic-slice_fusion
  110.9 0.1 slice.60
  111.0 0.5 constant_dynamic-slice_fusion.1
  111.5 3.6 %all-to-all-done.2 = f32[8,19,128]{2,1,0:T(8,128)S(1)} async-done(((f32[8,19,128]{2,1,0:T(8,128)}), f32[8,19,128]{2,1,0:T(8,128)S(1)}, u32[]{:S(2)}, u32[]{:S(2)}) %all-to-all-start.2) | async-done | bytes 77856 | tf_op jit(solution)/shard_map/all_to_all | solution.py:357
  115.2 1.2 %broadcast_subtract_fusion = (f32[2]{0:T(128)S(1)}, f32[2]{0:T(128)}) fusion(f32[]{:T(128)} %bitcast.9, f32[4]{0:T(128)S(1)} %slice_reduce_fusion), kind=kLoop, calls=%fused_computation.31 | loop fusion | flops 10 | bytes 36 | tf_op jit(solution)/shard_map/sub | solution.py:373
  116.5 0.7 fusion.10
  (13 shorter events, 0.2 us)
Async XLA Ops:
  0.6 48.0 %collective-permute-start.1 = (bf16[4,2,384,384]{3,2,1,0:T(8,128)(2,1)}, bf16[4,2,384,384]{3,2,1,0:T(8,128)(2,1)S(1)}, u32[]{:S(2)}, u32[]{:S(2)}) collective-permute-start(bf16[4,2,384,384]{3,2,1,0:T(8,128)(2,1)} %left.1), channel_id=1, source_target_pairs={{0,4},{4,0},{1,5},{5,1},{2,6},{6,2},{3,7},{7,3},{8,12},{12,8},{9,1... | collective-permute-start | bytes 7077896 | tf_op jit(solution)/shard_map/ppermute | solution.py:324
  9.4 39.2 %collective-permute-start.2 = (bf16[4,2,384,384]{3,2,1,0:T(8,128)(2,1)}, bf16[4,2,384,384]{3,2,1,0:T(8,128)(2,1)}, u32[]{:S(2)}, u32[]{:S(2)}) collective-permute-start(bf16[4,2,384,384]{3,2,1,0:T(8,128)(2,1)} %right.1), channel_id=1, source_target_pairs={{0,4},{4,0},{1,5},{5,1},{2,6},{6,2},{3,7},{7,3},{8,12},{12,8},{9,1... | collective-permute-start | bytes 7077896 | tf_op jit(solution)/shard_map/ppermute | solution.py:325
  32.5 16.1 %collective-permute-start = (bf16[2,384,384]{2,1,0:T(8,128)(2,1)}, bf16[2,384,384]{2,1,0:T(8,128)(2,1)S(1)}, u32[]{:S(2)}, u32[]{:S(2)}) collective-permute-start(bf16[2,384,384]{2,1,0:T(8,128)(2,1)} %get-tuple-element.11), channel_id=1, source_target_pairs={{0,1},{1,2},{2,3},{5,4},{6,5},{7,6},{8,9},{9,10},{10,11},{13,12},{... | collective-permute-start | bytes 1769480 | tf_op jit(solution)/shard_map/ppermute | solution.py:322
  33.8 26.3 %all-to-all-start = ((f32[128,2,128]{2,1,0:T(2,128)}), f32[128,2,128]{2,1,0:T(2,128)S(1)}, u32[]{:S(2)}, u32[]{:S(2)}) async-start(f32[128,2,128]{2,1,0:T(2,128)} %get-tuple-element.10), calls=%async_computation | async-start | bytes 262144 | tf_op jit(solution)/shard_map/all_to_all | solution.py:323
  48.6 0.8 copy-start.2
  48.7 1.6 %copy-start.1 = (bf16[4,2,384,384]{3,2,1,0:T(8,128)(2,1)}, bf16[4,2,384,384]{3,2,1,0:T(8,128)(2,1)S(1)}, u32[]{:S(2)}) copy-start(bf16[4,2,384,384]{3,2,1,0:T(8,128)(2,1)S(1)} %collective-permute-done.1.left_got.left) | copy-start | bytes 7077892
  50.3 9.8 %copy-start = (s32[15]{0:T(128)S(1)}, s32[15]{0:T(128)}, u32[]{:S(2)}) copy-start(s32[15]{0:T(128)} %get-tuple-element.9.table) | copy-start | bytes 184
  69.7 13.0 %copy-start.3 = (s32[8]{0:T(128)S(1)}, s32[8]{0:T(128)}, u32[]{:S(2)}) copy-start(s32[8]{0:T(128)} %sizes.1) | copy-start | bytes 100
  70.6 30.9 %all-to-all-start.1 = ((f16[64,40,128]{2,1,0:T(8,128)(2,1)}), f16[64,40,128]{2,1,0:T(8,128)(2,1)S(1)}, u32[]{:S(2)}, u32[]{:S(2)}) async-start(f16[64,40,128]{2,1,0:T(8,128)(2,1)} %convert_element_type.18), calls=%async_computation.1 | async-start | bytes 1310720 | tf_op jit(solution)/shard_map/all_to_all | solution.py:340
  102.9 12.2 %all-to-all-start.2 = ((f32[8,19,128]{2,1,0:T(8,128)}), f32[8,19,128]{2,1,0:T(8,128)S(1)}, u32[]{:S(2)}, u32[]{:S(2)}) async-start(f32[8,19,128]{2,1,0:T(8,128)} %bitcast.3), calls=%async_computation.2 | async-start | bytes 196608 | tf_op jit(solution)/shard_map/all_to_all | solution.py:357

commit v5 on v4

--- a/solution.py
+++ b/solution.py
@@ -53,14 +53,14 @@
     return pl.pallas_call(
         prep_kernel,
         in_specs=[VMEM] + [SMEM] * 3 + [HBM],
-        out_specs=[VMEM, HBM, SMEM],
+        out_specs=[VMEM, VMEM, SMEM],
         out_shape=[
             jax.ShapeDtypeStruct((ops, 2, LANES), F32),
             jax.ShapeDtypeStruct((2, size, size), BF16),
             jax.ShapeDtypeStruct((SHIFTS + shifts.shape[0] + sizes.shape[0],), jnp.int32),
         ],
         scratch_shapes=[pltpu.SemaphoreType.DMA((2,))],
-        compiler_params=pltpu.CompilerParams(vmem_limit_bytes=60_000_000),
+        compiler_params=pltpu.CompilerParams(vmem_limit_bytes=60000000),
         name="prepared",
     )(coef, energy, shifts, sizes, psi)
 
@@ -94,7 +94,7 @@
 
 
 def own_kernel(
-    sectors, table, psi, halo, left, right, left_got, right_got, terms, sources,
+    sectors, table, psi, halo, left, right, terms, sources,
     psis, halos, lefts, rights, made, src, sems, out_sems, more,
 ):
     core, blk = table[CORE], table[BLK]
@@ -123,14 +123,17 @@
             block = psis[v, slot] if slot < 2 else halos[v]
             src[slot, :, v * size : (v + 1) * size] = block * live
     source_copy = pltpu.make_async_copy(src, sources, more.at[2])
-    source_copy.start()
     outs = []
     for k in range(pairs):
         terms_k = product(core, table[SHIFTS + k], src, lefts.at[k], rights.at[k], copies[k])
         for v in range(2):
             made[k, v] = terms_k[v]
-        outs.append(pltpu.make_async_copy(made.at[k], terms.at[k], out_sems.at[k]))
-        outs[k].start()
+            outs.append(
+                pltpu.make_async_copy(made.at[k, v], terms.at[k, v], out_sems.at[2 * k + v])
+            )
+            outs[-1].start()
+        if k == 0:
+            source_copy.start()
     source_copy.wait()
     for out in outs:
         out.wait()
@@ -142,11 +145,11 @@
     )
 
 
-def own_terms(sectors, table, psi, halo, left, right, left_got, right_got):
+def own_terms(sectors, table, psi, halo, left, right):
     pairs, _, size, _ = left.shape
     return pl.pallas_call(
         functools.partial(own_kernel, sectors),
-        in_specs=[SMEM] + [HBM] * 6,
+        in_specs=[SMEM] + [HBM] * 4,
         out_specs=[HBM, HBM],
         out_shape=[
             jax.ShapeDtypeStruct((pairs, 2, size, size), F32),
@@ -160,13 +163,13 @@
             pltpu.VMEM((pairs, 2, size, size), F32),
             pltpu.VMEM((3, size, 2 * size), BF16),
             pltpu.SemaphoreType.DMA((2, pairs)),
-            pltpu.SemaphoreType.DMA((pairs,)),
+            pltpu.SemaphoreType.DMA((2 * pairs,)),
             pltpu.SemaphoreType.DMA((3,)),
         ],
-        compiler_params=pltpu.CompilerParams(vmem_limit_bytes=62_850_000),
-        cost_estimate=estimate(pairs, size),
+        compiler_params=pltpu.CompilerParams(vmem_limit_bytes=56200000),
+        cost_estimate=estimate(100 * pairs, size),
         name="own_terms",
-    )(table, psi, halo, left, right, left_got, right_got)
+    )(table, psi, halo, left, right)
 
 
 def level_of(top, head):
@@ -330,8 +333,6 @@
         halo,
         left_ops,
         right_ops,
-        left_got,
-        right_got,
     )
     packed, norm = sigma_blocks(
         chips, table, site_owner, words, own, sources, left_got, right_got

time: 118 us -> 100 us (0.85)
  Pallas kernels: 39.1 us -> 21.5 us
  waiting for transfers between devices: 22.7 us -> 21.1 us
  starting transfers between devices: 45.4 us -> 46.6 us
    pallas_call x1, Pallas kernels: 20.5 us -> 2.78 us  [prepared(): pl.pallas_call(prep_kernel, in_specs=[VMEM] + [SMEM] * 3 + [HBM], out_spe...]
    all_to_all x1, starting transfers between devices: 14.2 us -> 21 us  [on_device(): words = lax.all_to_all(words, OP, 0, 0, tiled=True)]
    ppermute x1, starting transfers between devices: 8.79 us -> 2.88 us  [on_device(): left_got = lax.ppermute(left_ops, 'core', swap)]
  transfers between devices with their start and end apart: 6 -> 6, of which waited for: 3 -> 2; matrix products, arithmetic and copies ran while one was open for 2% -> 3% of each run, Pallas kernels for 25% -> 9%
where the time goes in v5:
time: 100 us; the launch traced here: 99.8 us
  starting transfers between devices  46.6 us (47%)
  Pallas kernels  21.5 us (22%)
  waiting for transfers between devices  21.1 us (21%)
  other arithmetic  4.38 us (4%)
  local copies, waits for them, and re-layouts  4.08 us (4%)
  between operations  2.15 us (2%)
    all_to_all x1, starting transfers between devices, on_device(): words = lax.all_to_all(words, OP, 0, 0, tiled=True)  21 us
    all_to_all x1, waiting for transfers between devices, on_device(): blocks = lax.all_to_all(packed.astype(F16), 'chip', 0, 0, tiled=True)  18.4 us
    all_to_all x1, starting transfers between devices, on_device(): blocks = lax.all_to_all(packed.astype(F16), 'chip', 0, 0, tiled=True)  12.3 us
    pallas_call x1, Pallas kernels, sigma_blocks(): pl.pallas_call(sigma_kernel, in_specs=[SMEM] * 2 + [VMEM] + [HBM] * 4, ou...  10 us
    pallas_call x1, Pallas kernels, own_terms(): pl.pallas_call(functools.partial(own_kernel, sectors), in_specs=[SMEM] +...  8.69 us
    all_to_all x1, starting transfers between devices, on_device(): came = lax.all_to_all(sent, ('core', 'blk'), 0, 0, tiled=True)  7.19 us
    ppermute x1, starting transfers between devices, on_device(): left_got = lax.ppermute(left_ops, 'core', swap)  2.88 us
    pallas_call x1, Pallas kernels, prepared(): pl.pallas_call(prep_kernel, in_specs=[VMEM] + [SMEM] * 3 + [HBM], out_spe...  2.78 us
  transfers between devices with their start and end apart: 6, of which 2 were waited for; matrix products, arithmetic and copies ran while one was open for 3% of the time, Pallas kernels for 9%

profile of v5, /device:TPU:1, one launch (start us, length us, event | category | flops | bytes accessed | tf_op | source)
XLA Modules:
  0.0 99.8 jit_solution(12175748398320333179)
XLA Ops:
  1.3 2.8 %prepared.1 = (f32[128,2,128]{2,1,0:T(2,128)}, bf16[2,384,384]{2,1,0:T(8,128)(2,1)}, s32[15]{0:T(128)}) custom-call(f32[1,512]{1,0:T(1,128)} %coef.1, f32[1]{0:T(128)S(6)} %copy.25.energy, s32[4]{0:T(128)} %shifts.1, s32[8]{0:T(128)} %sizes.1, bf16[2,2,384,384]{3,2,1,0:T(8,128)(2,1)} %psi.3), custom_call_target="tpu_custom_call" | custom-call | tf_op jit(solution)/shard_map/prepared/pallas_call | solution.py:53
  4.1 1.3 %collective-permute-start = (bf16[2,384,384]{2,1,0:T(8,128)(2,1)}, bf16[2,384,384]{2,1,0:T(8,128)(2,1)S(1)}, u32[]{:S(2)}, u32[]{:S(2)}) collective-permute-start(bf16[2,384,384]{2,1,0:T(8,128)(2,1)} %get-tuple-element.11), channel_id=1, source_target_pairs={{0,1},{1,2},{2,3},{5,4},{6,5},{7,6},{8,9},{9,10},{10,11},{13,12},{... | collective-permute-start | bytes 1769480 | tf_op jit(solution)/shard_map/ppermute | solution.py:325
  5.4 21.0 %all-to-all-start = ((f32[128,2,128]{2,1,0:T(2,128)}), f32[128,2,128]{2,1,0:T(2,128)}, u32[]{:S(2)}, u32[]{:S(2)}) async-start(f32[128,2,128]{2,1,0:T(2,128)} %get-tuple-element.10), calls=%async_computation | async-start | bytes 262144 | tf_op jit(solution)/shard_map/all_to_all | solution.py:326
  26.4 2.9 %collective-permute-start.1 = (bf16[4,2,384,384]{3,2,1,0:T(8,128)(2,1)}, bf16[4,2,384,384]{3,2,1,0:T(8,128)(2,1)}, u32[]{:S(2)}, u32[]{:S(2)}) collective-permute-start(bf16[4,2,384,384]{3,2,1,0:T(8,128)(2,1)} %left.1), channel_id=1, source_target_pairs={{0,4},{4,0},{1,5},{5,1},{2,6},{6,2},{3,7},{7,3},{8,12},{12,8},{9,1... | collective-permute-start | bytes 7077896 | tf_op jit(solution)/shard_map/ppermute | solution.py:327
  29.3 1.9 %collective-permute-start.2 = (bf16[4,2,384,384]{3,2,1,0:T(8,128)(2,1)}, bf16[4,2,384,384]{3,2,1,0:T(8,128)(2,1)}, u32[]{:S(2)}, u32[]{:S(2)}) collective-permute-start(bf16[4,2,384,384]{3,2,1,0:T(8,128)(2,1)} %right.1), channel_id=1, source_target_pairs={{0,4},{4,0},{1,5},{5,1},{2,6},{6,2},{3,7},{7,3},{8,12},{12,8},{9,1... | collective-permute-start | bytes 7077896 | tf_op jit(solution)/shard_map/ppermute | solution.py:328
  31.9 0.0 collective-permute-done.halo
  31.9 0.0 copy-start.3
  31.9 0.8 copy-done.3
  32.7 0.0 copy-start
  32.7 0.7 copy-done
  33.3 0.0 copy-start.1
  33.3 8.7 %own_terms.1 = (f32[4,2,384,384]{3,2,1,0:T(8,128)}, bf16[3,384,768]{2,1,0:T(8,128)(2,1)}) custom-call(s32[15]{0:T(128)S(1)} %copy-done, bf16[2,2,384,384]{3,2,1,0:T(8,128)(2,1)} %psi.3, bf16[2,384,384]{2,1,0:T(8,128)(2,1)} %copy-done.3, bf16[4,2,384,384]{3,2,1,0:T(8,128)(2,1)} %left.1, bf16[4,2,384,384]{3,2,1,0:T(8,128)(2,1)} %right.1), custom_call_target="tpu_custom_call" | custom-call | flops 181193932800 | bytes 1179648000 | tf_op jit(solution)/shard_map/own_terms/pallas_call | solution.py:150
  42.0 0.0 all-to-all-done.words
  42.1 0.0 collective-permute-done.1.left
  42.1 0.0 collective-permute-done.2.right
  42.1 0.0 copy-done.1
  42.1 10.0 %sigma_blocks.1 = (f32[64,40,128]{2,1,0:T(8,128)S(1)}, f32[2,128]{1,0:T(2,128)S(1)}) custom-call(s32[15]{0:T(128)S(1)} %copy-done.1, s32[1]{0:T(128)} %copy.26.owner, f32[128,2,128]{2,1,0:T(2,128)} %all-to-all-done.words, f32[4,2,384,384]{3,2,1,0:T(8,128)} %get-tuple-element.12.own, bf16[3,384,768]{2,1,0:T(8,128)(2,1)} %get-tuple-element.13.sources, ...), custom_call_target="tpu_custom_call" | custom-call | flops 1811939328 | bytes 11796480 | tf_op jit(solution)/shard_map/sigma_blocks/pallas_call | solution.py:283
  52.1 0.0 copy-start.2
  52.1 0.9 convert_element_type.18
  53.0 12.3 %all-to-all-start.1 = ((f16[64,40,128]{2,1,0:T(8,128)(2,1)}), f16[64,40,128]{2,1,0:T(8,128)(2,1)S(1)}, u32[]{:S(2)}, u32[]{:S(2)}) async-start(f16[64,40,128]{2,1,0:T(8,128)(2,1)} %convert_element_type.18), calls=%async_computation.1 | async-start | bytes 1310720 | tf_op jit(solution)/shard_map/all_to_all | solution.py:341
  65.3 0.0 copy-done.2
  65.4 0.1 dynamic_slice.14
  65.4 0.1 broadcast_compare_fusion
  65.5 0.1 iota_compare_fusion
  65.6 0.1 broadcast_and_fusion
  65.7 0.1 slice_reduce_fusion.1
  65.8 18.4 %all-to-all-done.1 = f16[64,40,128]{2,1,0:T(8,128)(2,1)S(1)} async-done(((f16[64,40,128]{2,1,0:T(8,128)(2,1)}), f16[64,40,128]{2,1,0:T(8,128)(2,1)S(1)}, u32[]{:S(2)}, u32[]{:S(2)}) %all-to-all-start.1) | async-done | bytes 655392 | tf_op jit(solution)/shard_map/all_to_all | solution.py:341
  84.2 0.2 fusion.9
  84.4 0.1 fusion.7
  84.5 0.2 multiply_reduce_fusion
  84.8 0.1 fusion.11
  84.9 0.7 pad_maximum_fusion
  85.5 7.2 %all-to-all-start.2 = ((f32[8,19,128]{2,1,0:T(8,128)}), f32[8,19,128]{2,1,0:T(8,128)S(1)}, u32[]{:S(2)}, u32[]{:S(2)}) async-start(f32[8,19,128]{2,1,0:T(8,128)} %bitcast.3), calls=%async_computation.2 | async-start | bytes 196608 | tf_op jit(solution)/shard_map/all_to_all | solution.py:358
  92.7 0.8 constant_dynamic-slice_fusion
  93.5 1.0 slice.60
  94.5 0.5 constant_dynamic-slice_fusion.1
  95.0 2.7 %all-to-all-done.2 = f32[8,19,128]{2,1,0:T(8,128)S(1)} async-done(((f32[8,19,128]{2,1,0:T(8,128)}), f32[8,19,128]{2,1,0:T(8,128)S(1)}, u32[]{:S(2)}, u32[]{:S(2)}) %all-to-all-start.2) | async-done | bytes 77856 | tf_op jit(solution)/shard_map/all_to_all | solution.py:358
  97.9 1.2 %broadcast_subtract_fusion = (f32[2]{0:T(128)S(1)}, f32[2]{0:T(128)}) fusion(f32[]{:T(128)} %bitcast.9, f32[4]{0:T(128)S(1)} %slice_reduce_fusion), kind=kLoop, calls=%fused_computation.31 | loop fusion | flops 10 | bytes 36 | tf_op jit(solution)/shard_map/sub | solution.py:374
  99.1 0.7 fusion.10
  (13 shorter events, 0.2 us)
Async XLA Ops:
  4.1 27.8 %collective-permute-start = (bf16[2,384,384]{2,1,0:T(8,128)(2,1)}, bf16[2,384,384]{2,1,0:T(8,128)(2,1)S(1)}, u32[]{:S(2)}, u32[]{:S(2)}) collective-permute-start(bf16[2,384,384]{2,1,0:T(8,128)(2,1)} %get-tuple-element.11), channel_id=1, source_target_pairs={{0,1},{1,2},{2,3},{5,4},{6,5},{7,6},{8,9},{9,10},{10,11},{13,12},{... | collective-permute-start | bytes 1769480 | tf_op jit(solution)/shard_map/ppermute | solution.py:325
  5.4 36.7 %all-to-all-start = ((f32[128,2,128]{2,1,0:T(2,128)}), f32[128,2,128]{2,1,0:T(2,128)}, u32[]{:S(2)}, u32[]{:S(2)}) async-start(f32[128,2,128]{2,1,0:T(2,128)} %get-tuple-element.10), calls=%async_computation | async-start | bytes 262144 | tf_op jit(solution)/shard_map/all_to_all | solution.py:326
  26.4 15.7 %collective-permute-start.1 = (bf16[4,2,384,384]{3,2,1,0:T(8,128)(2,1)}, bf16[4,2,384,384]{3,2,1,0:T(8,128)(2,1)}, u32[]{:S(2)}, u32[]{:S(2)}) collective-permute-start(bf16[4,2,384,384]{3,2,1,0:T(8,128)(2,1)} %left.1), channel_id=1, source_target_pairs={{0,4},{4,0},{1,5},{5,1},{2,6},{6,2},{3,7},{7,3},{8,12},{12,8},{9,1... | collective-permute-start | bytes 7077896 | tf_op jit(solution)/shard_map/ppermute | solution.py:327
  29.3 12.8 %collective-permute-start.2 = (bf16[4,2,384,384]{3,2,1,0:T(8,128)(2,1)}, bf16[4,2,384,384]{3,2,1,0:T(8,128)(2,1)}, u32[]{:S(2)}, u32[]{:S(2)}) collective-permute-start(bf16[4,2,384,384]{3,2,1,0:T(8,128)(2,1)} %right.1), channel_id=1, source_target_pairs={{0,4},{4,0},{1,5},{5,1},{2,6},{6,2},{3,7},{7,3},{8,12},{12,8},{9,1... | collective-permute-start | bytes 7077896 | tf_op jit(solution)/shard_map/ppermute | solution.py:328
  31.9 0.8 copy-start.3
  32.7 0.7 copy-start
  33.3 8.7 %copy-start.1 = (s32[15]{0:T(128)S(1)}, s32[15]{0:T(128)}, u32[]{:S(2)}) copy-start(s32[15]{0:T(128)} %get-tuple-element.9.table) | copy-start | bytes 184
  52.1 13.2 %copy-start.2 = (s32[8]{0:T(128)S(1)}, s32[8]{0:T(128)}, u32[]{:S(2)}) copy-start(s32[8]{0:T(128)} %sizes.1) | copy-start | bytes 100
  53.0 31.1 %all-to-all-start.1 = ((f16[64,40,128]{2,1,0:T(8,128)(2,1)}), f16[64,40,128]{2,1,0:T(8,128)(2,1)S(1)}, u32[]{:S(2)}, u32[]{:S(2)}) async-start(f16[64,40,128]{2,1,0:T(8,128)(2,1)} %convert_element_type.18), calls=%async_computation.1 | async-start | bytes 1310720 | tf_op jit(solution)/shard_map/all_to_all | solution.py:341
  85.5 12.2 %all-to-all-start.2 = ((f32[8,19,128]{2,1,0:T(8,128)}), f32[8,19,128]{2,1,0:T(8,128)S(1)}, u32[]{:S(2)}, u32[]{:S(2)}) async-start(f32[8,19,128]{2,1,0:T(8,128)} %bitcast.3), calls=%async_computation.2 | async-start | bytes 196608 | tf_op jit(solution)/shard_map/all_to_all | solution.py:358

commit v6 on v5

--- a/solution.py
+++ b/solution.py
@@ -11,6 +11,7 @@
 OP = ("chip", "core")
 HEAD, PIECE = 1024.0, 2048.0
 TILES = 4
+EARLY = 2
 LANES = 128
 SMEM = pl.BlockSpec(memory_space=pltpu.SMEM)
 VMEM = pl.BlockSpec(memory_space=pltpu.VMEM)
@@ -60,18 +61,18 @@
             jax.ShapeDtypeStruct((SHIFTS + shifts.shape[0] + sizes.shape[0],), jnp.int32),
         ],
         scratch_shapes=[pltpu.SemaphoreType.DMA((2,))],
-        compiler_params=pltpu.CompilerParams(vmem_limit_bytes=60000000),
+        compiler_params=pltpu.CompilerParams(vmem_limit_bytes=60_000_000),
         name="prepared",
     )(coef, energy, shifts, sizes, psi)
 
 
-def loads(core, left, right, lefts, rights, sems):
+def loads(core, left, right, lefts, rights, sems, pairs, at=0):
     return [
         (
-            pltpu.make_async_copy(left.at[k, core], lefts.at[k], sems.at[0, k]),
-            pltpu.make_async_copy(right.at[k, core], rights.at[k], sems.at[1, k]),
+            pltpu.make_async_copy(left.at[k, core], lefts.at[at + i], sems.at[0, at + i]),
+            pltpu.make_async_copy(right.at[k, core], rights.at[at + i], sems.at[1, at + i]),
         )
-        for k in range(lefts.shape[0])
+        for i, k in enumerate(pairs)
     ]
 
 
@@ -98,12 +99,13 @@
     psis, halos, lefts, rights, made, src, sems, out_sems, more,
 ):
     core, blk = table[CORE], table[BLK]
-    pairs, size = lefts.shape[0], lefts.shape[1]
+    early, size = lefts.shape[0], lefts.shape[1]
+    pairs = left.shape[0]
     psi_copy = pltpu.make_async_copy(psi, psis, more.at[0])
     halo_copy = pltpu.make_async_copy(halo, halos, more.at[1])
     psi_copy.start()
     halo_copy.start()
-    copies = loads(core, left, right, lefts, rights, sems)
+    copies = loads(core, left, right, lefts, rights, sems, range(early))
     for pair in copies:
         for copy in pair:
             copy.start()
@@ -124,7 +126,7 @@
             src[slot, :, v * size : (v + 1) * size] = block * live
     source_copy = pltpu.make_async_copy(src, sources, more.at[2])
     outs = []
-    for k in range(pairs):
+    for k in range(early):
         terms_k = product(core, table[SHIFTS + k], src, lefts.at[k], rights.at[k], copies[k])
         for v in range(2):
             made[k, v] = terms_k[v]
@@ -152,21 +154,21 @@
         in_specs=[SMEM] + [HBM] * 4,
         out_specs=[HBM, HBM],
         out_shape=[
-            jax.ShapeDtypeStruct((pairs, 2, size, size), F32),
+            jax.ShapeDtypeStruct((EARLY, 2, size, size), F32),
             jax.ShapeDtypeStruct((3, size, 2 * size), BF16),
         ],
         scratch_shapes=[
             pltpu.VMEM(psi.shape, BF16),
             pltpu.VMEM(halo.shape, BF16),
-            pltpu.VMEM((pairs, size, size), BF16),
-            pltpu.VMEM((pairs, size, size), BF16),
-            pltpu.VMEM((pairs, 2, size, size), F32),
+            pltpu.VMEM((EARLY, size, size), BF16),
+            pltpu.VMEM((EARLY, size, size), BF16),
+            pltpu.VMEM((EARLY, 2, size, size), F32),
             pltpu.VMEM((3, size, 2 * size), BF16),
-            pltpu.SemaphoreType.DMA((2, pairs)),
-            pltpu.SemaphoreType.DMA((2 * pairs,)),
+            pltpu.SemaphoreType.DMA((2, EARLY)),
+            pltpu.SemaphoreType.DMA((2 * EARLY,)),
             pltpu.SemaphoreType.DMA((3,)),
         ],
-        compiler_params=pltpu.CompilerParams(vmem_limit_bytes=56200000),
+        compiler_params=pltpu.CompilerParams(vmem_limit_bytes=62_850_000),
         cost_estimate=estimate(100 * pairs, size),
         name="own_terms",
     )(table, psi, halo, left, right)
@@ -187,22 +189,22 @@
 
 
 def sigma_kernel(
-    table, owner, words, own, sources, left, right, packed, norm,
+    table, owner, words, own, sources, left, right, left_got, right_got, packed, norm,
     lefts, rights, owns, src, acc, sems, own_sems, more,
 ):
     core, chip = table[CORE], table[CHIP]
-    pairs, size = lefts.shape[0], lefts.shape[1]
+    pairs, size = left.shape[0], left.shape[2]
+    early = own.shape[0]
+    late = range(early, pairs)
     source_copy = pltpu.make_async_copy(sources, src, more.at[0])
     source_copy.start()
-    copies = loads(core, left, right, lefts, rights, sems)
+    copies = loads(core, left, right, lefts, rights, sems, late)
+    copies += loads(core, left_got, right_got, lefts, rights, sems, range(pairs), len(late))
     own_copies = [
-        pltpu.make_async_copy(own.at[k], owns.at[k], own_sems.at[k]) for k in range(pairs)
-    ]
-    for k in range(pairs):
-        copies[k][0].start()
-        copies[k][1].start()
-    for k in range(pairs):
-        own_copies[k].start()
+        pltpu.make_async_copy(own.at[k], owns.at[k], own_sems.at[k]) for k in range(early)
+    ]
+    for copy in [copy for pair in copies for copy in pair] + own_copies:
+        copy.start()
 
     chips = packed.shape[0]
     chip_rows = size // chips
@@ -215,18 +217,21 @@
     got_weight = pltpu.roll(line, LANES - first - (1 - core) * pairs, 1)
     facts = words[2 * chip + 1 - core, 1:2, :]
     spot = lax.broadcasted_iota(jnp.int32, (1, LANES), 1)
-    shifts = [
+    shifts = [table[SHIFTS + k] for k in late]
+    shifts += [
         jnp.sum(jnp.where(spot == 1 + k, facts, 0.0)).astype(jnp.int32) for k in range(pairs)
     ]
 
     source_copy.wait()
-    for k in range(pairs):
-        terms = product(core, shifts[k], src, lefts.at[k], rights.at[k], copies[k])
+    weights = [own_weight[0:1, k : k + 1] for k in late]
+    weights += [got_weight[0:1, k : k + 1] for k in range(pairs)]
+    for i, weight in enumerate(weights):
+        terms = product(core, shifts[i], src, lefts.at[i], rights.at[i], copies[i])
         for v in range(2):
-            total = got_weight[0:1, k : k + 1] * terms[v]
-            acc[v] = total if k == 0 else acc[v] + total
-    for k in range(pairs):
-        own_copies[k].wait()
+            total = weight * terms[v]
+            acc[v] = total if i == 0 else acc[v] + total
+    for copy in own_copies:
+        copy.wait()
 
     tile = size // TILES
     here = chips // TILES
@@ -238,7 +243,7 @@
         top = None
         for v in range(2):
             total = acc[v, rows, :]
-            for k in range(pairs):
+            for k in range(early):
                 total += own_weight[0:1, k : k + 1] * owns[k, v, rows, :]
             acc[v, rows, :] = total
             psi = src[core, rows, v * size : (v + 1) * size].astype(F32)
@@ -277,31 +282,31 @@
         norm[v : v + 1, :] = jnp.broadcast_to(jnp.sum(sums[2 + v], keepdims=True), (1, LANES))
 
 
-def sigma_blocks(chips, table, owner, words, own, sources, left, right):
+def sigma_blocks(chips, table, owner, words, own, sources, left, right, left_got, right_got):
     pairs, _, size, _ = left.shape
     lines = -(-(2 * size * size // chips // LANES + 1) // 8) * 8
     return pl.pallas_call(
         sigma_kernel,
-        in_specs=[SMEM] * 2 + [VMEM] + [HBM] * 4,
+        in_specs=[SMEM] * 2 + [VMEM] + [HBM] * 6,
         out_specs=[VMEM, VMEM],
         out_shape=[
             jax.ShapeDtypeStruct((chips, lines, LANES), F32),
             jax.ShapeDtypeStruct((2, LANES), F32),
         ],
         scratch_shapes=[
-            pltpu.VMEM((pairs, size, size), BF16),
-            pltpu.VMEM((pairs, size, size), BF16),
-            pltpu.VMEM((pairs, 2, size, size), F32),
+            pltpu.VMEM((2 * pairs - EARLY, size, size), BF16),
+            pltpu.VMEM((2 * pairs - EARLY, size, size), BF16),
+            pltpu.VMEM((EARLY, 2, size, size), F32),
             pltpu.VMEM((3, size, 2 * size), BF16),
             pltpu.VMEM((2, size, size), F32),
-            pltpu.SemaphoreType.DMA((2, pairs)),
-            pltpu.SemaphoreType.DMA((pairs,)),
+            pltpu.SemaphoreType.DMA((2, 2 * pairs - EARLY)),
+            pltpu.SemaphoreType.DMA((EARLY,)),
             pltpu.SemaphoreType.DMA((1,)),
         ],
         compiler_params=pltpu.CompilerParams(vmem_limit_bytes=55_000_000),
         cost_estimate=estimate(pairs, size),
         name="sigma_blocks",
-    )(table, owner, words, own, sources, left, right)
+    )(table, owner, words, own, sources, left, right, left_got, right_got)
 
 
 def on_device(
@@ -335,7 +340,16 @@
         right_ops,
     )
     packed, norm = sigma_blocks(
-        chips, table, site_owner, words, own, sources, left_got, right_got
+        chips,
+        table,
+        site_owner,
+        words,
+        own,
+        sources,
+        left_ops,
+        right_ops,
+        left_got,
+        right_got,
     )
 
     blocks = lax.all_to_all(packed.astype(F16), "chip", 0, 0, tiled=True)

time: 100 us -> 99.2 us (level)
    pallas_call x1, Pallas kernels: 8.69 us -> 6.13 us  [own_terms(): pl.pallas_call(functools.partial(own_kernel, sectors), in_specs=[SMEM] +...]
    pallas_call x1, Pallas kernels: 10 us -> 11.9 us  [sigma_blocks(): pl.pallas_call(sigma_kernel, in_specs=[SMEM] * 2 + [VMEM] + [HBM] * 6, ou...]
  transfers between devices with their start and end apart: 6 -> 6, of which waited for: 2 -> 2; matrix products, arithmetic and copies ran while one was open for 3% -> 3% of each run, Pallas kernels for 9% -> 6%
where the time goes in v6:
time: 99.2 us; the launch traced here: 98.5 us
  starting transfers between devices  46.6 us (47%)
  waiting for transfers between devices  21.1 us (21%)
  Pallas kernels  20.8 us (21%)
  other arithmetic  4.35 us (4%)
  local copies, waits for them, and re-layouts  3.52 us (4%)
  between operations  2.14 us (2%)
    all_to_all x1, starting transfers between devices, on_device(): words = lax.all_to_all(words, OP, 0, 0, tiled=True)  21 us
    all_to_all x1, waiting for transfers between devices, on_device(): blocks = lax.all_to_all(packed.astype(F16), 'chip', 0, 0, tiled=True)  18.4 us
    all_to_all x1, starting transfers between devices, on_device(): blocks = lax.all_to_all(packed.astype(F16), 'chip', 0, 0, tiled=True)  12.3 us
    pallas_call x1, Pallas kernels, sigma_blocks(): pl.pallas_call(sigma_kernel, in_specs=[SMEM] * 2 + [VMEM] + [HBM] * 6, ou...  11.9 us
    all_to_all x1, starting transfers between devices, on_device(): came = lax.all_to_all(sent, ('core', 'blk'), 0, 0, tiled=True)  7.17 us
    pallas_call x1, Pallas kernels, own_terms(): pl.pallas_call(functools.partial(own_kernel, sectors), in_specs=[SMEM] +...  6.13 us
    ppermute x1, starting transfers between devices, on_device(): left_got = lax.ppermute(left_ops, 'core', swap)  2.88 us
    pallas_call x1, Pallas kernels, prepared(): pl.pallas_call(prep_kernel, in_specs=[VMEM] + [SMEM] * 3 + [HBM], out_spe...  2.78 us
  transfers between devices with their start and end apart: 6, of which 2 were waited for; matrix products, arithmetic and copies ran while one was open for 3% of the time, Pallas kernels for 6%

profile of v6, /device:TPU:1, one launch (start us, length us, event | category | flops | bytes accessed | tf_op | source)
XLA Modules:
  0.0 98.5 jit_solution(16782682778568905105)
XLA Ops:
  1.3 2.8 %prepared.1 = (f32[128,2,128]{2,1,0:T(2,128)}, bf16[2,384,384]{2,1,0:T(8,128)(2,1)}, s32[15]{0:T(128)}) custom-call(f32[1,512]{1,0:T(1,128)} %coef.1, f32[1]{0:T(128)S(6)} %copy.25.energy, s32[4]{0:T(128)} %shifts.1, s32[8]{0:T(128)} %sizes.1, bf16[2,2,384,384]{3,2,1,0:T(8,128)(2,1)} %psi.3), custom_call_target="tpu_custom_call" | custom-call | tf_op jit(solution)/shard_map/prepared/pallas_call | solution.py:54
  4.1 1.3 %collective-permute-start = (bf16[2,384,384]{2,1,0:T(8,128)(2,1)}, bf16[2,384,384]{2,1,0:T(8,128)(2,1)S(1)}, u32[]{:S(2)}, u32[]{:S(2)}) collective-permute-start(bf16[2,384,384]{2,1,0:T(8,128)(2,1)} %get-tuple-element.11), channel_id=1, source_target_pairs={{0,1},{1,2},{2,3},{5,4},{6,5},{7,6},{8,9},{9,10},{10,11},{13,12},{... | collective-permute-start | bytes 1769480 | tf_op jit(solution)/shard_map/ppermute | solution.py:330
  5.4 21.0 %all-to-all-start = ((f32[128,2,128]{2,1,0:T(2,128)}), f32[128,2,128]{2,1,0:T(2,128)}, u32[]{:S(2)}, u32[]{:S(2)}) async-start(f32[128,2,128]{2,1,0:T(2,128)} %get-tuple-element.10), calls=%async_computation | async-start | bytes 262144 | tf_op jit(solution)/shard_map/all_to_all | solution.py:331
  26.4 2.9 %collective-permute-start.1 = (bf16[4,2,384,384]{3,2,1,0:T(8,128)(2,1)}, bf16[4,2,384,384]{3,2,1,0:T(8,128)(2,1)}, u32[]{:S(2)}, u32[]{:S(2)}) collective-permute-start(bf16[4,2,384,384]{3,2,1,0:T(8,128)(2,1)} %left.3), channel_id=1, source_target_pairs={{0,4},{4,0},{1,5},{5,1},{2,6},{6,2},{3,7},{7,3},{8,12},{12,8},{9,1... | collective-permute-start | bytes 7077896 | tf_op jit(solution)/shard_map/ppermute | solution.py:332
  29.3 1.9 %collective-permute-start.2 = (bf16[4,2,384,384]{3,2,1,0:T(8,128)(2,1)}, bf16[4,2,384,384]{3,2,1,0:T(8,128)(2,1)}, u32[]{:S(2)}, u32[]{:S(2)}) collective-permute-start(bf16[4,2,384,384]{3,2,1,0:T(8,128)(2,1)} %right.3), channel_id=1, source_target_pairs={{0,4},{4,0},{1,5},{5,1},{2,6},{6,2},{3,7},{7,3},{8,12},{12,8},{9,1... | collective-permute-start | bytes 7077896 | tf_op jit(solution)/shard_map/ppermute | solution.py:333
  31.9 0.0 collective-permute-done.halo
  31.9 0.0 copy-start.2
  31.9 0.9 copy-done.2
  32.8 0.0 copy-start
  32.8 6.1 %own_terms.1 = (f32[2,2,384,384]{3,2,1,0:T(8,128)}, bf16[3,384,768]{2,1,0:T(8,128)(2,1)}) custom-call(s32[15]{0:T(128)} %get-tuple-element.9.table, bf16[2,2,384,384]{3,2,1,0:T(8,128)(2,1)} %psi.3, bf16[2,384,384]{2,1,0:T(8,128)(2,1)} %copy-done.2, bf16[4,2,384,384]{3,2,1,0:T(8,128)(2,1)} %left.3, bf16[4,2,384,384]{3,2,1,0:T(8,128)(2,1)} %right.3), custom_call_target="tpu_custom_call" | custom-call | flops 181193932800 | bytes 1179648000 | tf_op jit(solution)/shard_map/own_terms/pallas_call | solution.py:152
  38.9 0.0 all-to-all-done.words
  38.9 0.0 collective-permute-done.1.left_got
  38.9 0.0 collective-permute-done.2.right_got
  39.0 0.0 copy-done
  39.0 11.9 %sigma_blocks.1 = (f32[64,40,128]{2,1,0:T(8,128)S(1)}, f32[2,128]{1,0:T(2,128)S(1)}) custom-call(s32[15]{0:T(128)S(1)} %copy-done, s32[1]{0:T(128)} %copy.26.owner, f32[128,2,128]{2,1,0:T(2,128)} %all-to-all-done.words, f32[2,2,384,384]{3,2,1,0:T(8,128)} %get-tuple-element.12.own, bf16[3,384,768]{2,1,0:T(8,128)(2,1)} %get-tuple-element.13.sources, ...), custom_call_target="tpu_custom_call" | custom-call | flops 1811939328 | bytes 11796480 | tf_op jit(solution)/shard_map/sigma_blocks/pallas_call | solution.py:288
  50.8 0.0 copy-start.1
  50.8 0.9 convert_element_type.18
  51.8 12.3 %all-to-all-start.1 = ((f16[64,40,128]{2,1,0:T(8,128)(2,1)}), f16[64,40,128]{2,1,0:T(8,128)(2,1)S(1)}, u32[]{:S(2)}, u32[]{:S(2)}) async-start(f16[64,40,128]{2,1,0:T(8,128)(2,1)} %convert_element_type.18), calls=%async_computation.1 | async-start | bytes 1310720 | tf_op jit(solution)/shard_map/all_to_all | solution.py:355
  64.1 0.0 copy-done.1
  64.1 0.1 dynamic_slice.14
  64.2 0.1 broadcast_compare_fusion
  64.2 0.1 iota_compare_fusion
  64.3 0.1 broadcast_and_fusion
  64.4 0.1 slice_reduce_fusion.1
  64.5 18.4 %all-to-all-done.1 = f16[64,40,128]{2,1,0:T(8,128)(2,1)S(1)} async-done(((f16[64,40,128]{2,1,0:T(8,128)(2,1)}), f16[64,40,128]{2,1,0:T(8,128)(2,1)S(1)}, u32[]{:S(2)}, u32[]{:S(2)}) %all-to-all-start.1) | async-done | bytes 655392 | tf_op jit(solution)/shard_map/all_to_all | solution.py:355
  83.0 0.2 fusion.9
  83.1 0.1 fusion.7
  83.3 0.2 multiply_reduce_fusion
  83.5 0.1 fusion.11
  83.6 0.6 pad_maximum_fusion
  84.3 7.2 %all-to-all-start.2 = ((f32[8,19,128]{2,1,0:T(8,128)}), f32[8,19,128]{2,1,0:T(8,128)S(1)}, u32[]{:S(2)}, u32[]{:S(2)}) async-start(f32[8,19,128]{2,1,0:T(8,128)} %bitcast.3), calls=%async_computation.2 | async-start | bytes 196608 | tf_op jit(solution)/shard_map/all_to_all | solution.py:372
  91.4 0.8 constant_dynamic-slice_fusion
  92.3 1.0 slice.60
  93.2 0.5 constant_dynamic-slice_fusion.1
  93.7 2.7 %all-to-all-done.2 = f32[8,19,128]{2,1,0:T(8,128)S(1)} async-done(((f32[8,19,128]{2,1,0:T(8,128)}), f32[8,19,128]{2,1,0:T(8,128)S(1)}, u32[]{:S(2)}, u32[]{:S(2)}) %all-to-all-start.2) | async-done | bytes 77856 | tf_op jit(solution)/shard_map/all_to_all | solution.py:372
  96.6 1.2 %broadcast_subtract_fusion = (f32[2]{0:T(128)S(1)}, f32[2]{0:T(128)}) fusion(f32[]{:T(128)} %bitcast.9, f32[4]{0:T(128)S(1)} %slice_reduce_fusion), kind=kLoop, calls=%fused_computation.31 | loop fusion | flops 10 | bytes 36 | tf_op jit(solution)/shard_map/sub | solution.py:388
  97.8 0.7 fusion.10
  (13 shorter events, 0.2 us)
Async XLA Ops:
  4.1 27.8 %collective-permute-start = (bf16[2,384,384]{2,1,0:T(8,128)(2,1)}, bf16[2,384,384]{2,1,0:T(8,128)(2,1)S(1)}, u32[]{:S(2)}, u32[]{:S(2)}) collective-permute-start(bf16[2,384,384]{2,1,0:T(8,128)(2,1)} %get-tuple-element.11), channel_id=1, source_target_pairs={{0,1},{1,2},{2,3},{5,4},{6,5},{7,6},{8,9},{9,10},{10,11},{13,12},{... | collective-permute-start | bytes 1769480 | tf_op jit(solution)/shard_map/ppermute | solution.py:330
  5.4 33.6 %all-to-all-start = ((f32[128,2,128]{2,1,0:T(2,128)}), f32[128,2,128]{2,1,0:T(2,128)}, u32[]{:S(2)}, u32[]{:S(2)}) async-start(f32[128,2,128]{2,1,0:T(2,128)} %get-tuple-element.10), calls=%async_computation | async-start | bytes 262144 | tf_op jit(solution)/shard_map/all_to_all | solution.py:331
  26.4 12.5 %collective-permute-start.1 = (bf16[4,2,384,384]{3,2,1,0:T(8,128)(2,1)}, bf16[4,2,384,384]{3,2,1,0:T(8,128)(2,1)}, u32[]{:S(2)}, u32[]{:S(2)}) collective-permute-start(bf16[4,2,384,384]{3,2,1,0:T(8,128)(2,1)} %left.3), channel_id=1, source_target_pairs={{0,4},{4,0},{1,5},{5,1},{2,6},{6,2},{3,7},{7,3},{8,12},{12,8},{9,1... | collective-permute-start | bytes 7077896 | tf_op jit(solution)/shard_map/ppermute | solution.py:332
  29.3 9.7 %collective-permute-start.2 = (bf16[4,2,384,384]{3,2,1,0:T(8,128)(2,1)}, bf16[4,2,384,384]{3,2,1,0:T(8,128)(2,1)}, u32[]{:S(2)}, u32[]{:S(2)}) collective-permute-start(bf16[4,2,384,384]{3,2,1,0:T(8,128)(2,1)} %right.3), channel_id=1, source_target_pairs={{0,4},{4,0},{1,5},{5,1},{2,6},{6,2},{3,7},{7,3},{8,12},{12,8},{9,1... | collective-permute-start | bytes 7077896 | tf_op jit(solution)/shard_map/ppermute | solution.py:333
  31.9 0.9 copy-start.2
  32.8 6.2 %copy-start = (s32[15]{0:T(128)S(1)}, s32[15]{0:T(128)}, u32[]{:S(2)}) copy-start(s32[15]{0:T(128)} %get-tuple-element.9.table) | copy-start | bytes 184
  50.8 13.2 %copy-start.1 = (s32[8]{0:T(128)S(1)}, s32[8]{0:T(128)}, u32[]{:S(2)}) copy-start(s32[8]{0:T(128)} %sizes.1) | copy-start | bytes 100
  51.8 31.2 %all-to-all-start.1 = ((f16[64,40,128]{2,1,0:T(8,128)(2,1)}), f16[64,40,128]{2,1,0:T(8,128)(2,1)S(1)}, u32[]{:S(2)}, u32[]{:S(2)}) async-start(f16[64,40,128]{2,1,0:T(8,128)(2,1)} %convert_element_type.18), calls=%async_computation.1 | async-start | bytes 1310720 | tf_op jit(solution)/shard_map/all_to_all | solution.py:355
  84.3 12.2 %all-to-all-start.2 = ((f32[8,19,128]{2,1,0:T(8,128)}), f32[8,19,128]{2,1,0:T(8,128)S(1)}, u32[]{:S(2)}, u32[]{:S(2)}) async-start(f32[8,19,128]{2,1,0:T(8,128)} %bitcast.3), calls=%async_computation.2 | async-start | bytes 196608 | tf_op jit(solution)/shard_map/all_to_all | solution.py:372

commit v7 on v6

--- a/solution.py
+++ b/solution.py
@@ -36,7 +36,7 @@
         table[SHIFTS + pairs + b] = sizes[b]
     spot = lax.broadcasted_iota(jnp.int32, (2, LANES), 1)
     row = lax.broadcasted_iota(jnp.int32, (2, LANES), 0)
-    facts = jnp.where(spot == 0, energy[0], 0.0)
+    facts = jnp.where(spot == 0, energy[0:1, 0:1], 0.0)
     for k in range(pairs):
         facts = jnp.where(spot == 1 + k, shifts[k].astype(F32), facts)
     lines = coef.shape[1] // LANES
@@ -53,7 +53,7 @@
     size = psi.shape[2]
     return pl.pallas_call(
         prep_kernel,
-        in_specs=[VMEM] + [SMEM] * 3 + [HBM],
+        in_specs=[VMEM] * 2 + [SMEM] * 2 + [HBM],
         out_specs=[VMEM, VMEM, SMEM],
         out_shape=[
             jax.ShapeDtypeStruct((ops, 2, LANES), F32),
@@ -76,22 +76,25 @@
     ]
 
 
-def product(core, shift, src, left, right, copies):
+def slot_of(core, shift):
+    slot = core - shift
+    return jnp.where((slot == 0) | (slot == 1), slot, 2)
+
+
+def product(slot, src, left, right):
     size = left.shape[0]
-    copies[0].wait()
-    slot = core - shift
-    slot = jnp.where((slot == 0) | (slot == 1), slot, 2)
     part = jnp.dot(left[...], src[slot], preferred_element_type=F32).astype(BF16)
-    copies[1].wait()
-    return [
-        lax.dot_general(
-            part[:, v * size : (v + 1) * size],
-            right[...],
-            (((1,), (1,)), ((), ())),
-            preferred_element_type=F32,
-        )
-        for v in range(2)
-    ]
+    part = jnp.concatenate([part[:, :size], part[:, size:]], axis=0)
+    terms = lax.dot_general(
+        part, right[...], (((1,), (1,)), ((), ())), preferred_element_type=F32
+    )
+    return [terms[:size], terms[size:]]
+
+
+def wait_for(pairs):
+    for copies in pairs:
+        for copy in copies:
+            copy.wait()
 
 
 def own_kernel(
@@ -127,7 +130,9 @@
     source_copy = pltpu.make_async_copy(src, sources, more.at[2])
     outs = []
     for k in range(early):
-        terms_k = product(core, table[SHIFTS + k], src, lefts.at[k], rights.at[k], copies[k])
+        if k == 0:
+            wait_for(copies)
+        terms_k = product(slot_of(core, table[SHIFTS + k]), src, lefts.at[k], rights.at[k])
         for v in range(2):
             made[k, v] = terms_k[v]
             outs.append(
@@ -196,14 +201,21 @@
     pairs, size = left.shape[0], left.shape[2]
     early = own.shape[0]
     late = range(early, pairs)
-    source_copy = pltpu.make_async_copy(sources, src, more.at[0])
-    source_copy.start()
+    first_slot = slot_of(core, table[SHIFTS + early])
+    source_copies = []
+    for i in range(3):
+        slot = lax.rem(first_slot + i, 3)
+        source_copies.append(
+            pltpu.make_async_copy(sources.at[slot], src.at[slot], more.at[i])
+        )
     copies = loads(core, left, right, lefts, rights, sems, late)
     copies += loads(core, left_got, right_got, lefts, rights, sems, range(pairs), len(late))
     own_copies = [
         pltpu.make_async_copy(own.at[k], owns.at[k], own_sems.at[k]) for k in range(early)
     ]
-    for copy in [copy for pair in copies for copy in pair] + own_copies:
+    ordered = [source_copies[0], *copies[0], *source_copies[1:]]
+    ordered += [copy for pair in copies[1:] for copy in pair] + own_copies
+    for copy in ordered:
         copy.start()
 
     chips = packed.shape[0]
@@ -222,11 +234,18 @@
         jnp.sum(jnp.where(spot == 1 + k, facts, 0.0)).astype(jnp.int32) for k in range(pairs)
     ]
 
-    source_copy.wait()
     weights = [own_weight[0:1, k : k + 1] for k in late]
     weights += [got_weight[0:1, k : k + 1] for k in range(pairs)]
     for i, weight in enumerate(weights):
-        terms = product(core, shifts[i], src, lefts.at[i], rights.at[i], copies[i])
+        if i == 0:
+            source_copies[0].wait()
+            wait_for(copies[:1])
+        if i == 1:
+            wait_for([source_copies[1:]])
+            wait_for(copies[1:3])
+        if i == 3:
+            wait_for(copies[3:])
+        terms = product(slot_of(core, shifts[i]), src, lefts.at[i], rights.at[i])
         for v in range(2):
             total = weight * terms[v]
             acc[v] = total if i == 0 else acc[v] + total
@@ -301,7 +320,7 @@
             pltpu.VMEM((2, size, size), F32),
             pltpu.SemaphoreType.DMA((2, 2 * pairs - EARLY)),
             pltpu.SemaphoreType.DMA((EARLY,)),
-            pltpu.SemaphoreType.DMA((1,)),
+            pltpu.SemaphoreType.DMA((3,)),
         ],
         compiler_params=pltpu.CompilerParams(vmem_limit_bytes=55_000_000),
         cost_estimate=estimate(pairs, size),
@@ -320,7 +339,7 @@
     rows = chip_rows // 2
     parts = size // LANES
     words, edge, table = prepared(
-        2 * chips, site_coef, site_energy, shifts, sector_sizes, wavefunction
+        2 * chips, site_coef, site_energy[None], shifts, sector_sizes, wavefunction
     )
 
     swap = [(0, 1), (1, 0)]

time: 99.2 us -> 95.7 us (0.965)
  Pallas kernels: 20.8 us -> 17.2 us
    pallas_call x1, Pallas kernels: 11.9 us -> 8.99 us  [sigma_blocks(): pl.pallas_call(sigma_kernel, in_specs=[SMEM] * 2 + [VMEM] + [HBM] * 6, ou...]
  transfers between devices with their start and end apart: 6 -> 6, of which waited for: 2 -> 3; matrix products, arithmetic and copies ran while one was open for 3% -> 3% of each run, Pallas kernels for 6% -> 6%
where the time goes in v7:
time: 95.7 us; the launch traced here: 94.9 us
  starting transfers between devices  46.4 us (48%)
  waiting for transfers between devices  21.4 us (22%)
  Pallas kernels  17.2 us (18%)
  other arithmetic  4.35 us (5%)
  local copies, waits for them, and re-layouts  3.52 us (4%)
  between operations  2.12 us (2%)
    all_to_all x1, starting transfers between devices, on_device(): words = lax.all_to_all(words, OP, 0, 0, tiled=True)  21 us
    all_to_all x1, waiting for transfers between devices, on_device(): blocks = lax.all_to_all(packed.astype(F16), 'chip', 0, 0, tiled=True)  18.4 us
    all_to_all x1, starting transfers between devices, on_device(): blocks = lax.all_to_all(packed.astype(F16), 'chip', 0, 0, tiled=True)  12.1 us
    pallas_call x1, Pallas kernels, sigma_blocks(): pl.pallas_call(sigma_kernel, in_specs=[SMEM] * 2 + [VMEM] + [HBM] * 6, ou...  8.99 us
    all_to_all x1, starting transfers between devices, on_device(): came = lax.all_to_all(sent, ('core', 'blk'), 0, 0, tiled=True)  7.17 us
    pallas_call x1, Pallas kernels, own_terms(): pl.pallas_call(functools.partial(own_kernel, sectors), in_specs=[SMEM] +...  5.42 us
    ppermute x1, starting transfers between devices, on_device(): left_got = lax.ppermute(left_ops, 'core', swap)  2.88 us
    pallas_call x1, Pallas kernels, prepared(): pl.pallas_call(prep_kernel, in_specs=[VMEM] * 2 + [SMEM] * 2 + [HBM], out...  2.79 us
  transfers between devices with their start and end apart: 6, of which 3 were waited for; matrix products, arithmetic and copies ran while one was open for 3% of the time, Pallas kernels for 6%

profile of v7, /device:TPU:1, one launch (start us, length us, event | category | flops | bytes accessed | tf_op | source)
XLA Modules:
  0.0 94.9 jit_solution(8976432117502116588)
XLA Ops:
  1.3 2.8 %prepared.1 = (f32[128,2,128]{2,1,0:T(2,128)}, bf16[2,384,384]{2,1,0:T(8,128)(2,1)}, s32[15]{0:T(128)}) custom-call(f32[1,512]{1,0:T(1,128)} %coef.1, f32[1,1]{1,0:T(1,128)} %bitcast.16.energy, s32[4]{0:T(128)} %shifts.1, s32[8]{0:T(128)} %sizes.1, bf16[2,2,384,384]{3,2,1,0:T(8,128)(2,1)} %psi.3), custom_call_target="tpu_custom_call" | custom-call | tf_op jit(solution)/shard_map/prepared/pallas_call | solution.py:54
  4.1 1.3 %collective-permute-start = (bf16[2,384,384]{2,1,0:T(8,128)(2,1)}, bf16[2,384,384]{2,1,0:T(8,128)(2,1)S(1)}, u32[]{:S(2)}, u32[]{:S(2)}) collective-permute-start(bf16[2,384,384]{2,1,0:T(8,128)(2,1)} %get-tuple-element.11), channel_id=1, source_target_pairs={{0,1},{1,2},{2,3},{5,4},{6,5},{7,6},{8,9},{9,10},{10,11},{13,12},{... | collective-permute-start | bytes 1769480 | tf_op jit(solution)/shard_map/ppermute | solution.py:349
  5.4 21.0 %all-to-all-start = ((f32[128,2,128]{2,1,0:T(2,128)}), f32[128,2,128]{2,1,0:T(2,128)}, u32[]{:S(2)}, u32[]{:S(2)}) async-start(f32[128,2,128]{2,1,0:T(2,128)} %get-tuple-element.10), calls=%async_computation | async-start | bytes 262144 | tf_op jit(solution)/shard_map/all_to_all | solution.py:350
  26.4 2.9 %collective-permute-start.1 = (bf16[4,2,384,384]{3,2,1,0:T(8,128)(2,1)}, bf16[4,2,384,384]{3,2,1,0:T(8,128)(2,1)}, u32[]{:S(2)}, u32[]{:S(2)}) collective-permute-start(bf16[4,2,384,384]{3,2,1,0:T(8,128)(2,1)} %left.3), channel_id=1, source_target_pairs={{0,4},{4,0},{1,5},{5,1},{2,6},{6,2},{3,7},{7,3},{8,12},{12,8},{9,1... | collective-permute-start | bytes 7077896 | tf_op jit(solution)/shard_map/ppermute | solution.py:351
  29.3 1.9 %collective-permute-start.2 = (bf16[4,2,384,384]{3,2,1,0:T(8,128)(2,1)}, bf16[4,2,384,384]{3,2,1,0:T(8,128)(2,1)}, u32[]{:S(2)}, u32[]{:S(2)}) collective-permute-start(bf16[4,2,384,384]{3,2,1,0:T(8,128)(2,1)} %right.3), channel_id=1, source_target_pairs={{0,4},{4,0},{1,5},{5,1},{2,6},{6,2},{3,7},{7,3},{8,12},{12,8},{9,1... | collective-permute-start | bytes 7077896 | tf_op jit(solution)/shard_map/ppermute | solution.py:352
  31.9 0.0 collective-permute-done.halo
  31.9 0.0 copy-start.2
  31.9 0.9 copy-done.2
  32.8 0.0 copy-start
  32.8 5.4 %own_terms.1 = (f32[2,2,384,384]{3,2,1,0:T(8,128)}, bf16[3,384,768]{2,1,0:T(8,128)(2,1)}) custom-call(s32[15]{0:T(128)} %get-tuple-element.9.table, bf16[2,2,384,384]{3,2,1,0:T(8,128)(2,1)} %psi.3, bf16[2,384,384]{2,1,0:T(8,128)(2,1)} %copy-done.2, bf16[4,2,384,384]{3,2,1,0:T(8,128)(2,1)} %left.3, bf16[4,2,384,384]{3,2,1,0:T(8,128)(2,1)} %right.3), custom_call_target="tpu_custom_call" | custom-call | flops 181193932800 | bytes 1179648000 | tf_op jit(solution)/shard_map/own_terms/pallas_call | solution.py:157
  38.2 0.3 all-to-all-done.words
  38.5 0.0 collective-permute-done.1.left_got
  38.5 0.0 collective-permute-done.2.right_got
  38.5 0.0 copy-done
  38.5 9.0 %sigma_blocks.1 = (f32[64,40,128]{2,1,0:T(8,128)S(1)}, f32[2,128]{1,0:T(2,128)S(1)}) custom-call(s32[15]{0:T(128)S(1)} %copy-done, s32[1]{0:T(128)} %copy.26.owner, f32[128,2,128]{2,1,0:T(2,128)} %all-to-all-done.words, f32[2,2,384,384]{3,2,1,0:T(8,128)} %get-tuple-element.12.own, bf16[3,384,768]{2,1,0:T(8,128)(2,1)} %get-tuple-element.13.sources, ...), custom_call_target="tpu_custom_call" | custom-call | flops 1811939328 | bytes 11796480 | tf_op jit(solution)/shard_map/sigma_blocks/pallas_call | solution.py:307
  47.5 0.0 copy-start.1
  47.5 0.9 convert_element_type.18
  48.4 12.1 %all-to-all-start.1 = ((f16[64,40,128]{2,1,0:T(8,128)(2,1)}), f16[64,40,128]{2,1,0:T(8,128)(2,1)S(1)}, u32[]{:S(2)}, u32[]{:S(2)}) async-start(f16[64,40,128]{2,1,0:T(8,128)(2,1)} %convert_element_type.18), calls=%async_computation.1 | async-start | bytes 1310720 | tf_op jit(solution)/shard_map/all_to_all | solution.py:374
  60.5 0.0 copy-done.1
  60.5 0.1 dynamic_slice.14
  60.6 0.1 broadcast_compare_fusion
  60.7 0.1 iota_compare_fusion
  60.8 0.1 broadcast_and_fusion
  60.8 0.1 slice_reduce_fusion.1
  61.0 18.4 %all-to-all-done.1 = f16[64,40,128]{2,1,0:T(8,128)(2,1)S(1)} async-done(((f16[64,40,128]{2,1,0:T(8,128)(2,1)}), f16[64,40,128]{2,1,0:T(8,128)(2,1)S(1)}, u32[]{:S(2)}, u32[]{:S(2)}) %all-to-all-start.1) | async-done | bytes 655392 | tf_op jit(solution)/shard_map/all_to_all | solution.py:374
  79.4 0.2 fusion.9
  79.6 0.1 fusion.7
  79.7 0.2 multiply_reduce_fusion
  80.0 0.1 fusion.11
  80.1 0.6 pad_maximum_fusion
  80.7 7.2 %all-to-all-start.2 = ((f32[8,19,128]{2,1,0:T(8,128)}), f32[8,19,128]{2,1,0:T(8,128)S(1)}, u32[]{:S(2)}, u32[]{:S(2)}) async-start(f32[8,19,128]{2,1,0:T(8,128)} %bitcast.4), calls=%async_computation.2 | async-start | bytes 196608 | tf_op jit(solution)/shard_map/all_to_all | solution.py:391
  87.9 0.8 constant_dynamic-slice_fusion
  88.7 1.0 %slice.60 = f32[128,1,1]{2,1,0:T(1,128)S(1)} slice(f32[128,2,128]{2,1,0:T(2,128)} %all-to-all-done.words), slice={[0:128], [1:2], [0:1]} | slice | bytes 1024 | tf_op jit(solution)/shard_map/slice | solution.py:393
  89.7 0.5 constant_dynamic-slice_fusion.1
  90.2 2.7 %all-to-all-done.2 = f32[8,19,128]{2,1,0:T(8,128)S(1)} async-done(((f32[8,19,128]{2,1,0:T(8,128)}), f32[8,19,128]{2,1,0:T(8,128)S(1)}, u32[]{:S(2)}, u32[]{:S(2)}) %all-to-all-start.2) | async-done | bytes 77856 | tf_op jit(solution)/shard_map/all_to_all | solution.py:391
  93.0 1.2 %broadcast_subtract_fusion = (f32[2]{0:T(128)S(1)}, f32[2]{0:T(128)}) fusion(f32[]{:T(128)} %bitcast.10, f32[4]{0:T(128)S(1)} %slice_reduce_fusion), kind=kLoop, calls=%fused_computation.31 | loop fusion | flops 10 | bytes 36 | tf_op jit(solution)/shard_map/sub | solution.py:407
  94.2 0.7 fusion.10
  (13 shorter events, 0.2 us)
Async XLA Ops:
  4.1 27.8 %collective-permute-start = (bf16[2,384,384]{2,1,0:T(8,128)(2,1)}, bf16[2,384,384]{2,1,0:T(8,128)(2,1)S(1)}, u32[]{:S(2)}, u32[]{:S(2)}) collective-permute-start(bf16[2,384,384]{2,1,0:T(8,128)(2,1)} %get-tuple-element.11), channel_id=1, source_target_pairs={{0,1},{1,2},{2,3},{5,4},{6,5},{7,6},{8,9},{9,10},{10,11},{13,12},{... | collective-permute-start | bytes 1769480 | tf_op jit(solution)/shard_map/ppermute | solution.py:349
  5.4 33.1 %all-to-all-start = ((f32[128,2,128]{2,1,0:T(2,128)}), f32[128,2,128]{2,1,0:T(2,128)}, u32[]{:S(2)}, u32[]{:S(2)}) async-start(f32[128,2,128]{2,1,0:T(2,128)} %get-tuple-element.10), calls=%async_computation | async-start | bytes 262144 | tf_op jit(solution)/shard_map/all_to_all | solution.py:350
  26.4 12.1 %collective-permute-start.1 = (bf16[4,2,384,384]{3,2,1,0:T(8,128)(2,1)}, bf16[4,2,384,384]{3,2,1,0:T(8,128)(2,1)}, u32[]{:S(2)}, u32[]{:S(2)}) collective-permute-start(bf16[4,2,384,384]{3,2,1,0:T(8,128)(2,1)} %left.3), channel_id=1, source_target_pairs={{0,4},{4,0},{1,5},{5,1},{2,6},{6,2},{3,7},{7,3},{8,12},{12,8},{9,1... | collective-permute-start | bytes 7077896 | tf_op jit(solution)/shard_map/ppermute | solution.py:351
  29.3 9.2 %collective-permute-start.2 = (bf16[4,2,384,384]{3,2,1,0:T(8,128)(2,1)}, bf16[4,2,384,384]{3,2,1,0:T(8,128)(2,1)}, u32[]{:S(2)}, u32[]{:S(2)}) collective-permute-start(bf16[4,2,384,384]{3,2,1,0:T(8,128)(2,1)} %right.3), channel_id=1, source_target_pairs={{0,4},{4,0},{1,5},{5,1},{2,6},{6,2},{3,7},{7,3},{8,12},{12,8},{9,1... | collective-permute-start | bytes 7077896 | tf_op jit(solution)/shard_map/ppermute | solution.py:352
  31.9 0.9 copy-start.2
  32.8 5.7 %copy-start = (s32[15]{0:T(128)S(1)}, s32[15]{0:T(128)}, u32[]{:S(2)}) copy-start(s32[15]{0:T(128)} %get-tuple-element.9.table) | copy-start | bytes 184
  47.5 13.0 %copy-start.1 = (s32[8]{0:T(128)S(1)}, s32[8]{0:T(128)}, u32[]{:S(2)}) copy-start(s32[8]{0:T(128)} %sizes.1) | copy-start | bytes 100
  48.4 30.9 %all-to-all-start.1 = ((f16[64,40,128]{2,1,0:T(8,128)(2,1)}), f16[64,40,128]{2,1,0:T(8,128)(2,1)S(1)}, u32[]{:S(2)}, u32[]{:S(2)}) async-start(f16[64,40,128]{2,1,0:T(8,128)(2,1)} %convert_element_type.18), calls=%async_computation.1 | async-start | bytes 1310720 | tf_op jit(solution)/shard_map/all_to_all | solution.py:374
  80.7 12.2 %all-to-all-start.2 = ((f32[8,19,128]{2,1,0:T(8,128)}), f32[8,19,128]{2,1,0:T(8,128)S(1)}, u32[]{:S(2)}, u32[]{:S(2)}) async-start(f32[8,19,128]{2,1,0:T(8,128)} %bitcast.4), calls=%async_computation.2 | async-start | bytes 196608 | tf_op jit(solution)/shard_map/all_to_all | solution.py:391

commit v8 on v7

--- a/solution.py
+++ b/solution.py
@@ -328,6 +328,43 @@
     )(table, owner, words, own, sources, left, right, left_got, right_got)
 
 
+def finish_kernel(came, energy, psi, live, residual, rayleigh):
+    blk = lax.axis_index("blk")
+    blks = came.shape[0] // 2
+    rows, size = psi.shape[0], psi.shape[3]
+    parts = size // LANES
+    sums = jnp.sum(came[:, came.shape[1] - 1, :], axis=0, keepdims=True)
+    for v in range(2):
+        norm = sums[:, 2 + v : 3 + v]
+        quotient = (sums[:, v : v + 1] + energy[...] * norm) / (norm + 1e-06)
+        rayleigh[v] = jnp.sum(quotient)
+        factor = energy[...] - quotient
+        for q in range(rows):
+            for b in range(2):
+                for t in range(parts):
+                    at = (v * parts + t) * rows + q
+                    lanes = slice(t * LANES, (t + 1) * LANES)
+                    value = came[b * blks + blk, at : at + 1, :]
+                    value = value + factor * psi[q, v, b : b + 1, lanes]
+                    residual[q, v, b : b + 1, lanes] = jnp.where(
+                        live[q, b : b + 1, lanes] > 0.0, value, 0.0
+                    )
+
+
+def finished(came, energy, psi, live):
+    return pl.pallas_call(
+        finish_kernel,
+        in_specs=[VMEM] * 4,
+        out_specs=[VMEM, SMEM],
+        out_shape=[
+            jax.ShapeDtypeStruct(psi.shape, F32),
+            jax.ShapeDtypeStruct((2,), F32),
+        ],
+        compiler_params=pltpu.CompilerParams(vmem_limit_bytes=16 * 1024 * 1024),
+        name="finished",
+    )(came, energy, psi, live)
+
+
 def on_device(
     wavefunction, left_ops, right_ops, shifts, sector_sizes, site_coef, site_energy, site_owner
 ):
@@ -389,23 +426,17 @@
     sums = jnp.broadcast_to(sums[None, None, None], (2, blks, 1, LANES))
     sent = jnp.concatenate([halves, sums], axis=2).reshape(2 * blks, -1, LANES)
     came = lax.all_to_all(sent, ("core", "blk"), 0, 0, tiled=True)
-    sums = jnp.sum(came[:, -1, :4], axis=0)
     energy = lax.dynamic_index_in_dim(words[:, 1, 0], site_owner[0], 0, keepdims=False)
-    cross_sum, norm_sum = sums[:2], sums[2:]
-    rayleigh = (cross_sum + energy * norm_sum) / (norm_sum + 1e-06)
-    ours = lax.dynamic_index_in_dim(came.reshape(2, blks, -1, LANES), blk, 1, keepdims=False)
-    ours = ours[:, :-1].reshape(2, 2, parts, rows, LANES).transpose(3, 1, 0, 2, 4)
-    ours = ours.reshape(rows, 2, 2, size)
 
     first = (chip * 2 + core) * rows
     own_sizes = lax.dynamic_slice_in_dim(sector_sizes, 2 * blk, 2, 0)[:, None]
     row_ids = (first + jnp.arange(rows, dtype=jnp.int32))[:, None, None, None]
     col_ids = jnp.arange(size, dtype=jnp.int32)
-    live = (row_ids < own_sizes) & (col_ids < own_sizes)
+    live = ((row_ids < own_sizes) & (col_ids < own_sizes))[:, 0].astype(F32)
     psi_rows = lax.dynamic_slice_in_dim(wavefunction, first, rows, 2)
     psi_rows = psi_rows.transpose(2, 0, 1, 3).astype(F32)
-    value = ours + (energy - rayleigh)[None, :, None, None] * psi_rows
-    return jnp.where(live, value, 0.0), rayleigh
+    residual, rayleigh = finished(came, energy.reshape(1, 1), psi_rows, live)
+    return residual, rayleigh
 
 
 def solution(mesh):

time: 95.7 us -> 95.1 us (level)
  Pallas kernels: 17.2 us -> 18.6 us
  other arithmetic: 4.35 us -> 3.23 us
    pallas_call x0 -> x1, Pallas kernels: none -> 1.48 us  [finished(): pl.pallas_call(finish_kernel, in_specs=[VMEM] * 4, out_specs=[VMEM, SMEM]...]
    sub x1 -> x0, other arithmetic: 1.23 us -> none  [on_device(): value = ours + (energy - rayleigh)[None, :, None, None] * psi_rows]
where the time goes in v8:
time: 95.1 us; the launch traced here: 94.3 us
  starting transfers between devices  46.3 us (49%)
  waiting for transfers between devices  21.5 us (23%)
  Pallas kernels  18.6 us (20%)
  other arithmetic  3.23 us (3%)
  local copies, waits for them, and re-layouts  2.62 us (3%)
  between operations  2.1 us (2%)
    all_to_all x1, starting transfers between devices, on_device(): words = lax.all_to_all(words, OP, 0, 0, tiled=True)  21 us
    all_to_all x1, waiting for transfers between devices, on_device(): blocks = lax.all_to_all(packed.astype(F16), 'chip', 0, 0, tiled=True)  18.4 us
    all_to_all x1, starting transfers between devices, on_device(): blocks = lax.all_to_all(packed.astype(F16), 'chip', 0, 0, tiled=True)  12 us
    pallas_call x1, Pallas kernels, sigma_blocks(): pl.pallas_call(sigma_kernel, in_specs=[SMEM] * 2 + [VMEM] + [HBM] * 6, ou...  8.99 us
    all_to_all x1, starting transfers between devices, on_device(): came = lax.all_to_all(sent, ('core', 'blk'), 0, 0, tiled=True)  7.18 us
    pallas_call x1, Pallas kernels, own_terms(): pl.pallas_call(functools.partial(own_kernel, sectors), in_specs=[SMEM] +...  5.42 us
    ppermute x1, starting transfers between devices, on_device(): left_got = lax.ppermute(left_ops, 'core', swap)  2.88 us
    pallas_call x1, Pallas kernels, prepared(): pl.pallas_call(prep_kernel, in_specs=[VMEM] * 2 + [SMEM] * 2 + [HBM], out...  2.77 us
  transfers between devices with their start and end apart: 6, of which 3 were waited for; matrix products, arithmetic and copies ran while one was open for 3% of the time, Pallas kernels for 6%

profile of v8, /device:TPU:1, one launch (start us, length us, event | category | flops | bytes accessed | tf_op | source)
XLA Modules:
  0.0 94.3 jit_solution(9625801910084793645)
XLA Ops:
  1.3 2.8 %prepared.1 = (f32[128,2,128]{2,1,0:T(2,128)}, bf16[2,384,384]{2,1,0:T(8,128)(2,1)}, s32[15]{0:T(128)}) custom-call(f32[1,512]{1,0:T(1,128)} %coef.1, f32[1,1]{1,0:T(1,128)} %bitcast.10.energy, s32[4]{0:T(128)} %shifts.1, s32[8]{0:T(128)} %sizes.1, bf16[2,2,384,384]{3,2,1,0:T(8,128)(2,1)} %psi.3), custom_call_target="tpu_custom_call" | custom-call | tf_op jit(solution)/shard_map/prepared/pallas_call | solution.py:54
  4.1 1.3 %collective-permute-start = (bf16[2,384,384]{2,1,0:T(8,128)(2,1)}, bf16[2,384,384]{2,1,0:T(8,128)(2,1)S(1)}, u32[]{:S(2)}, u32[]{:S(2)}) collective-permute-start(bf16[2,384,384]{2,1,0:T(8,128)(2,1)} %get-tuple-element.11), channel_id=1, source_target_pairs={{0,1},{1,2},{2,3},{5,4},{6,5},{7,6},{8,9},{9,10},{10,11},{13,12},{... | collective-permute-start | bytes 1769480 | tf_op jit(solution)/shard_map/ppermute | solution.py:386
  5.4 21.0 %all-to-all-start = ((f32[128,2,128]{2,1,0:T(2,128)}), f32[128,2,128]{2,1,0:T(2,128)}, u32[]{:S(2)}, u32[]{:S(2)}) async-start(f32[128,2,128]{2,1,0:T(2,128)} %get-tuple-element.10), calls=%async_computation | async-start | bytes 262144 | tf_op jit(solution)/shard_map/all_to_all | solution.py:387
  26.4 2.9 %collective-permute-start.1 = (bf16[4,2,384,384]{3,2,1,0:T(8,128)(2,1)}, bf16[4,2,384,384]{3,2,1,0:T(8,128)(2,1)}, u32[]{:S(2)}, u32[]{:S(2)}) collective-permute-start(bf16[4,2,384,384]{3,2,1,0:T(8,128)(2,1)} %left.3), channel_id=1, source_target_pairs={{0,4},{4,0},{1,5},{5,1},{2,6},{6,2},{3,7},{7,3},{8,12},{12,8},{9,1... | collective-permute-start | bytes 7077896 | tf_op jit(solution)/shard_map/ppermute | solution.py:388
  29.3 1.9 %collective-permute-start.2 = (bf16[4,2,384,384]{3,2,1,0:T(8,128)(2,1)}, bf16[4,2,384,384]{3,2,1,0:T(8,128)(2,1)}, u32[]{:S(2)}, u32[]{:S(2)}) collective-permute-start(bf16[4,2,384,384]{3,2,1,0:T(8,128)(2,1)} %right.3), channel_id=1, source_target_pairs={{0,4},{4,0},{1,5},{5,1},{2,6},{6,2},{3,7},{7,3},{8,12},{12,8},{9,1... | collective-permute-start | bytes 7077896 | tf_op jit(solution)/shard_map/ppermute | solution.py:389
  31.9 0.0 collective-permute-done.halo
  31.9 0.0 copy-start.2
  31.9 0.9 copy-done.2
  32.8 0.0 copy-start
  32.8 5.4 %own_terms.1 = (f32[2,2,384,384]{3,2,1,0:T(8,128)}, bf16[3,384,768]{2,1,0:T(8,128)(2,1)}) custom-call(s32[15]{0:T(128)} %get-tuple-element.9.table, bf16[2,2,384,384]{3,2,1,0:T(8,128)(2,1)} %psi.3, bf16[2,384,384]{2,1,0:T(8,128)(2,1)} %copy-done.2, bf16[4,2,384,384]{3,2,1,0:T(8,128)(2,1)} %left.3, bf16[4,2,384,384]{3,2,1,0:T(8,128)(2,1)} %right.3), custom_call_target="tpu_custom_call" | custom-call | flops 181193932800 | bytes 1179648000 | tf_op jit(solution)/shard_map/own_terms/pallas_call | solution.py:157
  38.2 0.4 all-to-all-done.words
  38.5 0.0 collective-permute-done.1.left_got
  38.5 0.0 collective-permute-done.2.right_got
  38.5 0.0 copy-done
  38.5 9.0 %sigma_blocks.1 = (f32[64,40,128]{2,1,0:T(8,128)S(1)}, f32[2,128]{1,0:T(2,128)S(1)}) custom-call(s32[15]{0:T(128)S(1)} %copy-done, s32[1]{0:T(128)} %copy.19.owner, f32[128,2,128]{2,1,0:T(2,128)} %all-to-all-done.words, f32[2,2,384,384]{3,2,1,0:T(8,128)} %get-tuple-element.12.own, bf16[3,384,768]{2,1,0:T(8,128)(2,1)} %get-tuple-element.13.sources, ...), custom_call_target="tpu_custom_call" | custom-call | flops 1811939328 | bytes 11796480 | tf_op jit(solution)/shard_map/sigma_blocks/pallas_call | solution.py:307
  47.5 0.0 copy-start.1
  47.6 0.9 convert_element_type.22
  48.5 12.0 %all-to-all-start.1 = ((f16[64,40,128]{2,1,0:T(8,128)(2,1)}), f16[64,40,128]{2,1,0:T(8,128)(2,1)S(1)}, u32[]{:S(2)}, u32[]{:S(2)}) async-start(f16[64,40,128]{2,1,0:T(8,128)(2,1)} %convert_element_type.22), calls=%async_computation.1 | async-start | bytes 1310720 | tf_op jit(solution)/shard_map/all_to_all | solution.py:411
  60.5 0.0 copy-done.1
  60.5 0.1 dynamic_slice.12
  60.6 0.1 broadcast_compare_fusion
  60.6 0.1 iota_compare_fusion
  60.7 0.1 and_convert_fusion.live
  60.8 0.1 slice_reduce_fusion
  60.9 18.4 %all-to-all-done.1 = f16[64,40,128]{2,1,0:T(8,128)(2,1)S(1)} async-done(((f16[64,40,128]{2,1,0:T(8,128)(2,1)}), f16[64,40,128]{2,1,0:T(8,128)(2,1)S(1)}, u32[]{:S(2)}, u32[]{:S(2)}) %all-to-all-start.1) | async-done | bytes 655392 | tf_op jit(solution)/shard_map/all_to_all | solution.py:411
  79.4 0.2 fusion.9
  79.5 0.1 fusion.7
  79.7 0.2 multiply_reduce_fusion
  79.9 0.1 fusion.10
  80.0 0.6 pad_maximum_fusion
  80.7 7.2 %all-to-all-start.2 = ((f32[8,19,128]{2,1,0:T(8,128)}), f32[8,19,128]{2,1,0:T(8,128)S(1)}, u32[]{:S(2)}, u32[]{:S(2)}) async-start(f32[8,19,128]{2,1,0:T(8,128)} %bitcast.4), calls=%async_computation.2 | async-start | bytes 196608 | tf_op jit(solution)/shard_map/all_to_all | solution.py:428
  87.8 0.8 dynamic-slice_convert_fusion
  88.7 1.0 %slice.43 = f32[128,1,1]{2,1,0:T(1,128)S(1)} slice(f32[128,2,128]{2,1,0:T(2,128)} %all-to-all-done.words), slice={[0:128], [1:2], [0:1]} | slice | bytes 1024 | tf_op jit(solution)/shard_map/slice | solution.py:429
  89.7 0.5 constant_dynamic-slice_fusion
  90.2 2.7 %all-to-all-done.2.came = f32[8,19,128]{2,1,0:T(8,128)S(1)} async-done(((f32[8,19,128]{2,1,0:T(8,128)}), f32[8,19,128]{2,1,0:T(8,128)S(1)}, u32[]{:S(2)}, u32[]{:S(2)}) %all-to-all-start.2) | async-done | bytes 77856 | tf_op jit(solution)/shard_map/all_to_all | solution.py:428
  92.8 1.5 %finished.1 = (f32[3,2,2,384]{3,2,1,0:T(2,128)}, f32[2]{0:T(128)}) custom-call(f32[8,19,128]{2,1,0:T(8,128)S(1)} %all-to-all-done.2.came, f32[1,1]{1,0:T(1,128)} %bitcast.6.energy, f32[3,2,2,384]{3,2,1,0:T(2,128)S(1)} %bitcast.14, f32[3,2,384]{2,1,0:T(2,128)S(1)} %and_convert_fusion.live), custom_call_target="tpu_custom_call" | custom-call | tf_op jit(solution)/shard_map/finished/pallas_call | solution.py:355
  (8 shorter events, 0.1 us)
Async XLA Ops:
  4.1 27.8 %collective-permute-start = (bf16[2,384,384]{2,1,0:T(8,128)(2,1)}, bf16[2,384,384]{2,1,0:T(8,128)(2,1)S(1)}, u32[]{:S(2)}, u32[]{:S(2)}) collective-permute-start(bf16[2,384,384]{2,1,0:T(8,128)(2,1)} %get-tuple-element.11), channel_id=1, source_target_pairs={{0,1},{1,2},{2,3},{5,4},{6,5},{7,6},{8,9},{9,10},{10,11},{13,12},{... | collective-permute-start | bytes 1769480 | tf_op jit(solution)/shard_map/ppermute | solution.py:386
  5.4 33.2 %all-to-all-start = ((f32[128,2,128]{2,1,0:T(2,128)}), f32[128,2,128]{2,1,0:T(2,128)}, u32[]{:S(2)}, u32[]{:S(2)}) async-start(f32[128,2,128]{2,1,0:T(2,128)} %get-tuple-element.10), calls=%async_computation | async-start | bytes 262144 | tf_op jit(solution)/shard_map/all_to_all | solution.py:387
  26.4 12.1 %collective-permute-start.1 = (bf16[4,2,384,384]{3,2,1,0:T(8,128)(2,1)}, bf16[4,2,384,384]{3,2,1,0:T(8,128)(2,1)}, u32[]{:S(2)}, u32[]{:S(2)}) collective-permute-start(bf16[4,2,384,384]{3,2,1,0:T(8,128)(2,1)} %left.3), channel_id=1, source_target_pairs={{0,4},{4,0},{1,5},{5,1},{2,6},{6,2},{3,7},{7,3},{8,12},{12,8},{9,1... | collective-permute-start | bytes 7077896 | tf_op jit(solution)/shard_map/ppermute | solution.py:388
  29.3 9.3 %collective-permute-start.2 = (bf16[4,2,384,384]{3,2,1,0:T(8,128)(2,1)}, bf16[4,2,384,384]{3,2,1,0:T(8,128)(2,1)}, u32[]{:S(2)}, u32[]{:S(2)}) collective-permute-start(bf16[4,2,384,384]{3,2,1,0:T(8,128)(2,1)} %right.3), channel_id=1, source_target_pairs={{0,4},{4,0},{1,5},{5,1},{2,6},{6,2},{3,7},{7,3},{8,12},{12,8},{9,1... | collective-permute-start | bytes 7077896 | tf_op jit(solution)/shard_map/ppermute | solution.py:389
  31.9 0.9 copy-start.2
  32.8 5.8 %copy-start = (s32[15]{0:T(128)S(1)}, s32[15]{0:T(128)}, u32[]{:S(2)}) copy-start(s32[15]{0:T(128)} %get-tuple-element.9.table) | copy-start | bytes 184
  47.5 12.9 %copy-start.1 = (s32[8]{0:T(128)S(1)}, s32[8]{0:T(128)}, u32[]{:S(2)}) copy-start(s32[8]{0:T(128)} %sizes.1) | copy-start | bytes 100
  48.5 30.8 %all-to-all-start.1 = ((f16[64,40,128]{2,1,0:T(8,128)(2,1)}), f16[64,40,128]{2,1,0:T(8,128)(2,1)S(1)}, u32[]{:S(2)}, u32[]{:S(2)}) async-start(f16[64,40,128]{2,1,0:T(8,128)(2,1)} %convert_element_type.22), calls=%async_computation.1 | async-start | bytes 1310720 | tf_op jit(solution)/shard_map/all_to_all | solution.py:411
  80.7 12.2 %all-to-all-start.2 = ((f32[8,19,128]{2,1,0:T(8,128)}), f32[8,19,128]{2,1,0:T(8,128)S(1)}, u32[]{:S(2)}, u32[]{:S(2)}) async-start(f32[8,19,128]{2,1,0:T(8,128)} %bitcast.4), calls=%async_computation.2 | async-start | bytes 196608 | tf_op jit(solution)/shard_map/all_to_all | solution.py:428

commit v9 on v8

--- a/solution.py
+++ b/solution.py
@@ -19,10 +19,12 @@
 CORE, BLK, CHIP, SHIFTS = 0, 1, 2, 3
 
 
-def prep_kernel(coef, energy, shifts, sizes, psi, words, edge, table, sems):
+def prep_kernel(
+    coef, energy, shifts, sizes, psi, words, edge, table, made, held, sems, out_sems
+):
     core = lax.axis_index("core")
     copies = [
-        pltpu.make_async_copy(psi.at[v, 1 - core], edge.at[v], sems.at[v]) for v in range(2)
+        pltpu.make_async_copy(psi.at[v, 1 - core], held.at[v], sems.at[v]) for v in range(2)
     ]
     for copy in copies:
         copy.start()
@@ -44,9 +46,15 @@
     for i in range(lines):
         line = jnp.broadcast_to(coef[0:1, i * LANES : (i + 1) * LANES], (2, LANES))
         block = jnp.where(row == 0, line, facts)
-        words[i * each : (i + 1) * each] = jnp.broadcast_to(block[None], (each, 2, LANES))
-    for copy in copies:
-        copy.wait()
+        made[i * each : (i + 1) * each] = jnp.broadcast_to(block[None], (each, 2, LANES))
+    outs = [pltpu.make_async_copy(made, words, out_sems.at[2])]
+    outs[0].start()
+    for v in range(2):
+        copies[v].wait()
+        outs.append(pltpu.make_async_copy(held.at[v], edge.at[v], out_sems.at[v]))
+        outs[-1].start()
+    for out in outs:
+        out.wait()
 
 
 def prepared(ops, coef, energy, shifts, sizes, psi):
@@ -54,13 +62,18 @@
     return pl.pallas_call(
         prep_kernel,
         in_specs=[VMEM] * 2 + [SMEM] * 2 + [HBM],
-        out_specs=[VMEM, VMEM, SMEM],
+        out_specs=[HBM, HBM, SMEM],
         out_shape=[
             jax.ShapeDtypeStruct((ops, 2, LANES), F32),
             jax.ShapeDtypeStruct((2, size, size), BF16),
             jax.ShapeDtypeStruct((SHIFTS + shifts.shape[0] + sizes.shape[0],), jnp.int32),
         ],
-        scratch_shapes=[pltpu.SemaphoreType.DMA((2,))],
+        scratch_shapes=[
+            pltpu.VMEM((ops, 2, LANES), F32),
+            pltpu.VMEM((2, size, size), BF16),
+            pltpu.SemaphoreType.DMA((2,)),
+            pltpu.SemaphoreType.DMA((3,)),
+        ],
         compiler_params=pltpu.CompilerParams(vmem_limit_bytes=60_000_000),
         name="prepared",
     )(coef, energy, shifts, sizes, psi)

time: 95.1 us -> 95.5 us (level)
  no operation moved by 1% of the time
where the time goes in v9:
time: 95.5 us; the launch traced here: 94.8 us
  starting transfers between devices  46.3 us (48%)
  waiting for transfers between devices  21.5 us (23%)
  Pallas kernels  19.1 us (20%)
  other arithmetic  3.23 us (3%)
  local copies, waits for them, and re-layouts  2.62 us (3%)
  between operations  2.1 us (2%)
    all_to_all x1, starting transfers between devices, on_device(): words = lax.all_to_all(words, OP, 0, 0, tiled=True)  21 us
    all_to_all x1, waiting for transfers between devices, on_device(): blocks = lax.all_to_all(packed.astype(F16), 'chip', 0, 0, tiled=True)  18.4 us
    all_to_all x1, starting transfers between devices, on_device(): blocks = lax.all_to_all(packed.astype(F16), 'chip', 0, 0, tiled=True)  12 us
    pallas_call x1, Pallas kernels, sigma_blocks(): pl.pallas_call(sigma_kernel, in_specs=[SMEM] * 2 + [VMEM] + [HBM] * 6, ou...  8.99 us
    all_to_all x1, starting transfers between devices, on_device(): came = lax.all_to_all(sent, ('core', 'blk'), 0, 0, tiled=True)  7.18 us
    pallas_call x1, Pallas kernels, own_terms(): pl.pallas_call(functools.partial(own_kernel, sectors), in_specs=[SMEM] +...  5.42 us
    pallas_call x1, Pallas kernels, prepared(): pl.pallas_call(prep_kernel, in_specs=[VMEM] * 2 + [SMEM] * 2 + [HBM], out...  3.2 us
    ppermute x1, starting transfers between devices, on_device(): left_got = lax.ppermute(left_ops, 'core', swap)  2.88 us
  transfers between devices with their start and end apart: 6, of which 3 were waited for; matrix products, arithmetic and copies ran while one was open for 3% of the time, Pallas kernels for 6%

profile of v9, /device:TPU:1, one launch (start us, length us, event | category | flops | bytes accessed | tf_op | source)
XLA Modules:
  0.0 94.8 jit_solution(15936577048976396176)
XLA Ops:
  1.3 3.2 %prepared.1 = (f32[128,2,128]{2,1,0:T(2,128)}, bf16[2,384,384]{2,1,0:T(8,128)(2,1)}, s32[15]{0:T(128)}) custom-call(f32[1,512]{1,0:T(1,128)} %coef.1, f32[1,1]{1,0:T(1,128)} %bitcast.10.energy, s32[4]{0:T(128)} %shifts.1, s32[8]{0:T(128)} %sizes.1, bf16[2,2,384,384]{3,2,1,0:T(8,128)(2,1)} %psi.3), custom_call_target="tpu_custom_call" | custom-call | tf_op jit(solution)/shard_map/prepared/pallas_call | solution.py:62
  4.5 1.3 %collective-permute-start = (bf16[2,384,384]{2,1,0:T(8,128)(2,1)}, bf16[2,384,384]{2,1,0:T(8,128)(2,1)S(1)}, u32[]{:S(2)}, u32[]{:S(2)}) collective-permute-start(bf16[2,384,384]{2,1,0:T(8,128)(2,1)} %get-tuple-element.11), channel_id=1, source_target_pairs={{0,1},{1,2},{2,3},{5,4},{6,5},{7,6},{8,9},{9,10},{10,11},{13,12},{... | collective-permute-start | bytes 1769480 | tf_op jit(solution)/shard_map/ppermute | solution.py:399
  5.8 21.0 %all-to-all-start = ((f32[128,2,128]{2,1,0:T(2,128)}), f32[128,2,128]{2,1,0:T(2,128)}, u32[]{:S(2)}, u32[]{:S(2)}) async-start(f32[128,2,128]{2,1,0:T(2,128)} %get-tuple-element.10), calls=%async_computation | async-start | bytes 262144 | tf_op jit(solution)/shard_map/all_to_all | solution.py:400
  26.8 2.9 %collective-permute-start.1 = (bf16[4,2,384,384]{3,2,1,0:T(8,128)(2,1)}, bf16[4,2,384,384]{3,2,1,0:T(8,128)(2,1)}, u32[]{:S(2)}, u32[]{:S(2)}) collective-permute-start(bf16[4,2,384,384]{3,2,1,0:T(8,128)(2,1)} %left.3), channel_id=1, source_target_pairs={{0,4},{4,0},{1,5},{5,1},{2,6},{6,2},{3,7},{7,3},{8,12},{12,8},{9,1... | collective-permute-start | bytes 7077896 | tf_op jit(solution)/shard_map/ppermute | solution.py:401
  29.7 1.9 %collective-permute-start.2 = (bf16[4,2,384,384]{3,2,1,0:T(8,128)(2,1)}, bf16[4,2,384,384]{3,2,1,0:T(8,128)(2,1)}, u32[]{:S(2)}, u32[]{:S(2)}) collective-permute-start(bf16[4,2,384,384]{3,2,1,0:T(8,128)(2,1)} %right.3), channel_id=1, source_target_pairs={{0,4},{4,0},{1,5},{5,1},{2,6},{6,2},{3,7},{7,3},{8,12},{12,8},{9,1... | collective-permute-start | bytes 7077896 | tf_op jit(solution)/shard_map/ppermute | solution.py:402
  32.3 0.0 collective-permute-done.halo
  32.3 0.0 copy-start.2
  32.3 0.9 copy-done.2
  33.2 0.0 copy-start
  33.2 5.4 %own_terms.1 = (f32[2,2,384,384]{3,2,1,0:T(8,128)}, bf16[3,384,768]{2,1,0:T(8,128)(2,1)}) custom-call(s32[15]{0:T(128)} %get-tuple-element.9.table, bf16[2,2,384,384]{3,2,1,0:T(8,128)(2,1)} %psi.3, bf16[2,384,384]{2,1,0:T(8,128)(2,1)} %copy-done.2, bf16[4,2,384,384]{3,2,1,0:T(8,128)(2,1)} %left.3, bf16[4,2,384,384]{3,2,1,0:T(8,128)(2,1)} %right.3), custom_call_target="tpu_custom_call" | custom-call | flops 181193932800 | bytes 1179648000 | tf_op jit(solution)/shard_map/own_terms/pallas_call | solution.py:170
  38.6 0.4 all-to-all-done.words
  39.0 0.0 collective-permute-done.1.left_got
  39.0 0.0 collective-permute-done.2.right_got
  39.0 0.0 copy-done
  39.0 9.0 %sigma_blocks.1 = (f32[64,40,128]{2,1,0:T(8,128)S(1)}, f32[2,128]{1,0:T(2,128)S(1)}) custom-call(s32[15]{0:T(128)S(1)} %copy-done, s32[1]{0:T(128)} %copy.19.owner, f32[128,2,128]{2,1,0:T(2,128)} %all-to-all-done.words, f32[2,2,384,384]{3,2,1,0:T(8,128)} %get-tuple-element.12.own, bf16[3,384,768]{2,1,0:T(8,128)(2,1)} %get-tuple-element.13.sources, ...), custom_call_target="tpu_custom_call" | custom-call | flops 1811939328 | bytes 11796480 | tf_op jit(solution)/shard_map/sigma_blocks/pallas_call | solution.py:320
  48.0 0.0 copy-start.1
  48.0 0.9 convert_element_type.22
  48.9 12.0 %all-to-all-start.1 = ((f16[64,40,128]{2,1,0:T(8,128)(2,1)}), f16[64,40,128]{2,1,0:T(8,128)(2,1)S(1)}, u32[]{:S(2)}, u32[]{:S(2)}) async-start(f16[64,40,128]{2,1,0:T(8,128)(2,1)} %convert_element_type.22), calls=%async_computation.1 | async-start | bytes 1310720 | tf_op jit(solution)/shard_map/all_to_all | solution.py:424
  60.9 0.0 copy-done.1
  60.9 0.1 dynamic_slice.12
  61.0 0.1 broadcast_compare_fusion
  61.1 0.1 iota_compare_fusion
  61.1 0.1 and_convert_fusion.live
  61.2 0.1 slice_reduce_fusion
  61.3 18.4 %all-to-all-done.1 = f16[64,40,128]{2,1,0:T(8,128)(2,1)S(1)} async-done(((f16[64,40,128]{2,1,0:T(8,128)(2,1)}), f16[64,40,128]{2,1,0:T(8,128)(2,1)S(1)}, u32[]{:S(2)}, u32[]{:S(2)}) %all-to-all-start.1) | async-done | bytes 655392 | tf_op jit(solution)/shard_map/all_to_all | solution.py:424
  79.8 0.2 fusion.9
  80.0 0.1 fusion.7
  80.1 0.2 multiply_reduce_fusion
  80.4 0.1 fusion.10
  80.5 0.6 pad_maximum_fusion
  81.1 7.2 %all-to-all-start.2 = ((f32[8,19,128]{2,1,0:T(8,128)}), f32[8,19,128]{2,1,0:T(8,128)S(1)}, u32[]{:S(2)}, u32[]{:S(2)}) async-start(f32[8,19,128]{2,1,0:T(8,128)} %bitcast.4), calls=%async_computation.2 | async-start | bytes 196608 | tf_op jit(solution)/shard_map/all_to_all | solution.py:441
  88.3 0.8 dynamic-slice_convert_fusion
  89.1 1.0 %slice.43 = f32[128,1,1]{2,1,0:T(1,128)S(1)} slice(f32[128,2,128]{2,1,0:T(2,128)} %all-to-all-done.words), slice={[0:128], [1:2], [0:1]} | slice | bytes 1024 | tf_op jit(solution)/shard_map/slice | solution.py:442
  90.1 0.5 constant_dynamic-slice_fusion
  90.6 2.7 %all-to-all-done.2.came = f32[8,19,128]{2,1,0:T(8,128)S(1)} async-done(((f32[8,19,128]{2,1,0:T(8,128)}), f32[8,19,128]{2,1,0:T(8,128)S(1)}, u32[]{:S(2)}, u32[]{:S(2)}) %all-to-all-start.2) | async-done | bytes 77856 | tf_op jit(solution)/shard_map/all_to_all | solution.py:441
  93.3 1.5 %finished.1 = (f32[3,2,2,384]{3,2,1,0:T(2,128)}, f32[2]{0:T(128)}) custom-call(f32[8,19,128]{2,1,0:T(8,128)S(1)} %all-to-all-done.2.came, f32[1,1]{1,0:T(1,128)} %bitcast.6.energy, f32[3,2,2,384]{3,2,1,0:T(2,128)S(1)} %bitcast.14, f32[3,2,384]{2,1,0:T(2,128)S(1)} %and_convert_fusion.live), custom_call_target="tpu_custom_call" | custom-call | tf_op jit(solution)/shard_map/finished/pallas_call | solution.py:368
  (8 shorter events, 0.1 us)
Async XLA Ops:
  4.5 27.8 %collective-permute-start = (bf16[2,384,384]{2,1,0:T(8,128)(2,1)}, bf16[2,384,384]{2,1,0:T(8,128)(2,1)S(1)}, u32[]{:S(2)}, u32[]{:S(2)}) collective-permute-start(bf16[2,384,384]{2,1,0:T(8,128)(2,1)} %get-tuple-element.11), channel_id=1, source_target_pairs={{0,1},{1,2},{2,3},{5,4},{6,5},{7,6},{8,9},{9,10},{10,11},{13,12},{... | collective-permute-start | bytes 1769480 | tf_op jit(solution)/shard_map/ppermute | solution.py:399
  5.8 33.2 %all-to-all-start = ((f32[128,2,128]{2,1,0:T(2,128)}), f32[128,2,128]{2,1,0:T(2,128)}, u32[]{:S(2)}, u32[]{:S(2)}) async-start(f32[128,2,128]{2,1,0:T(2,128)} %get-tuple-element.10), calls=%async_computation | async-start | bytes 262144 | tf_op jit(solution)/shard_map/all_to_all | solution.py:400
  26.8 12.1 %collective-permute-start.1 = (bf16[4,2,384,384]{3,2,1,0:T(8,128)(2,1)}, bf16[4,2,384,384]{3,2,1,0:T(8,128)(2,1)}, u32[]{:S(2)}, u32[]{:S(2)}) collective-permute-start(bf16[4,2,384,384]{3,2,1,0:T(8,128)(2,1)} %left.3), channel_id=1, source_target_pairs={{0,4},{4,0},{1,5},{5,1},{2,6},{6,2},{3,7},{7,3},{8,12},{12,8},{9,1... | collective-permute-start | bytes 7077896 | tf_op jit(solution)/shard_map/ppermute | solution.py:401
  29.7 9.3 %collective-permute-start.2 = (bf16[4,2,384,384]{3,2,1,0:T(8,128)(2,1)}, bf16[4,2,384,384]{3,2,1,0:T(8,128)(2,1)}, u32[]{:S(2)}, u32[]{:S(2)}) collective-permute-start(bf16[4,2,384,384]{3,2,1,0:T(8,128)(2,1)} %right.3), channel_id=1, source_target_pairs={{0,4},{4,0},{1,5},{5,1},{2,6},{6,2},{3,7},{7,3},{8,12},{12,8},{9,1... | collective-permute-start | bytes 7077896 | tf_op jit(solution)/shard_map/ppermute | solution.py:402
  32.3 0.9 copy-start.2
  33.2 5.8 %copy-start = (s32[15]{0:T(128)S(1)}, s32[15]{0:T(128)}, u32[]{:S(2)}) copy-start(s32[15]{0:T(128)} %get-tuple-element.9.table) | copy-start | bytes 184
  48.0 12.9 %copy-start.1 = (s32[8]{0:T(128)S(1)}, s32[8]{0:T(128)}, u32[]{:S(2)}) copy-start(s32[8]{0:T(128)} %sizes.1) | copy-start | bytes 100
  48.9 30.8 %all-to-all-start.1 = ((f16[64,40,128]{2,1,0:T(8,128)(2,1)}), f16[64,40,128]{2,1,0:T(8,128)(2,1)S(1)}, u32[]{:S(2)}, u32[]{:S(2)}) async-start(f16[64,40,128]{2,1,0:T(8,128)(2,1)} %convert_element_type.22), calls=%async_computation.1 | async-start | bytes 1310720 | tf_op jit(solution)/shard_map/all_to_all | solution.py:424
  81.1 12.2 %all-to-all-start.2 = ((f32[8,19,128]{2,1,0:T(8,128)}), f32[8,19,128]{2,1,0:T(8,128)S(1)}, u32[]{:S(2)}, u32[]{:S(2)}) async-start(f32[8,19,128]{2,1,0:T(8,128)} %bitcast.4), calls=%async_computation.2 | async-start | bytes 196608 | tf_op jit(solution)/shard_map/all_to_all | solution.py:441
